TPU v7x, 512 devices: a whole 4x4x16 slice. The times are simulated.
512 devices in a mesh: dp: 32 (over y, z_hi, core), feat: 16 (over z_lo, x).
Axes of the slice: x: 4, y: 4, z: 16 (z_hi: 4, z_lo: 4; z = z_hi * 4 + z_lo), core: 2. Of those that a mesh axis runs over, the one named last changes fastest.
Arguments:
- h_a: bfloat16 [4096, 4096], P('dp', 'feat'), may hold values from -6 to 6
- h_b: bfloat16 [4096, 4096], P('dp', 'feat'), may hold values from -6 to 6
- z_a: bfloat16 [4096, 4096], P('dp', 'feat'), may hold values from -700 to 700
- z_b: bfloat16 [4096, 4096], P('dp', 'feat'), may hold values from -700 to 700
Outputs:
- weight_grad: float32 [16, 32, 8, 4096], P(None, 'dp', None, 'feat')
All inputs are finite; a program needn't handle non-finite values.
Results may differ from a plain program's by a relative error of at most 0.034.
Values may be sent and summed in bfloat16 or wider, within the bound.
No kernel may reach another device: no remote copies, remote signals or barrier semaphores. Data moves between devices by JAX's collectives and lax.ppermute only.
A program may use at most 64 MiB of HBM per device.

v0:
```python
import jax
import jax.numpy as jnp
from jax import lax
from jax.sharding import PartitionSpec as P

epsilon = 1e-05
off_weight = 0.0051


def finish(floats, total, squares, pair_count):
    col_mean = total / pair_count
    variance = squares / pair_count - col_mean * col_mean
    inverse = lax.rsqrt(variance + epsilon)
    return (((floats - col_mean) * inverse).astype(jnp.bfloat16), inverse)


def norm_back(upstream, normed, inverse, first_sum, second_sum, pair_count):
    floats = normed.astype(jnp.float32)
    first = first_sum / pair_count
    second = second_sum / pair_count
    return (inverse * (upstream - first - floats * second)).astype(jnp.bfloat16)


def weight_fold(inputs, piece):
    return jnp.dot(inputs.T, piece.astype(jnp.float32))


def body(h_a, h_b, z_a, z_b):
    n_data = lax.axis_size("dp")
    n_feature = lax.axis_size("feat")
    local_rows, block_width = z_a.shape
    pair_count = local_rows * n_data
    sub_width = block_width // n_data
    floats_a = z_a.astype(jnp.float32)
    floats_b = z_b.astype(jnp.float32)
    sums = lax.psum(
        (
            jnp.sum(floats_a, axis=0),
            jnp.sum(floats_a * floats_a, axis=0),
            jnp.sum(floats_b, axis=0),
            jnp.sum(floats_b * floats_b, axis=0),
        ),
        "dp",
    )
    zn_a, inv_a = finish(floats_a, sums[0], sums[1], pair_count)
    zn_b, inv_b = finish(floats_b, sums[2], sums[3], pair_count)
    all_a = lax.all_gather(zn_a, "dp", axis=0, tiled=True)
    pieces_b = lax.all_to_all(zn_b, "dp", split_axis=1, concat_axis=0, tiled=True)
    cols_b = lax.all_gather(pieces_b, "feat", axis=1, tiled=True)
    input_pieces = (
        lax.all_to_all(h_a, "dp", split_axis=1, concat_axis=0, tiled=True),
        lax.all_to_all(h_b, "dp", split_axis=1, concat_axis=0, tiled=True),
    )
    input_cols = (
        lax.all_gather(input_pieces[0], "feat", axis=1, tiled=True),
        lax.all_gather(input_pieces[1], "feat", axis=1, tiled=True),
    )
    inputs_a = input_cols[0].astype(jnp.float32)
    inputs_b = input_cols[1].astype(jnp.float32)
    all_a_floats = all_a.astype(jnp.float32)
    cols_b_floats = cols_b.astype(jnp.float32)
    correlation = jnp.dot(all_a_floats.T, cols_b_floats) / pair_count
    row_global = lax.axis_index("feat") * block_width + jnp.arange(block_width, dtype=jnp.int32)
    lanes = jnp.arange(n_feature * sub_width, dtype=jnp.int32)
    col_global = (
        lanes // sub_width * block_width + lax.axis_index("dp") * sub_width + lanes % sub_width
    )
    on_diagonal = row_global[:, None] == col_global[None, :]
    grad_block = jnp.where(
        on_diagonal, -2.0 * (1.0 - correlation), 2.0 * off_weight * correlation
    ).astype(jnp.bfloat16)
    grad_floats = grad_block.astype(jnp.float32)
    part_a = jnp.dot(cols_b_floats, grad_floats.T) / pair_count
    part_b = jnp.dot(all_a_floats, grad_floats) / pair_count
    dzn_a = lax.psum_scatter(
        part_a.astype(jnp.bfloat16), "dp", scatter_dimension=0, tiled=True
    ).astype(jnp.float32)
    zn_a_floats = zn_a.astype(jnp.float32)
    moments_a = lax.psum((jnp.sum(dzn_a, axis=0), jnp.sum(dzn_a * zn_a_floats, axis=0)), "dp")
    dz_a = norm_back(dzn_a, zn_a, inv_a, moments_a[0], moments_a[1], pair_count)
    grad_a = weight_fold(inputs_a, lax.all_gather(dz_a, "dp", axis=0, tiled=True))
    summed_b = lax.psum_scatter(
        part_b.astype(jnp.bfloat16), "feat", scatter_dimension=1, tiled=True
    ).astype(jnp.float32)
    dzn_b = lax.all_to_all(
        summed_b.astype(jnp.bfloat16), "dp", split_axis=0, concat_axis=1, tiled=True
    ).astype(summed_b.dtype)
    zn_b_floats = zn_b.astype(jnp.float32)
    moments_b = lax.psum((jnp.sum(dzn_b, axis=0), jnp.sum(dzn_b * zn_b_floats, axis=0)), "dp")
    dz_b = norm_back(dzn_b, zn_b, inv_b, moments_b[0], moments_b[1], pair_count)
    grad_b = weight_fold(inputs_b, lax.all_gather(dz_b, "dp", axis=0, tiled=True))
    result = (grad_a + grad_b) * pair_count
    return result.reshape(n_feature, 1, sub_width, block_width)


def solution(mesh):
    return jax.shard_map(
        body,
        mesh=mesh,
        in_specs=(P("dp", "feat"), P("dp", "feat"), P("dp", "feat"), P("dp", "feat")),
        out_specs=P(None, "dp", None, "feat"),
        check_vma=False,
    )
```

profile of v0, /device:TPU:1, one launch (start us, length us, event | category | flops | bytes accessed | tf_op | source)
XLA Modules:
  0.0 839.2 jit_solution(15153074249478000189)
XLA Ops:
  6.5 0.9 fusion.13
  7.4 0.9 copy.7
  8.4 0.2 convert_reduce_fusion.1
  8.5 90.7 %all-reduce.1 = (f32[256]{0:T(256)S(1)}, f32[256]{0:T(256)S(1)}, f32[256]{0:T(256)S(1)}, f32[256]{0:T(256)S(1)}) all-reduce(f32[256]{0:T(256)S(1)} %get-tuple-element.10, f32[256]{0:T(256)S(1)} %get-tuple-element.9, f32[256]{0:T(256)S(1)} %get-tuple-element.8, f32[256]{0:T(256)S(1)} %get-tuple-element.7), channel_id=1, replica_groups=mesh['dp'=32,'feat'=16] {'dp'}, use_global_device_ids=true, to_apply=%region_3.0 | all-reduce | flops 1024 | bytes 8192 | tf_op jit(solution)/shard_map/psum | solution.py:36
  99.3 0.1 fusion.45
  99.4 26.0 %all_to_all.70 = bf16[128,32,8]{0,2,1:T(8,128)(2,1)} all-to-all(bf16[128,32,8]{0,2,1:T(8,128)(2,1)S(1)} %fusion.45), channel_id=1, replica_groups=mesh['dp'=32,'feat'=16] {'dp'}, dimensions={1} | all-to-all | bytes 131072 | tf_op jit(solution)/shard_map/all_to_all | solution.py:48
  125.4 0.0 all-gather.7.cloned.1.call-update
  125.4 0.0 all-gather.9.cloned.1.call-start
  125.5 1.5 fusion.15
  127.0 0.0 all-gather.9.cloned.1.call-update
  127.0 0.0 reduce-scatter.5.cloned.1.call-start
  127.1 65.8 %all-gather.7.cloned.1.call-done = bf16[4096,128]{0,1:T(8,128)(2,1)} async-done(((bf16[4096,8]{0,1:T(8,128)(2,1)}), bf16[4096,128]{0,1:T(8,128)(2,1)}) %all-gather.7.cloned.1.call-update) | async-done | bytes 1048592 | tf_op jit(solution)/shard_map/all_gather | solution.py:49
  192.8 90.1 %all-gather.9.cloned.1.call-done = bf16[4096,256]{1,0:T(8,128)(2,1)} async-done(((bf16[128,256]{1,0:T(8,128)(2,1)}), bf16[4096,256]{1,0:T(8,128)(2,1)}) %all-gather.9.cloned.1.call-update) | async-done | bytes 2097168 | tf_op jit(solution)/shard_map/all_gather | solution.py:47
  282.9 2.7 fusion.46
  285.7 1.9 fusion.1
  287.6 0.0 reduce-scatter.5.cloned.1.call-update
  287.6 0.0 copy-start.3
  287.6 0.0 reduce-scatter.3.cloned.1.call-start
  287.7 2.1 fusion
  289.8 0.0 reduce-scatter.3.cloned.1.call-update
  289.9 0.0 all-gather.17.cloned.1.call-start
  289.9 0.1 copy.9
  290.0 23.5 %all_to_all.71 = bf16[128,32,8]{0,2,1:T(8,128)(2,1)} all-to-all(bf16[128,32,8]{0,2,1:T(8,128)(2,1)S(1)} %bitcast.43), channel_id=1, replica_groups=mesh['dp'=32,'feat'=16] {'dp'}, dimensions={1} | all-to-all | bytes 131072 | tf_op jit(solution)/shard_map/all_to_all | solution.py:52
  313.6 0.0 all-gather.17.cloned.1.call-update
  313.6 0.0 all-gather.15.cloned.1.call-start
  313.6 48.6 %reduce-scatter.5.cloned.1.call-done = bf16[4096,8]{0,1:T(8,128)(2,1)} async-done(((bf16[4096,128]{0,1:T(8,128)(2,1)}), bf16[4096,8]{0,1:T(8,128)(2,1)}) %reduce-scatter.5.cloned.1.call-update) | async-done | bytes 65552 | tf_op jit(solution)/shard_map/reduce_scatter | solution.py:82
  362.2 38.1 %all_to_all.72 = bf16[32,128,8]{1,2,0:T(8,128)(2,1)S(1)} all-to-all(bf16[32,128,8]{1,2,0:T(8,128)(2,1)} %bitcast.45), channel_id=1, replica_groups=mesh['dp'=32,'feat'=16] {'dp'}, dimensions={0} | all-to-all | bytes 131072 | tf_op jit(solution)/shard_map/all_to_all | solution.py:85
  400.3 0.1 convert_reduce_fusion.3
  400.4 0.1 reduce_sum.81
  400.5 0.2 fusion.12
  400.7 93.7 %reduce-scatter.3.cloned.1.call-done = bf16[128,256]{1,0:T(8,128)(2,1)} async-done(((bf16[4096,256]{1,0:T(8,128)(2,1)}), bf16[128,256]{1,0:T(8,128)(2,1)}) %reduce-scatter.3.cloned.1.call-update) | async-done | bytes 65552 | tf_op jit(solution)/shard_map/reduce_scatter | solution.py:75
  494.4 0.9 convert_reduce_fusion
  495.3 85.5 %all-reduce = (f32[256]{0:T(256)S(1)}, f32[256]{0:T(256)S(1)}, f32[256]{0:T(256)S(1)}, f32[256]{0:T(256)S(1)}) all-reduce(f32[256]{0:T(256)S(1)} %fusion.12, f32[256]{0:T(256)S(1)} %reduce_sum.81, f32[256]{0:T(256)S(1)} %get-tuple-element.6, f32[256]{0:T(256)S(1)} %get-tuple-element.5), channel_id=1, replica_groups=mesh['dp'=32,'feat'=16] {'dp'}, use_global_device_ids=true, to_apply=%region_17.18 | all-reduce | flops 1024 | bytes 8192 | tf_op jit(solution)/shard_map/psum | solution.py:89
  580.8 0.8 fusion.11
  581.6 0.0 all-gather.15.cloned.1.call-update
  581.7 0.0 all-gather.13.cloned.1.call-start
  581.7 0.1 copy.8
  581.8 21.9 %all_to_all.73 = bf16[128,32,8]{0,2,1:T(8,128)(2,1)} all-to-all(bf16[128,32,8]{0,2,1:T(8,128)(2,1)S(1)} %bitcast.44), channel_id=1, replica_groups=mesh['dp'=32,'feat'=16] {'dp'}, dimensions={1} | all-to-all | bytes 131072 | tf_op jit(solution)/shard_map/all_to_all | solution.py:51
  603.7 0.0 all-gather.13.cloned.1.call-update
  603.8 0.0 all-gather.11.cloned.1.call-start
  603.8 1.5 fusion.8
  605.4 0.0 all-gather.11.cloned.1.call-update
  605.4 0.0 all-gather.17.cloned.1.call-done
  605.4 60.4 %all-gather.15.cloned.1.call-done = bf16[4096,256]{0,1:T(8,128)(2,1)} async-done(((bf16[128,256]{0,1:T(8,128)(2,1)}), bf16[4096,256]{0,1:T(8,128)(2,1)}) %all-gather.15.cloned.1.call-update) | async-done | bytes 2097168 | tf_op jit(solution)/shard_map/all_gather | solution.py:91
  665.8 2.7 fusion.47
  668.5 70.3 %all-gather.13.cloned.1.call-done = bf16[4096,128]{0,1:T(8,128)(2,1)} async-done(((bf16[4096,8]{0,1:T(8,128)(2,1)}), bf16[4096,128]{0,1:T(8,128)(2,1)}) %all-gather.13.cloned.1.call-update) | async-done | bytes 1048592 | tf_op jit(solution)/shard_map/all_gather | solution.py:55
  738.8 90.6 %all-gather.11.cloned.1.call-done = bf16[4096,256]{1,0:T(8,128)(2,1)} async-done(((bf16[128,256]{1,0:T(8,128)(2,1)}), bf16[4096,256]{1,0:T(8,128)(2,1)}) %all-gather.11.cloned.1.call-update) | async-done | bytes 2097168 | tf_op jit(solution)/shard_map/all_gather | solution.py:81
  829.3 3.0 fusion.3
  (16 shorter events, 0.1 us)
Async XLA Ops:
  6.5 186.3 %all-gather.7.cloned.1.call-start = ((), (), s32[]{:S(2)}) async-start(), calls=%async_computation.6 | async-start | bytes 1114112 | tf_op jit(solution)/shard_map/all_gather | solution.py:49
  125.4 157.5 %all-gather.9.cloned.1.call-start = ((), (), s32[]{:S(2)}) async-start(), calls=%async_computation.7 | async-start | bytes 2162688 | tf_op jit(solution)/shard_map/all_gather | solution.py:47
  127.0 235.2 %reduce-scatter.5.cloned.1.call-start = ((), (), s32[]{:S(2)}) async-start(), calls=%async_computation.11 | async-start | bytes 1114112 | tf_op jit(solution)/shard_map/reduce_scatter | solution.py:82
  282.9 2.8 copy-start
  285.7 2.0 copy-start.1
  287.6 2.3 copy-start.3
  287.6 206.8 %reduce-scatter.3.cloned.1.call-start = ((), (), s32[]{:S(2)}) async-start(), calls=%async_computation.8 | async-start | bytes 2162688 | tf_op jit(solution)/shard_map/reduce_scatter | solution.py:75
  289.8 204.6 %copy-start.2 = (bf16[128,256]{1,0:T(8,128)(2,1)S(1)}, bf16[128,256]{1,0:T(8,128)(2,1)}, u32[]{:S(2)}) copy-start(bf16[128,256]{1,0:T(8,128)(2,1)} %param.6) | copy-start | bytes 196612
  289.8 291.9 %copy-start.4 = (bf16[128,256]{1,0:T(8,128)(2,1)S(1)}, bf16[128,256]{1,0:T(8,128)(2,1)}, u32[]{:S(2)}) copy-start(bf16[128,256]{1,0:T(8,128)(2,1)} %param.4) | copy-start | bytes 196612
  289.9 315.5 %all-gather.17.cloned.1.call-start = ((), (), s32[]{:S(2)}) async-start(), calls=%async_computation.13 | async-start | bytes 1114112 | tf_op jit(solution)/shard_map/all_gather | solution.py:56
  313.6 352.2 %all-gather.15.cloned.1.call-start = ((), (), s32[]{:S(2)}) async-start(), calls=%async_computation.12 | async-start | bytes 2162688 | tf_op jit(solution)/shard_map/all_gather | solution.py:91
  581.7 157.1 %all-gather.13.cloned.1.call-start = ((), (), s32[]{:S(2)}) async-start(), calls=%async_computation.10 | async-start | bytes 1114112 | tf_op jit(solution)/shard_map/all_gather | solution.py:55
  603.8 225.5 %all-gather.11.cloned.1.call-start = ((), (), s32[]{:S(2)}) async-start(), calls=%async_computation.9 | async-start | bytes 2162688 | tf_op jit(solution)/shard_map/all_gather | solution.py:81
Sparse Core Ops, SparseCore 0:
  125.5 67.2 all-gather.6
  196.0 86.8 all-gather.8
  287.7 74.4 reduce-scatter.4
  367.1 127.2 reduce-scatter.2
  496.5 72.0 all-gather.16
  581.8 83.9 all-gather.14
  668.1 70.6 all-gather.12
  742.4 86.9 all-gather.10
where the time goes:
time: 840 us; the launch traced here: 839 us
  waiting for transfers between devices  519 us (62%)
  blocking collectives  286 us (34%)
  between operations  13.6 us (2%)
  matrix products  12.5 us (1%)
    reduce_scatter x1, waiting for transfers between devices, body(): lax.psum_scatter(part_a.astype(jnp.bfloat16), 'dp', scatter_dimension=0,...  93.7 us
    psum x1, blocking collectives, body(): lax.psum((jnp.sum(floats_a, axis=0), jnp.sum(floats_a * floats_a, axis=0)...  90.7 us
    all_gather x1, waiting for transfers between devices, body(): lax.all_gather(dz_a, 'dp', axis=0, tiled=True)  90.6 us
    all_gather x1, waiting for transfers between devices, body(): all_a = lax.all_gather(zn_a, 'dp', axis=0, tiled=True)  90.1 us
    psum x1, blocking collectives, body(): lax.psum((jnp.sum(dzn_b, axis=0), jnp.sum(dzn_b * zn_b_floats, axis=0)),...  85.5 us
    all_gather x1, waiting for transfers between devices, body(): lax.all_gather(input_pieces[0], 'feat', axis=1, tiled=True)  70.3 us
    all_gather x1, waiting for transfers between devices, body(): cols_b = lax.all_gather(pieces_b, 'feat', axis=1, tiled=True)  65.8 us
    all_gather x1, waiting for transfers between devices, body(): lax.all_gather(dz_b, 'dp', axis=0, tiled=True)  60.4 us
  transfers between devices with their start and end apart: 8, of which 7 were waited for; matrix products, arithmetic and copies ran while one was open for 1% of the time, Pallas kernels for 0%

commit v1 on v0

v1 whole, which is shorter than its diff:
```python
import jax
import jax.numpy as jnp
from jax import lax
from jax.sharding import Mesh, PartitionSpec as P

epsilon = 1e-05
off_weight = 0.0051

SIZES = (("y", 4), ("zh", 4), ("c", 2), ("zl", 4), ("x", 4))
DP = ("y", "zh", "c")
FEAT = ("zl", "x")
bf16 = jnp.bfloat16
f32 = jnp.float32


def gather(block, axis):
    count = lax.axis_size(axis)
    copies = jnp.broadcast_to(block[None], (count, *block.shape))
    return lax.all_to_all(copies, axis, 0, 0, tiled=True)


def stats(total, squares, pair_count):
    mean = total / pair_count
    variance = squares / pair_count - mean * mean
    return mean, lax.rsqrt(variance + epsilon)


def dot(left, right, dims):
    return lax.dot_general(left, right, (dims, ((), ())), preferred_element_type=f32)


def body(h_a, h_b, z_a, z_b):
    local_rows, width = z_a.shape
    n_dp = lax.axis_size(DP)
    n_feat = lax.axis_size(FEAT)
    n_y, n_zh, n_c = (lax.axis_size(a) for a in DP)
    n_zl, n_x = (lax.axis_size(a) for a in FEAT)
    pairs = local_rows * n_dp
    sub = width // n_dp
    owned = n_feat * sub

    with jax.named_scope("columns"):
        cut = jnp.stack([v.T.reshape(n_dp, sub, local_rows) for v in (z_b, h_a, h_b)], axis=1)
        cut = lax.all_to_all(cut, DP, 0, 0, tiled=True)
        cut = cut.reshape(n_y, n_zh, n_c, 3, sub, local_rows)
        cut = cut.transpose(3, 4, 2, 0, 1, 5).reshape(3, sub, pairs)

    with jax.named_scope("rows"):
        rows = jnp.concatenate([z_a, z_b], axis=1)
        rows = gather(rows, "zh")
        rows = gather(rows, "y")
        rows = gather(rows, "c").reshape(pairs, 2 * width)

    with jax.named_scope("cols_b"):
        cols_b = gather(gather(cut[0], "zl"), "x").reshape(owned, pairs)
    with jax.named_scope("cols_h"):
        cols_h = gather(gather(cut[1:], "zl"), "x").reshape(2 * owned, pairs)

    with jax.named_scope("normalize"):
        floats = rows.astype(f32)
        mean, inverse = stats(jnp.sum(floats, 0), jnp.sum(floats * floats, 0), pairs)
        normed = ((floats - mean) * inverse).astype(bf16)
        floats_b = cols_b.astype(f32)
        mean_b, inverse_b = stats(jnp.sum(floats_b, 1), jnp.sum(floats_b * floats_b, 1), pairs)
        normed_b = ((floats_b - mean_b[:, None]) * inverse_b[:, None]).astype(bf16)

    with jax.named_scope("grad"):
        corr = dot(normed_b, normed[:, :width], ((1,), (0,))) / pairs
        f_index = lax.axis_index(FEAT)
        p_index = lax.axis_index(DP)
        lane = lax.broadcasted_iota(jnp.int32, (owned, width), 1)
        row = lax.broadcasted_iota(jnp.int32, (owned, width), 0)
        row_f = (row // sub % n_zl) * n_x + row // (sub * n_zl)
        diagonal = (row_f == f_index) & (p_index * sub + row % sub == lane)
        grad = jnp.where(diagonal, -2.0 * (1.0 - corr), 2.0 * off_weight * corr).astype(bf16)

    with jax.named_scope("grad_rows"):
        grads = gather(gather(gather(grad, "zh"), "y"), "c")
        grads = grads.reshape(n_c, n_y, n_zh, n_x, n_zl, sub, width)
        grads = grads.transpose(3, 4, 1, 2, 0, 5, 6).reshape(n_x, n_zl, width, width)

    with jax.named_scope("products"):
        prod = dot(cols_h, normed, ((1,), (0,))).reshape(n_x, n_zl, 2, sub, 2, width)
        h_sum = jnp.sum(cols_h.astype(f32), 1).reshape(n_x, n_zl, 2, sub)
        h_sum = h_sum.transpose(2, 0, 1, 3).reshape(2, owned)
        z_sum = jnp.sum(normed.astype(f32), 0).reshape(2, width)
        prod = prod.transpose(2, 4, 0, 1, 3, 5).reshape(2, 2, owned, width)
        p_ab = (prod[0, 1] - h_sum[0][:, None] * z_sum[1] / pairs).astype(bf16)
        p_ba = (prod[1, 0] - h_sum[1][:, None] * z_sum[0] / pairs).astype(bf16)
        p_ab_all = gather(gather(p_ab.T, "zl"), "x").reshape(n_feat * width, owned)

    with jax.named_scope("moments"):
        g = grads.astype(f32)
        four = lambda d: lax.broadcasted_iota(jnp.int32, g.shape, d)
        on = (four(1) * n_x + four(0) == f_index) & (four(2) == four(3))
        weighed = g * jnp.where(on, 1.0 + 0.5 * g, g * (0.5 / off_weight)) / pairs
        second_a = jnp.sum(weighed, (0, 1, 2))
        part_b = jnp.sum(weighed, 3)

    with jax.named_scope("weight_b"):
        flat = grads.reshape(n_feat * width, width)
        w_b = dot(flat, p_ba, ((1,), (1,))).astype(bf16).reshape(n_x, n_zl, width, owned)

        def with_moments(w, m):
            high = m.astype(bf16)
            low = (m - high.astype(f32)).astype(bf16)
            lead = m.shape[:-1]
            extra = jnp.concatenate(
                [high.reshape(*lead, -1, owned), low.reshape(*lead, -1, owned)], axis=-2
            )
            pad = jnp.zeros((*lead, 16 - extra.shape[-2], owned), bf16)
            return jnp.concatenate([w, extra, pad], axis=-2)

        def parted(total):
            n_extra = width // owned
            m = total[..., width : width + n_extra, :] + total[..., width + n_extra : width + 2 * n_extra, :]
            return total[..., :width, :], m.reshape(*m.shape[:-2], width)

        got = lax.all_to_all(with_moments(w_b, part_b), "x", 0, 0, tiled=True)
        w, m = parted(jnp.sum(got.astype(f32), 0))
        got = lax.all_to_all(with_moments(w.astype(bf16), m), "zl", 0, 0, tiled=True)
        w_b, second_b = parted(jnp.sum(got.astype(f32), 0))

    with jax.named_scope("weight_a"):
        w_a = dot(p_ab_all, flat, ((0,), (0,)))

    with jax.named_scope("finish"):
        inv_a, inv_b = inverse[:width], inverse[width:]
        result = inv_a * (w_a - pairs * prod[0, 0] * second_a)
        result = result + inv_b * (w_b.T - pairs * prod[1, 1] * second_b)
        result = result.reshape(n_x, n_zl, sub, width).transpose(1, 0, 2, 3)
        return result.reshape(n_feat, 1, sub, width)


def solution(mesh):
    names = tuple(n for n, _ in SIZES)
    fine = Mesh(mesh.devices.reshape(tuple(s for _, s in SIZES)), names)
    spec = P(DP, FEAT)
    return jax.shard_map(
        body,
        mesh=fine,
        in_specs=(spec, spec, spec, spec),
        out_specs=P(None, DP, None, FEAT),
        check_vma=False,
    )
```

time: 840 us -> 315 us (0.38)
  waiting for transfers between devices: 519 us -> 102 us
  blocking collectives: 286 us -> 101 us
  starting transfers between devices: 0.29 us -> 43.2 us
  local copies, waits for them, and re-layouts: 1.28 us -> 36.8 us
  between operations: 13.6 us -> 0.39 us
  other arithmetic: 6.26 us -> 18.9 us
    all_gather x6 -> x0, waiting for transfers between devices: 377 us -> none  [the longest x1 90.6 us: body(): lax.all_gather(dz_a, 'dp', axis=0, tiled=True)]
    psum x2 -> x0, blocking collectives: 176 us -> none  [the longest x1 90.7 us: body(): lax.psum((jnp.sum(floats_a, axis=0), jnp.sum(floats_a * floats_a, axis=0)...]
    reduce_scatter x2 -> x0, waiting for transfers between devices: 142 us -> none  [the longest x1 93.7 us: body(): lax.psum_scatter(part_a.astype(jnp.bfloat16), 'dp', scatter_dimension=0,...]
    all_to_all x0 -> x10, waiting for transfers between devices: none -> 102 us  [the longest x9 88 us: gather(): return lax.all_to_all(copies, axis, 0, 0, tiled=True)]
    all_to_all x0 -> x10, starting transfers between devices: none -> 43.2 us  [the longest x9 39.6 us: gather(): return lax.all_to_all(copies, axis, 0, 0, tiled=True)]
    broadcast_in_dim x0 -> x13, local copies, waits for them, and re-layouts: none -> 13.2 us  [the longest x12 13.2 us: gather(): copies = jnp.broadcast_to(block[None], (count, *block.shape))]
    all_to_all x0 -> x3, local copies, waits for them, and re-layouts: none -> 10.2 us  [gather(): return lax.all_to_all(copies, axis, 0, 0, tiled=True)]
    all_to_all x4 -> x5, blocking collectives: 110 us -> 101 us  [the longest x3 52.1 us: gather(): return lax.all_to_all(copies, axis, 0, 0, tiled=True)]
  transfers between devices with their start and end apart: 8 -> 10, of which waited for: 7 -> 10; matrix products, arithmetic and copies ran while one was open for 1% -> 13% of each run, Pallas kernels for 0% -> 0%
where the time goes in v1:
time: 315 us; the launch traced here: 311 us
  waiting for transfers between devices  102 us (32%)
  blocking collectives  101 us (32%)
  starting transfers between devices  43.2 us (14%)
  local copies, waits for them, and re-layouts  36.8 us (12%)
  other arithmetic  18.9 us (6%)
  matrix products  8.72 us (3%)
    all_to_all x9, waiting for transfers between devices, gather(): return lax.all_to_all(copies, axis, 0, 0, tiled=True)  88 us
    all_to_all x3, blocking collectives, gather(): return lax.all_to_all(copies, axis, 0, 0, tiled=True)  52.1 us
    all_to_all x9, starting transfers between devices, gather(): return lax.all_to_all(copies, axis, 0, 0, tiled=True)  39.6 us
    all_to_all x1, blocking collectives, body(): cut = lax.all_to_all(cut, DP, 0, 0, tiled=True)  38.8 us
    all_to_all x1, waiting for transfers between devices, body(): got = lax.all_to_all(with_moments(w_b, part_b), 'x', 0, 0, tiled=True)  14.3 us
    broadcast_in_dim x12, local copies, waits for them, and re-layouts, gather(): copies = jnp.broadcast_to(block[None], (count, *block.shape))  13.2 us
    all_to_all x1, blocking collectives, body(): lax.all_to_all(with_moments(w.astype(bf16), m), 'zl', 0, 0, tiled=True)  10.4 us
    all_to_all x3, local copies, waits for them, and re-layouts, gather(): return lax.all_to_all(copies, axis, 0, 0, tiled=True)  10.2 us
  transfers between devices with their start and end apart: 10, of which 10 were waited for; matrix products, arithmetic and copies ran while one was open for 13% of the time, Pallas kernels for 0%

profile of v1, /device:TPU:1, one launch (start us, length us, event | category | flops | bytes accessed | tf_op | source)
XLA Modules:
  0.0 311.4 jit_solution(15733525801431470911)
XLA Ops:
  0.0 0.9 copy.78
  1.0 1.0 copy.79
  1.9 1.0 copy.77
  3.0 38.8 %all_to_all.75 = bf16[32,3,8,128]{3,2,1,0:T(8,128)(2,1)S(1)} all-to-all(bf16[32,3,8,128]{3,2,1,0:T(8,128)(2,1)S(1)} %copy.80), channel_id=1, replica_groups=mesh['y'=4,'zh'=4,'c'=2,'zl'=4,'x'=4] {'y','zh','c'}, dimensions={0} | all-to-all | bytes 393216 | tf_op jit(solution)/shard_map/columns/all_to_all | solution.py:44
  42.5 4.0 %all-to-all-start.8 = ((bf16[4,8,4096]{2,1,0:T(8,128)(2,1)}), bf16[4,8,4096]{2,1,0:T(8,128)(2,1)S(1)}, u32[]{:S(2)}, u32[]{:S(2)}) async-start(bf16[4,8,4096]{2,1,0:T(8,128)(2,1)} %broadcast_in_dim.41), calls=%async_computation.8 | async-start | bytes 524288 | tf_op jit(solution)/shard_map/cols_b/all_to_all | solution.py:19
  47.5 6.4 %all-to-all-done.8 = bf16[4,8,4096]{2,1,0:T(8,128)(2,1)S(1)} async-done(((bf16[4,8,4096]{2,1,0:T(8,128)(2,1)}), bf16[4,8,4096]{2,1,0:T(8,128)(2,1)S(1)}, u32[]{:S(2)}, u32[]{:S(2)}) %all-to-all-start.8) | async-done | bytes 262176 | tf_op jit(solution)/shard_map/cols_b/all_to_all | solution.py:19
  53.9 29.9 %all_to_all.76 = bf16[4,128,512]{1,2,0:T(8,128)(2,1)S(1)} all-to-all(bf16[4,128,512]{1,2,0:T(8,128)(2,1)S(1)} %broadcast_in_dim.32), channel_id=1, replica_groups=mesh['y'=4,'zh'=4,'c'=2,'zl'=4,'x'=4] {'zh'}, dimensions={0} | all-to-all | bytes 1048576 | tf_op jit(solution)/shard_map/rows/all_to_all | solution.py:19
  83.8 1.1 broadcast_in_dim.42
  84.9 4.0 %all-to-all-start.9 = ((bf16[4,4,8,4096]{3,2,1,0:T(8,128)(2,1)}), bf16[4,4,8,4096]{3,2,1,0:T(8,128)(2,1)S(1)}, u32[]{:S(2)}, u32[]{:S(2)}) async-start(bf16[4,4,8,4096]{3,2,1,0:T(8,128)(2,1)} %broadcast_in_dim.42), calls=%async_computation.9 | async-start | bytes 2097152 | tf_op jit(solution)/shard_map/cols_b/all_to_all | solution.py:19
  89.3 13.3 %all-to-all-done.9 = bf16[4,4,8,4096]{3,2,1,0:T(8,128)(2,1)S(1)} async-done(((bf16[4,4,8,4096]{3,2,1,0:T(8,128)(2,1)}), bf16[4,4,8,4096]{3,2,1,0:T(8,128)(2,1)S(1)}, u32[]{:S(2)}, u32[]{:S(2)}) %all-to-all-start.9) | async-done | bytes 1048608 | tf_op jit(solution)/shard_map/cols_b/all_to_all | solution.py:19
  102.6 1.9 broadcast_in_dim.33
  104.5 3.6 %all-to-all-start.1 = ((bf16[4,4,128,512]{2,1,3,0:T(4,128)(2,1)}), bf16[4,4,128,512]{2,1,3,0:T(4,128)(2,1)S(1)}, u32[]{:S(2)}, u32[]{:S(2)}) async-start(bf16[4,4,128,512]{2,1,3,0:T(4,128)(2,1)} %broadcast_in_dim.33), calls=%async_computation.1 | async-start | bytes 4194304 | tf_op jit(solution)/shard_map/rows/all_to_all | solution.py:19
  108.3 22.7 %all-to-all-done.1 = bf16[4,4,128,512]{2,1,3,0:T(4,128)(2,1)S(1)} async-done(((bf16[4,4,128,512]{2,1,3,0:T(4,128)(2,1)}), bf16[4,4,128,512]{2,1,3,0:T(4,128)(2,1)S(1)}, u32[]{:S(2)}, u32[]{:S(2)}) %all-to-all-start.1) | async-done | bytes 2097184 | tf_op jit(solution)/shard_map/rows/all_to_all | solution.py:19
  132.0 7.1 %all-to-all-start.4 = ((bf16[4,2,8,4096]{3,2,1,0:T(8,128)(2,1)}), bf16[4,2,8,4096]{3,2,1,0:T(8,128)(2,1)}, u32[]{:S(2)}, u32[]{:S(2)}) async-start(bf16[4,2,8,4096]{3,2,1,0:T(8,128)(2,1)} %broadcast_in_dim.36), calls=%async_computation.4 | async-start | bytes 1048576 | tf_op jit(solution)/shard_map/cols_h/all_to_all | solution.py:19
  139.7 1.4 fusion.13
  141.0 2.3 copy.75
  143.3 6.8 %all-to-all-done.4 = bf16[4,2,8,4096]{3,2,1,0:T(8,128)(2,1)} async-done(((bf16[4,2,8,4096]{3,2,1,0:T(8,128)(2,1)}), bf16[4,2,8,4096]{3,2,1,0:T(8,128)(2,1)}, u32[]{:S(2)}, u32[]{:S(2)}) %all-to-all-start.4) | async-done | bytes 524320 | tf_op jit(solution)/shard_map/cols_h/all_to_all | solution.py:19
  150.1 1.1 broadcast_in_dim.34
  151.2 12.3 %all_to_all.77 = bf16[2,4,4,128,512]{3,2,1,4,0:T(4,128)(2,1)} all-to-all(bf16[2,4,4,128,512]{3,2,1,4,0:T(4,128)(2,1)S(1)} %broadcast_in_dim.34), channel_id=1, replica_groups=mesh['y'=4,'zh'=4,'c'=2,'zl'=4,'x'=4] {'c'}, dimensions={0} | all-to-all | bytes 8388608 | tf_op jit(solution)/shard_map/rows/all_to_all | solution.py:19
  163.5 2.6 broadcast_in_dim.37
  166.1 3.6 %all-to-all-start.5 = ((bf16[4,4,2,8,4096]{4,3,2,1,0:T(8,128)(2,1)}), bf16[4,4,2,8,4096]{4,3,2,1,0:T(8,128)(2,1)S(1)}, u32[]{:S(2)}, u32[]{:S(2)}) async-start(bf16[4,4,2,8,4096]{4,3,2,1,0:T(8,128)(2,1)} %broadcast_in_dim.37), calls=%async_computation.5 | async-start | bytes 4194304 | tf_op jit(solution)/shard_map/cols_h/all_to_all | solution.py:19
  169.7 7.4 %copy.76 = bf16[2,4,4,128,512]{4,3,2,1,0:T(8,128)(2,1)} copy(bf16[2,4,4,128,512]{3,2,1,4,0:T(4,128)(2,1)} %all_to_all.77) | data formatting | bytes 8388608 | tf_op jit(solution)/shard_map/rows/all_to_all | solution.py:19
  177.2 3.6 %convert_reduce_fusion.1 = (f32[512]{0:T(512)S(1)}, f32[512]{0:T(512)S(1)}) fusion(bf16[2,4,4,128,512]{4,3,2,1,0:T(8,128)(2,1)} %copy.76), kind=kLoop, calls=%fused_computation.9 | loop fusion | flops 8387584 | bytes 4198400 | tf_op jit(solution)/shard_map/normalize/reduce_sum | solution.py:61
  180.8 3.0 fusion.1
  183.8 6.6 %copy.92 = bf16[512,4096]{1,0:T(8,128)(2,1)} copy(bf16[512,4096]{0,1:T(8,128)(2,1)} %bitcast.95) | data formatting | bytes 8388608 | tf_op jit(solution)/shard_map/products/dot_general | solution.py:29
  190.4 2.1 select_convert_fusion
  192.5 3.3 %all-to-all-done.5 = bf16[4,4,2,8,4096]{4,3,2,1,0:T(8,128)(2,1)S(1)} async-done(((bf16[4,4,2,8,4096]{4,3,2,1,0:T(8,128)(2,1)}), bf16[4,4,2,8,4096]{4,3,2,1,0:T(8,128)(2,1)S(1)}, u32[]{:S(2)}, u32[]{:S(2)}) %all-to-all-start.5) | async-done | bytes 2097184 | tf_op jit(solution)/shard_map/cols_h/all_to_all | solution.py:19
  196.5 6.1 %all-to-all-start.10 = ((bf16[4,128,256]{2,1,0:T(8,128)(2,1)}), bf16[4,128,256]{2,1,0:T(8,128)(2,1)S(1)}, u32[]{:S(2)}, u32[]{:S(2)}) async-start(bf16[4,128,256]{2,1,0:T(8,128)(2,1)} %broadcast_in_dim.43), calls=%async_computation.10 | async-start | bytes 524288 | tf_op jit(solution)/shard_map/grad_rows/all_to_all | solution.py:19
  202.6 3.3 %convert_reduce_fusion = f32[512]{0:T(512)S(1)} fusion(bf16[2,4,4,128,512]{4,3,2,1,0:T(8,128)(2,1)} %copy.76, f32[512]{0:T(512)S(1)} %get-tuple-element.22, f32[512]{0:T(512)S(1)} %get-tuple-element.21), kind=kLoop, calls=%fused_computation.3 | loop fusion | flops 12582400 | bytes 4200448 | tf_op jit(solution)/shard_map/products/reduce_sum | solution.py:86
  206.5 11.2 %all-to-all-done.10 = bf16[4,128,256]{2,1,0:T(8,128)(2,1)S(1)} async-done(((bf16[4,128,256]{2,1,0:T(8,128)(2,1)}), bf16[4,128,256]{2,1,0:T(8,128)(2,1)S(1)}, u32[]{:S(2)}, u32[]{:S(2)}) %all-to-all-start.10) | async-done | bytes 262176 | tf_op jit(solution)/shard_map/grad_rows/all_to_all | solution.py:19
  217.7 1.1 broadcast_in_dim.44
  218.7 3.7 %all-to-all-start.11 = ((bf16[4,4,128,256]{3,2,1,0:T(8,128)(2,1)}), bf16[4,4,128,256]{3,2,1,0:T(8,128)(2,1)S(1)}, u32[]{:S(2)}, u32[]{:S(2)}) async-start(bf16[4,4,128,256]{3,2,1,0:T(8,128)(2,1)} %broadcast_in_dim.44), calls=%async_computation.11 | async-start | bytes 2097152 | tf_op jit(solution)/shard_map/grad_rows/all_to_all | solution.py:19
  222.4 3.5 %fusion.14 = f32[2,2,4,4,8,256]{5,4,1,0,3,2:T(8,128)S(1)} fusion(bf16[2,256,4096,1,1,1]{2,1,0,5,4,3:T(8,128)(2,1)} %bitcast.97, bf16[4,4,2,8,4096]{4,3,2,1,0:T(8,128)(2,1)S(1)} %all-to-all-done.5), kind=kOutput, calls=%fused_computation.29 | convolution fusion | flops 1073741824 | bytes 6815744 | tf_op jit(solution)/shard_map/products/dot_general | solution.py:29
  226.8 6.6 %all-to-all-done.11 = bf16[4,4,128,256]{3,2,1,0:T(8,128)(2,1)S(1)} async-done(((bf16[4,4,128,256]{3,2,1,0:T(8,128)(2,1)}), bf16[4,4,128,256]{3,2,1,0:T(8,128)(2,1)S(1)}, u32[]{:S(2)}, u32[]{:S(2)}) %all-to-all-start.11) | async-done | bytes 1048608 | tf_op jit(solution)/shard_map/grad_rows/all_to_all | solution.py:19
  233.6 10.0 %all_to_all.78 = bf16[2,4,4,128,256]{4,3,2,1,0:T(8,128)(2,1)S(1)} all-to-all(bf16[2,4,4,128,256]{4,3,2,1,0:T(8,128)(2,1)S(1)} %broadcast_in_dim.45), channel_id=1, replica_groups=mesh['y'=4,'zh'=4,'c'=2,'zl'=4,'x'=4] {'c'}, dimensions={0} | all-to-all | bytes 4194304 | tf_op jit(solution)/shard_map/grad_rows/all_to_all | solution.py:19
  243.8 2.5 fusion.7
  246.9 1.7 convolution_convert_fusion
  248.6 1.3 maximum_maximum_fusion
  249.9 3.5 %all-to-all-start.13 = ((bf16[4,4,272,128]{3,2,1,0:T(8,128)(2,1)}), bf16[4,4,272,128]{3,2,1,0:T(8,128)(2,1)S(1)}, u32[]{:S(2)}, u32[]{:S(2)}) async-start(bf16[4,4,272,128]{3,2,1,0:T(8,128)(2,1)} %maximum_maximum_fusion), calls=%async_computation.13 | async-start | bytes 2228224 | tf_op jit(solution)/shard_map/weight_b/all_to_all | solution.py:119
  253.5 1.0 fusion.33
  254.6 14.3 %all-to-all-done.13 = bf16[4,4,272,128]{3,2,1,0:T(8,128)(2,1)S(1)} async-done(((bf16[4,4,272,128]{3,2,1,0:T(8,128)(2,1)}), bf16[4,4,272,128]{3,2,1,0:T(8,128)(2,1)S(1)}, u32[]{:S(2)}, u32[]{:S(2)}) %all-to-all-start.13) | async-done | bytes 1114144 | tf_op jit(solution)/shard_map/weight_b/all_to_all | solution.py:119
  269.6 4.0 %all-to-all-start.6 = ((bf16[4,256,128]{2,1,0:T(8,128)(2,1)}), bf16[4,256,128]{2,1,0:T(8,128)(2,1)}, u32[]{:S(2)}, u32[]{:S(2)}) async-start(bf16[4,256,128]{2,1,0:T(8,128)(2,1)} %broadcast_in_dim.38), calls=%async_computation.6 | async-start | bytes 524288 | tf_op jit(solution)/shard_map/products/all_to_all | solution.py:19
  274.0 7.3 %all-to-all-done.6 = bf16[4,256,128]{2,1,0:T(8,128)(2,1)} async-done(((bf16[4,256,128]{2,1,0:T(8,128)(2,1)}), bf16[4,256,128]{2,1,0:T(8,128)(2,1)}, u32[]{:S(2)}, u32[]{:S(2)}) %all-to-all-start.6) | async-done | bytes 262176 | tf_op jit(solution)/shard_map/products/all_to_all | solution.py:19
  281.3 10.4 %all_to_all.79 = bf16[4,272,128]{2,1,0:T(8,128)(2,1)S(1)} all-to-all(bf16[4,272,128]{2,1,0:T(8,128)(2,1)S(1)} %maximum_maximum_fusion.1), channel_id=1, replica_groups=mesh['y'=4,'zh'=4,'c'=2,'zl'=4,'x'=4] {'zl'}, dimensions={0} | all-to-all | bytes 557056 | tf_op jit(solution)/shard_map/weight_b/all_to_all | solution.py:121
  291.7 2.1 broadcast_in_dim.39
  293.8 3.5 %all-to-all-start.7 = ((bf16[4,4,256,128]{3,2,1,0:T(8,128)(2,1)}), bf16[4,4,256,128]{3,2,1,0:T(8,128)(2,1)S(1)}, u32[]{:S(2)}, u32[]{:S(2)}) async-start(bf16[4,4,256,128]{3,2,1,0:T(8,128)(2,1)} %broadcast_in_dim.39), calls=%async_computation.7 | async-start | bytes 2097152 | tf_op jit(solution)/shard_map/products/all_to_all | solution.py:19
  298.9 10.3 %all-to-all-done.7 = bf16[4,4,256,128]{3,2,1,0:T(8,128)(2,1)S(1)} async-done(((bf16[4,4,256,128]{3,2,1,0:T(8,128)(2,1)}), bf16[4,4,256,128]{3,2,1,0:T(8,128)(2,1)S(1)}, u32[]{:S(2)}, u32[]{:S(2)}) %all-to-all-start.7) | async-done | bytes 1048608 | tf_op jit(solution)/shard_map/products/all_to_all | solution.py:19
  309.3 1.5 fusion.18
  (60 shorter events, 10.6 us)
Async XLA Ops:
  42.5 11.4 %all-to-all-start.8 = ((bf16[4,8,4096]{2,1,0:T(8,128)(2,1)}), bf16[4,8,4096]{2,1,0:T(8,128)(2,1)S(1)}, u32[]{:S(2)}, u32[]{:S(2)}) async-start(bf16[4,8,4096]{2,1,0:T(8,128)(2,1)} %broadcast_in_dim.41), calls=%async_computation.8 | async-start | bytes 524288 | tf_op jit(solution)/shard_map/cols_b/all_to_all | solution.py:19
  84.9 17.8 %all-to-all-start.9 = ((bf16[4,4,8,4096]{3,2,1,0:T(8,128)(2,1)}), bf16[4,4,8,4096]{3,2,1,0:T(8,128)(2,1)S(1)}, u32[]{:S(2)}, u32[]{:S(2)}) async-start(bf16[4,4,8,4096]{3,2,1,0:T(8,128)(2,1)} %broadcast_in_dim.42), calls=%async_computation.9 | async-start | bytes 2097152 | tf_op jit(solution)/shard_map/cols_b/all_to_all | solution.py:19
  104.5 26.6 %all-to-all-start.1 = ((bf16[4,4,128,512]{2,1,3,0:T(4,128)(2,1)}), bf16[4,4,128,512]{2,1,3,0:T(4,128)(2,1)S(1)}, u32[]{:S(2)}, u32[]{:S(2)}) async-start(bf16[4,4,128,512]{2,1,3,0:T(4,128)(2,1)} %broadcast_in_dim.33), calls=%async_computation.1 | async-start | bytes 4194304 | tf_op jit(solution)/shard_map/rows/all_to_all | solution.py:19
  131.1 8.6 %copy-start.1 = (bf16[4,4,128,512]{2,1,3,0:T(4,128)(2,1)}, bf16[4,4,128,512]{2,1,3,0:T(4,128)(2,1)S(1)}, u32[]{:S(2)}) copy-start(bf16[4,4,128,512]{2,1,3,0:T(4,128)(2,1)S(1)} %all-to-all-done.1) | copy-start | bytes 6291460
  132.0 18.2 %all-to-all-start.4 = ((bf16[4,2,8,4096]{3,2,1,0:T(8,128)(2,1)}), bf16[4,2,8,4096]{3,2,1,0:T(8,128)(2,1)}, u32[]{:S(2)}, u32[]{:S(2)}) async-start(bf16[4,2,8,4096]{3,2,1,0:T(8,128)(2,1)} %broadcast_in_dim.36), calls=%async_computation.4 | async-start | bytes 1048576 | tf_op jit(solution)/shard_map/cols_h/all_to_all | solution.py:19
  166.1 29.7 %all-to-all-start.5 = ((bf16[4,4,2,8,4096]{4,3,2,1,0:T(8,128)(2,1)}), bf16[4,4,2,8,4096]{4,3,2,1,0:T(8,128)(2,1)S(1)}, u32[]{:S(2)}, u32[]{:S(2)}) async-start(bf16[4,4,2,8,4096]{4,3,2,1,0:T(8,128)(2,1)} %broadcast_in_dim.37), calls=%async_computation.5 | async-start | bytes 4194304 | tf_op jit(solution)/shard_map/cols_h/all_to_all | solution.py:19
  177.2 3.6 %copy-start = (bf16[2,4,4,128,512]{4,3,2,1,0:T(8,128)(2,1)S(1)}, bf16[2,4,4,128,512]{4,3,2,1,0:T(8,128)(2,1)}, u32[]{:S(2)}) copy-start(bf16[2,4,4,128,512]{4,3,2,1,0:T(8,128)(2,1)} %copy.76) | copy-start | bytes 12582916
  183.8 6.6 %copy-start.2 = (bf16[128,4096]{1,0:T(8,128)(2,1)S(1)}, bf16[128,4096]{1,0:T(8,128)(2,1)}, u32[]{:S(2)}) copy-start(bf16[128,4096]{1,0:T(8,128)(2,1)} %fusion.13) | copy-start | bytes 3145732
  196.5 21.1 %all-to-all-start.10 = ((bf16[4,128,256]{2,1,0:T(8,128)(2,1)}), bf16[4,128,256]{2,1,0:T(8,128)(2,1)S(1)}, u32[]{:S(2)}, u32[]{:S(2)}) async-start(bf16[4,128,256]{2,1,0:T(8,128)(2,1)} %broadcast_in_dim.43), calls=%async_computation.10 | async-start | bytes 524288 | tf_op jit(solution)/shard_map/grad_rows/all_to_all | solution.py:19
  218.7 14.6 %all-to-all-start.11 = ((bf16[4,4,128,256]{3,2,1,0:T(8,128)(2,1)}), bf16[4,4,128,256]{3,2,1,0:T(8,128)(2,1)S(1)}, u32[]{:S(2)}, u32[]{:S(2)}) async-start(bf16[4,4,128,256]{3,2,1,0:T(8,128)(2,1)} %broadcast_in_dim.44), calls=%async_computation.11 | async-start | bytes 2097152 | tf_op jit(solution)/shard_map/grad_rows/all_to_all | solution.py:19
  249.9 19.0 %all-to-all-start.13 = ((bf16[4,4,272,128]{3,2,1,0:T(8,128)(2,1)}), bf16[4,4,272,128]{3,2,1,0:T(8,128)(2,1)S(1)}, u32[]{:S(2)}, u32[]{:S(2)}) async-start(bf16[4,4,272,128]{3,2,1,0:T(8,128)(2,1)} %maximum_maximum_fusion), calls=%async_computation.13 | async-start | bytes 2228224 | tf_op jit(solution)/shard_map/weight_b/all_to_all | solution.py:119
  269.6 11.7 %all-to-all-start.6 = ((bf16[4,256,128]{2,1,0:T(8,128)(2,1)}), bf16[4,256,128]{2,1,0:T(8,128)(2,1)}, u32[]{:S(2)}, u32[]{:S(2)}) async-start(bf16[4,256,128]{2,1,0:T(8,128)(2,1)} %broadcast_in_dim.38), calls=%async_computation.6 | async-start | bytes 524288 | tf_op jit(solution)/shard_map/products/all_to_all | solution.py:19
  293.8 15.4 %all-to-all-start.7 = ((bf16[4,4,256,128]{3,2,1,0:T(8,128)(2,1)}), bf16[4,4,256,128]{3,2,1,0:T(8,128)(2,1)S(1)}, u32[]{:S(2)}, u32[]{:S(2)}) async-start(bf16[4,4,256,128]{3,2,1,0:T(8,128)(2,1)} %broadcast_in_dim.39), calls=%async_computation.7 | async-start | bytes 2097152 | tf_op jit(solution)/shard_map/products/all_to_all | solution.py:19
  297.4 0.7 copy-start.3

commit v2 on v1

v2 whole, which is shorter than its diff:
```python
import jax
import jax.numpy as jnp
from jax import lax
from jax.experimental import pallas as pl
from jax.experimental.pallas import tpu as pltpu
from jax.sharding import Mesh, PartitionSpec as P

epsilon = 1e-05
off_weight = 0.0051

SIZES = (("y", 4), ("zh", 4), ("c", 2), ("zl", 4), ("x", 4))
DP = ("y", "zh", "c")
FEAT = ("zl", "x")
bf16 = jnp.bfloat16
f32 = jnp.float32


def gather(block, axis):
    count = lax.axis_size(axis)
    copies = jnp.broadcast_to(block[None], (count, *block.shape))
    return lax.all_to_all(copies, axis, 0, 0, tiled=True)


def stats(total, squares, pair_count):
    mean = total / pair_count
    variance = squares / pair_count - mean * mean
    return mean, lax.rsqrt(variance + epsilon)


def dot(left, right, dims):
    return lax.dot_general(left, right, (dims, ((), ())), preferred_element_type=f32)


def collect(block, axis):
    return lax.all_gather(block, axis, axis=0, tiled=False)


STEP = 256


def at(i):
    return pl.ds(pl.multiple_of(i * STEP, STEP), STEP)


def fold(v):
    return jnp.sum(v.reshape(v.shape[0] // 8, 8, v.shape[1]), 0)


def lanes(v):
    return v[:, :128] + v[:, 128:]


def chunk(halves, side, i):
    own, other = halves
    count = own.shape[0] * own.shape[2] // STEP
    each = STEP // own.shape[2]
    ref = own if i < count else other
    first = (i % count) * each
    return jnp.concatenate([ref[first + j, side] for j in range(each)], axis=0)


def column_stats(halves, side, pairs):
    width = halves[0].shape[3]
    total = squares = jnp.zeros((8, width), f32)
    for i in range(pairs // STEP):
        v = chunk(halves, side, i).astype(f32)
        total, squares = total + fold(v), squares + fold(v * v)
    return stats(jnp.sum(total, 0, keepdims=True), jnp.sum(squares, 0, keepdims=True), pairs)


def row_stats(cols_ref):
    owned, pairs = cols_ref.shape

    def add(i, carry):
        v = cols_ref[:, at(i)].astype(f32)
        return carry[0] + lanes(v), carry[1] + lanes(v * v)

    empty = jnp.zeros((owned, 128), f32)
    total, squares = lax.fori_loop(0, pairs // STEP, add, (empty, empty))
    return stats(jnp.sum(total, 1, keepdims=True), jnp.sum(squares, 1, keepdims=True), pairs)


def normalize(v, mean, inverse):
    return ((v.astype(f32) - mean) * inverse).astype(bf16)


def matmul(left, right):
    return jnp.dot(left, right, preferred_element_type=f32)


def grad_kernel(own_ref, other_ref, cols_ref, target_ref, grad_ref, stats_ref):
    owned, pairs = cols_ref.shape
    halves = (own_ref, other_ref)
    width = grad_ref.shape[1]
    mean, inverse = column_stats(halves, 0, pairs)
    mean_b, inverse_b = row_stats(cols_ref)
    stats_ref[0:8, :] = jnp.broadcast_to(mean, (8, width))
    stats_ref[8:16, :] = jnp.broadcast_to(inverse, (8, width))
    corr = jnp.zeros((owned, width), f32)
    for i in range(pairs // STEP):
        v = normalize(chunk(halves, 0, i), mean, inverse)
        b = normalize(cols_ref[:, pl.ds(i * STEP, STEP)], mean_b, inverse_b)
        corr = corr + matmul(b, v)
    corr = corr / pairs
    diagonal = lax.broadcasted_iota(jnp.int32, (owned, width), 1) == target_ref[...]
    grad_ref[...] = jnp.where(diagonal, -2.0 * (1.0 - corr), 2.0 * off_weight * corr).astype(bf16)


def product_kernel(cols_ref, own_ref, other_ref, stats_ref, prod_ref, centered_ref, inverse_ref):
    owned, pairs = cols_ref.shape
    halves = (own_ref, other_ref)
    width = own_ref.shape[3]
    mean_a, inverse_a = stats_ref[0:1, :], stats_ref[8:9, :]
    mean_b, inverse_b = column_stats(halves, 1, pairs)
    inverse_ref[...] = jnp.broadcast_to(inverse_b, (8, width))
    prod_a = prod_b = jnp.zeros((owned, width), f32)
    sum_a = sum_b = jnp.zeros((8, width), f32)
    sum_h = jnp.zeros((owned, 128), f32)
    for i in range(pairs // STEP):
        h = cols_ref[:, pl.ds(i * STEP, STEP)]
        a = normalize(chunk(halves, 0, i), mean_a, inverse_a)
        b = normalize(chunk(halves, 1, i), mean_b, inverse_b)
        prod_a, prod_b = prod_a + matmul(h, a), prod_b + matmul(h, b)
        sum_a, sum_b = sum_a + fold(a.astype(f32)), sum_b + fold(b.astype(f32))
        sum_h = sum_h + lanes(h.astype(f32))
    sum_h = jnp.sum(sum_h, 1, keepdims=True)
    for side, prod, sums in ((0, prod_a, sum_a), (1, prod_b, sum_b)):
        part = pl.ds(side * width, width)
        sums = jnp.sum(sums, 0, keepdims=True) / pairs
        prod_ref[:, part] = prod
        centered_ref[:, part] = (prod - sum_h * sums).astype(bf16)


def call(kernel, name, flops, shapes, *operands):
    size = lambda v: v.size * v.dtype.itemsize
    moved = sum(size(v) for v in operands) + sum(size(v) for v in shapes)
    return pl.pallas_call(
        kernel,
        out_shape=shapes,
        in_specs=[pl.BlockSpec(memory_space=pltpu.VMEM)] * len(operands),
        out_specs=[pl.BlockSpec(memory_space=pltpu.VMEM)] * len(shapes),
        compiler_params=pltpu.CompilerParams(vmem_limit_bytes=32 * 2**20),
        cost_estimate=pl.CostEstimate(flops=flops, bytes_accessed=moved, transcendentals=0),
        name=name,
    )(*operands)


def body(h_a, h_b, z_a, z_b):
    local_rows, width = z_a.shape
    n_dp = lax.axis_size(DP)
    n_feat = lax.axis_size(FEAT)
    n_y, n_zh, n_c = (lax.axis_size(a) for a in DP)
    n_zl, n_x = (lax.axis_size(a) for a in FEAT)
    pairs = local_rows * n_dp
    sub = width // n_dp
    owned = n_feat * sub
    shape = jax.ShapeDtypeStruct
    together = lax.optimization_barrier

    core = lax.axis_index("c")

    def swap(v):
        return lax.ppermute(v, "c", [(0, 1), (1, 0)])

    with jax.named_scope("columns"):
        cut = jnp.stack([v.T.reshape(n_dp, sub, local_rows) for v in (z_b, h_a, h_b)], axis=1)
        cut = lax.all_to_all(cut, DP, 0, 0, tiled=True)
    with jax.named_scope("rows"):
        rows = collect(jnp.stack([z_a, z_b]), "zh")
    cut, rows = together((cut, rows))
    with jax.named_scope("columns"):
        cut = cut.reshape(n_y, n_zh, n_c, 3, sub, local_rows)
        cut = jnp.where(core == 0, cut, jnp.flip(cut, 2))
        cut = cut.transpose(3, 4, 2, 0, 1, 5).reshape(3, sub, pairs)

    with jax.named_scope("rows"):
        rows = collect(rows, "y")
    with jax.named_scope("columns"):
        cut = collect(cut, "zl")
        cols_b = gather(cut[:, 0], "x").reshape(owned, pairs)
    rows, cols_b, cut = together((rows, cols_b, cut))
    with jax.named_scope("columns"):
        cols_h = collect(cut[:, 1:], "x").reshape(2 * owned, pairs)
    with jax.named_scope("rows"):
        own = rows.reshape(n_y * n_zh, 2, local_rows, width)
        other = swap(own)

    with jax.named_scope("grad"):
        f_index = lax.axis_index(FEAT)
        p_index = lax.axis_index(DP)
        row = lax.broadcasted_iota(jnp.int32, (owned, 1), 0)
        row_f = (row // sub % n_zl) * n_x + row // (sub * n_zl)
        target = jnp.where(row_f == f_index, p_index * sub + row % sub, -1)
        grad, stats_a = call(
            grad_kernel, "grad_block", 2 * pairs * owned * width,
            (shape((owned, width), bf16), shape((16, width), f32)),
            own, other, cols_b, target,
        )

    with jax.named_scope("grad_rows"):
        grads = gather(grad, "zh")
    grads, cols_h = together((grads, cols_h))

    with jax.named_scope("grad_rows"):
        grads = gather(grads, "y")
    with jax.named_scope("products"):
        prod, centered, inverse_b = call(
            product_kernel, "products", 8 * pairs * owned * width,
            (shape((2 * owned, 2 * width), f32), shape((2 * owned, 2 * width), bf16), shape((8, width), f32)),
            cols_h, own, other, stats_a,
        )
        halves = lambda v: v.reshape(n_x * n_zl, 2, sub, 2 * width)
        prod, centered = halves(prod), halves(centered)
        p_aa = prod[:, 0, :, :width].reshape(owned, width)
        p_bb = prod[:, 1, :, width:].reshape(owned, width)
        p_ab = centered[:, 0, :, width:].reshape(owned, width)
        p_ba = centered[:, 1, :, :width].reshape(owned, width)
        p_ab_all = collect(p_ab, "zl")
    grads, p_ab_all, p_ba = together((grads, p_ab_all, p_ba))

    with jax.named_scope("grad_rows"):
        grads = gather(grads, "c")
        grads = grads.reshape(n_c, n_y, n_zh, n_x, n_zl, sub, width)
        grads = grads.transpose(3, 4, 1, 2, 0, 5, 6).reshape(n_x, n_zl, width, width)
    with jax.named_scope("products"):
        p_ab_all = collect(p_ab_all, "x")

    with jax.named_scope("moments"):
        g = grads.astype(f32)
        four = lambda d: lax.broadcasted_iota(jnp.int32, g.shape, d)
        on = (four(1) * n_x + four(0) == f_index) & (four(2) == four(3))
        weighed = g * jnp.where(on, 1.0 + 0.5 * g, g * (0.5 / off_weight)) / pairs
        second_a = jnp.sum(weighed, (0, 1, 2))
        part_b = jnp.sum(weighed, 3)

    with jax.named_scope("weight_b"):
        flat = grads.reshape(n_feat * width, width)
        w_b = dot(flat, p_ba, ((1,), (1,))).astype(bf16).reshape(n_x, n_zl, width, owned)

        def with_moments(w, m):
            high = m.astype(bf16)
            low = (m - high.astype(f32)).astype(bf16)
            lead = m.shape[:-1]
            extra = jnp.concatenate(
                [high.reshape(*lead, -1, owned), low.reshape(*lead, -1, owned)], axis=-2
            )
            pad = jnp.zeros((*lead, 16 - extra.shape[-2], owned), bf16)
            return jnp.concatenate([w, extra, pad], axis=-2)

        def parted(total):
            n_extra = width // owned
            m = total[..., width : width + n_extra, :] + total[..., width + n_extra : width + 2 * n_extra, :]
            return total[..., :width, :], m.reshape(*m.shape[:-2], width)

        got = lax.all_to_all(with_moments(w_b, part_b), "x", 0, 0, tiled=True)
        w, m = parted(jnp.sum(got.astype(f32), 0))
        got = lax.all_to_all(with_moments(w.astype(bf16), m), "zl", 0, 0, tiled=True)
        w_b, second_b = parted(jnp.sum(got.astype(f32), 0))

    with jax.named_scope("weight_a"):
        w_a = dot(p_ab_all, grads, ((0, 1, 3), (0, 1, 2)))

    with jax.named_scope("finish"):
        inv_a, inv_b = stats_a[8], inverse_b[0]
        result = inv_a * (w_a - pairs * p_aa * second_a)
        result = result + inv_b * (w_b.T - pairs * p_bb * second_b)
        result = result.reshape(n_x, n_zl, sub, width).transpose(1, 0, 2, 3)
        return result.reshape(n_feat, 1, sub, width)


def solution(mesh):
    names = tuple(n for n, _ in SIZES)
    fine = Mesh(mesh.devices.reshape(tuple(s for _, s in SIZES)), names)
    spec = P(DP, FEAT)
    return jax.shard_map(
        body,
        mesh=fine,
        in_specs=(spec, spec, spec, spec),
        out_specs=P(None, DP, None, FEAT),
        check_vma=False,
    )
```

time: 315 us -> 230 us (0.73)
  waiting for transfers between devices: 102 us -> 38 us
  local copies, waits for them, and re-layouts: 36.8 us -> 13.7 us
  blocking collectives: 101 us -> 115 us
  between operations: 0.39 us -> 13.4 us
  other arithmetic: 18.9 us -> 7.13 us
  starting transfers between devices: 43.2 us -> 34.8 us
  matrix products: 8.72 us -> 2.38 us
  Pallas kernels: 0 us -> 4.66 us
    all_to_all x9 -> x1, waiting for transfers between devices: 88 us -> 0.01 us  [gather(): return lax.all_to_all(copies, axis, 0, 0, tiled=True)]
    all_gather x0 -> x3, blocking collectives: none -> 64.3 us  [collect(): return lax.all_gather(block, axis, axis=0, tiled=False)]
    all_to_all x2 -> x0, blocking collectives: 49.1 us -> none  [the longest x1 38.8 us: body(): cut = lax.all_to_all(cut, DP, 0, 0, tiled=True)]
    all_to_all x9 -> x1, starting transfers between devices: 39.6 us -> 4.25 us  [gather(): return lax.all_to_all(copies, axis, 0, 0, tiled=True)]
    all_to_all x0 -> x2, starting transfers between devices: none -> 23.6 us  [the longest x1 19.4 us: body(): cut = lax.all_to_all(cut, DP, 0, 0, tiled=True)]
    all_gather x0 -> x3, waiting for transfers between devices: none -> 12.2 us  [collect(): return lax.all_gather(block, axis, axis=0, tiled=False)]
    broadcast_in_dim x12 -> x5, local copies, waits for them, and re-layouts: 13.2 us -> 2.74 us  [gather(): copies = jnp.broadcast_to(block[None], (count, *block.shape))]
    all_to_all x3 -> x0, local copies, waits for them, and re-layouts: 10.2 us -> none  [gather(): return lax.all_to_all(copies, axis, 0, 0, tiled=True)]
  transfers between devices with their start and end apart: 10 -> 8, of which waited for: 10 -> 6; matrix products, arithmetic and copies ran while one was open for 13% -> 2% of each run, Pallas kernels for 0% -> 2%
where the time goes in v2:
time: 230 us; the launch traced here: 229 us
  blocking collectives  115 us (50%)
  waiting for transfers between devices  38 us (17%)
  starting transfers between devices  34.8 us (15%)
  local copies, waits for them, and re-layouts  13.7 us (6%)
  between operations  13.4 us (6%)
  other arithmetic  7.13 us (3%)
  Pallas kernels  4.66 us (2%)
  matrix products  2.38 us (1%)
    all_gather x3, blocking collectives, collect(): return lax.all_gather(block, axis, axis=0, tiled=False)  64.3 us
    all_to_all x3, blocking collectives, gather(): return lax.all_to_all(copies, axis, 0, 0, tiled=True)  50.7 us
    all_to_all x1, starting transfers between devices, body(): cut = lax.all_to_all(cut, DP, 0, 0, tiled=True)  19.4 us
    all_to_all x1, waiting for transfers between devices, body(): got = lax.all_to_all(with_moments(w_b, part_b), 'x', 0, 0, tiled=True)  14.8 us
    all_gather x3, waiting for transfers between devices, collect(): return lax.all_gather(block, axis, axis=0, tiled=False)  12.2 us
    unnamed x14, local copies, waits for them, and re-layouts  7.73 us
    all_to_all x1, waiting for transfers between devices, body(): lax.all_to_all(with_moments(w.astype(bf16), m), 'zl', 0, 0, tiled=True)  6.36 us
    pallas_call x2, Pallas kernels, call(): pl.pallas_call(kernel, out_shape=shapes, in_specs=[pl.BlockSpec(memory_sp...  4.66 us
  transfers between devices with their start and end apart: 8, of which 6 were waited for; matrix products, arithmetic and copies ran while one was open for 2% of the time, Pallas kernels for 2%

profile of v2, /device:TPU:1, one launch (start us, length us, event | category | flops | bytes accessed | tf_op | source)
XLA Modules:
  0.0 229.1 jit_solution(6810821887683993315)
XLA Ops:
  6.5 0.9 copy.42
  7.5 1.0 copy.43
  8.4 1.0 copy.44
  9.4 0.7 copy.45
  10.2 19.4 %all-to-all-start = ((bf16[32,3,8,128]{3,2,1,0:T(8,128)(2,1)}), bf16[32,3,8,128]{3,2,1,0:T(8,128)(2,1)S(1)}, u32[]{:S(2)}, u32[]{:S(2)}) async-start(bf16[32,3,8,128]{3,2,1,0:T(8,128)(2,1)} %copy.45), calls=%async_computation | async-start | bytes 393216 | tf_op jit(solution)/shard_map/columns/all_to_all | solution.py:167
  29.5 0.0 all-gather.8.cloned.1.call-start
  29.6 0.9 pad_maximum_fusion.1
  30.5 34.6 %all-gather = bf16[8,128,256]{2,1,0:T(8,128)(2,1)} all-gather(bf16[2,128,256]{2,1,0:T(8,128)(2,1)S(1)} %pad_maximum_fusion.1), channel_id=2, replica_groups=mesh['y'=4,'zh'=4,'c'=2,'zl'=4,'x'=4] {'zh'}, dimensions={0}, use_global_device_ids=true | all-gather | bytes 655360 | tf_op jit(solution)/shard_map/rows/all_gather | solution.py:35
  65.0 0.0 all-gather.8.cloned.1.call-update
  65.1 0.0 all-gather.10.cloned.1.call-start
  65.2 15.5 %all_gather.34 = bf16[4,3,8,4096]{3,2,1,0:T(8,128)(2,1)S(1)} all-gather(bf16[1,3,8,4096]{3,2,1,0:T(8,128)(2,1)S(1)} %bitcast.83), channel_id=1, replica_groups=mesh['y'=4,'zh'=4,'c'=2,'zl'=4,'x'=4] {'zl'}, dimensions={0}, use_global_device_ids=true | all-gather | bytes 983040 | tf_op jit(solution)/shard_map/columns/all_gather | solution.py:35
  80.7 0.1 broadcast_in_dim.17
  80.8 14.6 %all_to_all.35 = bf16[4,4,8,4096]{3,2,1,0:T(8,128)(2,1)S(1)} all-to-all(bf16[4,4,8,4096]{3,2,1,0:T(8,128)(2,1)S(1)} %broadcast_in_dim.17), channel_id=1, replica_groups=mesh['y'=4,'zh'=4,'c'=2,'zl'=4,'x'=4] {'x'}, dimensions={0} | all-to-all | bytes 2097152 | tf_op jit(solution)/shard_map/columns/all_to_all | solution.py:21
  95.4 5.1 %all-gather.8.cloned.1.call-done = bf16[16,2,128,256]{3,2,1,0:T(8,128)(2,1)} async-done(((bf16[4,2,128,256]{3,2,1,0:T(8,128)(2,1)}), bf16[16,2,128,256]{3,2,1,0:T(8,128)(2,1)}) %all-gather.8.cloned.1.call-update) | async-done | bytes 2097168 | tf_op jit(solution)/shard_map/rows/all_gather | solution.py:35
  100.5 0.8 slice.45
  101.4 2.6 %collective-permute-start = (bf16[16,2,128,256]{3,2,1,0:T(8,128)(2,1)}, bf16[16,2,128,256]{3,2,1,0:T(8,128)(2,1)S(1)}, u32[]{:S(2)}, u32[]{:S(2)}) collective-permute-start(bf16[16,2,128,256]{3,2,1,0:T(8,128)(2,1)} %all-gather.8.cloned.1.call-done), channel_id=1, source_target_pairs={{0,16},{16,0},{1,17},{17,1},{2,18},{18,2},{3,19},{19,3},{4,20},{20... | collective-permute-start | bytes 6291464 | tf_op jit(solution)/shard_map/rows/ppermute | solution.py:163
  104.0 3.9 %collective-permute-done.other_ref = bf16[16,2,128,256]{3,2,1,0:T(8,128)(2,1)S(1)} collective-permute-done((bf16[16,2,128,256]{3,2,1,0:T(8,128)(2,1)}, bf16[16,2,128,256]{3,2,1,0:T(8,128)(2,1)S(1)}, u32[]{:S(2)}, u32[]{:S(2)}) %collective-permute-start) | collective-permute-done | bytes 2097184 | tf_op jit(solution)/shard_map/rows/ppermute | solution.py:163
  107.9 1.6 copy-done
  109.5 2.0 grad_block.1
  111.6 27.9 %all_to_all.36 = bf16[4,128,256]{2,1,0:T(8,128)(2,1)S(1)} all-to-all(bf16[4,128,256]{2,1,0:T(8,128)(2,1)S(1)} %broadcast_in_dim.18), channel_id=1, replica_groups=mesh['y'=4,'zh'=4,'c'=2,'zl'=4,'x'=4] {'zh'}, dimensions={0} | all-to-all | bytes 524288 | tf_op jit(solution)/shard_map/grad_rows/all_to_all | solution.py:21
  139.5 1.7 all-gather.10.cloned.1.call-done
  141.2 1.1 broadcast_in_dim.19
  142.3 4.2 %all-to-all-start.3 = ((bf16[4,4,128,256]{3,2,1,0:T(8,128)(2,1)}), bf16[4,4,128,256]{3,2,1,0:T(8,128)(2,1)}, u32[]{:S(2)}, u32[]{:S(2)}) async-start(bf16[4,4,128,256]{3,2,1,0:T(8,128)(2,1)} %broadcast_in_dim.19), calls=%async_computation.3 | async-start | bytes 2097152 | tf_op jit(solution)/shard_map/grad_rows/all_to_all | solution.py:21
  146.6 0.1 pad.7.clone
  146.7 1.6 copy-done.3
  148.3 1.6 copy-done.4
  149.9 2.7 %products.1 = (f32[256,512]{1,0:T(8,128)S(1)}, bf16[256,512]{1,0:T(8,128)(2,1)S(1)}, f32[8,256]{1,0:T(8,128)S(1)}) custom-call(bf16[256,4096]{1,0:T(8,128)(2,1)S(1)} %bitcast.72, bf16[16,2,128,256]{3,2,1,0:T(8,128)(2,1)S(1)} %copy-done.1, bf16[16,2,128,256]{3,2,1,0:T(8,128)(2,1)S(1)} %copy-done.3, f32[16,256]{1,0:T(8,128)S(1)} %get-tuple-element.24.stats_ref), custom_call_target="tpu_custom_call" | custom-call | flops 1073741824 | bytes 7102464 | tf_op jit(solution)/shard_map/products/products/pallas_call | solution.py:137
  152.6 14.3 %all_gather.37 = bf16[4,128,256]{2,1,0:T(8,128)(2,1)} all-gather(bf16[1,128,256]{2,1,0:T(8,128)(2,1)S(1)} %get-tuple-element.42), channel_id=1, replica_groups=mesh['y'=4,'zh'=4,'c'=2,'zl'=4,'x'=4] {'zl'}, dimensions={0}, use_global_device_ids=true | all-gather | bytes 327680 | tf_op jit(solution)/shard_map/products/all_gather | solution.py:35
  166.9 1.5 broadcast_in_dim.38
  168.4 8.1 %all_to_all.37 = bf16[2,4,4,128,256]{4,3,2,1,0:T(8,128)(2,1)S(1)} all-to-all(bf16[2,4,4,128,256]{4,3,2,1,0:T(8,128)(2,1)S(1)} %broadcast_in_dim.38), channel_id=1, replica_groups=mesh['y'=4,'zh'=4,'c'=2,'zl'=4,'x'=4] {'c'}, dimensions={0} | all-to-all | bytes 4194304 | tf_op jit(solution)/shard_map/grad_rows/all_to_all | solution.py:21
  176.5 0.3 copy.47
  176.8 2.5 %fusion.5 = (f32[256]{0:T(256)S(1)}, f32[4,4,4,4,2,8]{5,1,0,3,2,4:T(4,128)S(1)}) fusion(bf16[4,4,4,4,2,8,256]{6,5,1,0,3,2,4:T(8,128)(2,1)S(1)} %bitcast.78, s32[4,4,2,8]{3,1,0,2:T(4,128)S(1)} %multiply_add_fusion, s32[]{:T(128)S(6)} %add.108, s32[4]{0:T(128)S(1)} %iota_multiply_fusion), kind=kLoop, calls=%fused_computation.11 | loop fusion | flops 13627136 | bytes 2115604 | tf_op jit(solution)/shard_map/moments/reduce_sum | solution.py:233
  179.2 0.2 copy.49
  179.4 0.4 reduce_sum.40
  179.8 0.7 convolution_convert_fusion
  180.6 1.3 maximum_maximum_fusion
  181.9 4.3 %all-to-all-start.5 = ((bf16[4,4,272,128]{3,2,1,0:T(8,128)(2,1)}), bf16[4,4,272,128]{3,2,1,0:T(8,128)(2,1)}, u32[]{:S(2)}, u32[]{:S(2)}) async-start(bf16[4,4,272,128]{3,2,1,0:T(8,128)(2,1)} %maximum_maximum_fusion), calls=%async_computation.5 | async-start | bytes 2228224 | tf_op jit(solution)/shard_map/weight_b/all_to_all | solution.py:255
  186.1 0.0 all-gather.12.cloned.1.call-start
  186.2 0.7 all-gather.12.cloned.1.call-update
  186.9 14.8 %all-to-all-done.5 = bf16[4,4,272,128]{3,2,1,0:T(8,128)(2,1)} async-done(((bf16[4,4,272,128]{3,2,1,0:T(8,128)(2,1)}), bf16[4,4,272,128]{3,2,1,0:T(8,128)(2,1)}, u32[]{:S(2)}, u32[]{:S(2)}) %all-to-all-start.5) | async-done | bytes 1114144 | tf_op jit(solution)/shard_map/weight_b/all_to_all | solution.py:255
  201.7 1.5 convert_reduce_fusion
  203.2 0.8 maximum_maximum_fusion.1
  204.0 4.2 %all-to-all-start.6 = ((bf16[4,272,128]{2,1,0:T(8,128)(2,1)}), bf16[4,272,128]{2,1,0:T(8,128)(2,1)S(1)}, u32[]{:S(2)}, u32[]{:S(2)}) async-start(bf16[4,272,128]{2,1,0:T(8,128)(2,1)} %maximum_maximum_fusion.1), calls=%async_computation.6 | async-start | bytes 557056 | tf_op jit(solution)/shard_map/weight_b/all_to_all | solution.py:257
  208.3 6.4 %all-to-all-done.6 = bf16[4,272,128]{2,1,0:T(8,128)(2,1)S(1)} async-done(((bf16[4,272,128]{2,1,0:T(8,128)(2,1)}), bf16[4,272,128]{2,1,0:T(8,128)(2,1)S(1)}, u32[]{:S(2)}, u32[]{:S(2)}) %all-to-all-start.6) | async-done | bytes 278560 | tf_op jit(solution)/shard_map/weight_b/all_to_all | solution.py:257
  214.7 0.1 copy.53
  214.8 5.4 %all-gather.12.cloned.1.call-done = bf16[16,128,256]{2,1,0:T(8,128)(2,1)} async-done(((bf16[4,128,256]{2,1,0:T(8,128)(2,1)}), bf16[16,128,256]{2,1,0:T(8,128)(2,1)}) %all-gather.12.cloned.1.call-update) | async-done | bytes 1048592 | tf_op jit(solution)/shard_map/products/all_gather | solution.py:35
  220.2 1.7 fusion.15
  221.9 0.7 copy.51
  (29 shorter events, 0.3 us)
Async XLA Ops:
  10.2 54.9 %all-to-all-start = ((bf16[32,3,8,128]{3,2,1,0:T(8,128)(2,1)}), bf16[32,3,8,128]{3,2,1,0:T(8,128)(2,1)S(1)}, u32[]{:S(2)}, u32[]{:S(2)}) async-start(bf16[32,3,8,128]{3,2,1,0:T(8,128)(2,1)} %copy.45), calls=%async_computation | async-start | bytes 393216 | tf_op jit(solution)/shard_map/columns/all_to_all | solution.py:167
  29.5 71.0 %all-gather.8.cloned.1.call-start = ((), (), s32[]{:S(2)}) async-start(), calls=%async_computation.7 | async-start | bytes 2621440 | tf_op jit(solution)/shard_map/rows/all_gather | solution.py:35
  65.1 76.1 %all-gather.10.cloned.1.call-start = ((), (), s32[]{:S(2)}) async-start(), calls=%async_computation.8 | async-start | bytes 2621440 | tf_op jit(solution)/shard_map/columns/all_gather | solution.py:35
  101.4 6.6 %collective-permute-start = (bf16[16,2,128,256]{3,2,1,0:T(8,128)(2,1)}, bf16[16,2,128,256]{3,2,1,0:T(8,128)(2,1)S(1)}, u32[]{:S(2)}, u32[]{:S(2)}) collective-permute-start(bf16[16,2,128,256]{3,2,1,0:T(8,128)(2,1)} %all-gather.8.cloned.1.call-done), channel_id=1, source_target_pairs={{0,16},{16,0},{1,17},{17,1},{2,18},{18,2},{3,19},{19,3},{4,20},{20... | collective-permute-start | bytes 6291464 | tf_op jit(solution)/shard_map/rows/ppermute | solution.py:163
  107.9 1.6 copy-start
  109.5 2.0 copy-start.2
  111.5 35.2 %copy-start.1 = (bf16[16,2,128,256]{3,2,1,0:T(8,128)(2,1)S(1)}, bf16[16,2,128,256]{3,2,1,0:T(8,128)(2,1)}, u32[]{:S(2)}) copy-start(bf16[16,2,128,256]{3,2,1,0:T(8,128)(2,1)} %all-gather.8.cloned.1.call-done) | copy-start | bytes 6291460
  142.3 24.6 %all-to-all-start.3 = ((bf16[4,4,128,256]{3,2,1,0:T(8,128)(2,1)}), bf16[4,4,128,256]{3,2,1,0:T(8,128)(2,1)}, u32[]{:S(2)}, u32[]{:S(2)}) async-start(bf16[4,4,128,256]{3,2,1,0:T(8,128)(2,1)} %broadcast_in_dim.19), calls=%async_computation.3 | async-start | bytes 2097152 | tf_op jit(solution)/shard_map/grad_rows/all_to_all | solution.py:21
  146.7 1.6 copy-start.3
  148.3 1.6 copy-start.4
  181.9 19.8 %all-to-all-start.5 = ((bf16[4,4,272,128]{3,2,1,0:T(8,128)(2,1)}), bf16[4,4,272,128]{3,2,1,0:T(8,128)(2,1)}, u32[]{:S(2)}, u32[]{:S(2)}) async-start(bf16[4,4,272,128]{3,2,1,0:T(8,128)(2,1)} %maximum_maximum_fusion), calls=%async_computation.5 | async-start | bytes 2228224 | tf_op jit(solution)/shard_map/weight_b/all_to_all | solution.py:255
  186.1 34.1 %all-gather.12.cloned.1.call-start = ((), (), s32[]{:S(2)}) async-start(), calls=%async_computation.9 | async-start | bytes 1310720 | tf_op jit(solution)/shard_map/products/all_gather | solution.py:35
  204.0 10.6 %all-to-all-start.6 = ((bf16[4,272,128]{2,1,0:T(8,128)(2,1)}), bf16[4,272,128]{2,1,0:T(8,128)(2,1)S(1)}, u32[]{:S(2)}, u32[]{:S(2)}) async-start(bf16[4,272,128]{2,1,0:T(8,128)(2,1)} %maximum_maximum_fusion.1), calls=%async_computation.6 | async-start | bytes 557056 | tf_op jit(solution)/shard_map/weight_b/all_to_all | solution.py:257
Sparse Core Ops, SparseCore 0:
  65.2 35.2 all-gather.7
  102.6 38.5 all-gather.9
  189.1 31.1 all-gather.11

commit v3 on v2

--- a/solution.py
+++ b/solution.py
@@ -36,10 +36,6 @@
 
 
 STEP = 256
-
-
-def at(i):
-    return pl.ds(pl.multiple_of(i * STEP, STEP), STEP)
 
 
 def fold(v):
@@ -59,6 +55,11 @@
     return jnp.concatenate([ref[first + j, side] for j in range(each)], axis=0)
 
 
+def columns(cols_ref, views, i):
+    at = pl.ds(i * STEP, STEP)
+    return jnp.concatenate([cols_ref[x, v, :, at] for x in range(cols_ref.shape[0]) for v in views], axis=0)
+
+
 def column_stats(halves, side, pairs):
     width = halves[0].shape[3]
     total = squares = jnp.zeros((8, width), f32)
@@ -68,15 +69,11 @@
     return stats(jnp.sum(total, 0, keepdims=True), jnp.sum(squares, 0, keepdims=True), pairs)
 
 
-def row_stats(cols_ref):
-    owned, pairs = cols_ref.shape
-
-    def add(i, carry):
-        v = cols_ref[:, at(i)].astype(f32)
-        return carry[0] + lanes(v), carry[1] + lanes(v * v)
-
-    empty = jnp.zeros((owned, 128), f32)
-    total, squares = lax.fori_loop(0, pairs // STEP, add, (empty, empty))
+def row_stats(cols_ref, view, pairs):
+    total = squares = 0.0
+    for i in range(pairs // STEP):
+        v = columns(cols_ref, (view,), i).astype(f32)
+        total, squares = total + lanes(v), squares + lanes(v * v)
     return stats(jnp.sum(total, 1, keepdims=True), jnp.sum(squares, 1, keepdims=True), pairs)
 
 
@@ -89,17 +86,17 @@
 
 
 def grad_kernel(own_ref, other_ref, cols_ref, target_ref, grad_ref, stats_ref):
-    owned, pairs = cols_ref.shape
+    pairs = cols_ref.shape[3]
     halves = (own_ref, other_ref)
-    width = grad_ref.shape[1]
+    owned, width = grad_ref.shape
     mean, inverse = column_stats(halves, 0, pairs)
-    mean_b, inverse_b = row_stats(cols_ref)
+    mean_b, inverse_b = row_stats(cols_ref, 0, pairs)
     stats_ref[0:8, :] = jnp.broadcast_to(mean, (8, width))
     stats_ref[8:16, :] = jnp.broadcast_to(inverse, (8, width))
     corr = jnp.zeros((owned, width), f32)
     for i in range(pairs // STEP):
         v = normalize(chunk(halves, 0, i), mean, inverse)
-        b = normalize(cols_ref[:, pl.ds(i * STEP, STEP)], mean_b, inverse_b)
+        b = normalize(columns(cols_ref, (0,), i), mean_b, inverse_b)
         corr = corr + matmul(b, v)
     corr = corr / pairs
     diagonal = lax.broadcasted_iota(jnp.int32, (owned, width), 1) == target_ref[...]
@@ -107,9 +104,9 @@
 
 
 def product_kernel(cols_ref, own_ref, other_ref, stats_ref, prod_ref, centered_ref, inverse_ref):
-    owned, pairs = cols_ref.shape
+    pairs = cols_ref.shape[3]
     halves = (own_ref, other_ref)
-    width = own_ref.shape[3]
+    owned, width = prod_ref.shape[0], prod_ref.shape[1] // 2
     mean_a, inverse_a = stats_ref[0:1, :], stats_ref[8:9, :]
     mean_b, inverse_b = column_stats(halves, 1, pairs)
     inverse_ref[...] = jnp.broadcast_to(inverse_b, (8, width))
@@ -117,7 +114,7 @@
     sum_a = sum_b = jnp.zeros((8, width), f32)
     sum_h = jnp.zeros((owned, 128), f32)
     for i in range(pairs // STEP):
-        h = cols_ref[:, pl.ds(i * STEP, STEP)]
+        h = columns(cols_ref, (0, 1), i)
         a = normalize(chunk(halves, 0, i), mean_a, inverse_a)
         b = normalize(chunk(halves, 1, i), mean_b, inverse_b)
         prod_a, prod_b = prod_a + matmul(h, a), prod_b + matmul(h, b)
@@ -125,21 +122,74 @@
         sum_h = sum_h + lanes(h.astype(f32))
     sum_h = jnp.sum(sum_h, 1, keepdims=True)
     for side, prod, sums in ((0, prod_a, sum_a), (1, prod_b, sum_b)):
-        part = pl.ds(side * width, width)
+        cols = pl.ds(side * width, width)
         sums = jnp.sum(sums, 0, keepdims=True) / pairs
-        prod_ref[:, part] = prod
-        centered_ref[:, part] = (prod - sum_h * sums).astype(bf16)
+        prod_ref[:, cols] = prod
+        centered_ref[:, cols] = (prod - sum_h * sums).astype(bf16)
+
+
+def weight_a_kernel(pairs, blocks_ref, grads_ref, aa_ref, bb_ref, stats_ref, inverse_ref, second_ref, out_ref):
+    owned, width = aa_ref.shape
+    total = jnp.zeros((owned, width), f32)
+    for x in range(blocks_ref.shape[0]):
+        for zl in range(blocks_ref.shape[1]):
+            total = total + matmul(blocks_ref[x, zl], grads_ref[x, zl])
+    inv_b = inverse_ref[0:1, :]
+    out_ref[0:owned, :] = stats_ref[8:9, :] * (total - pairs * aa_ref[...] * second_ref[...])
+    out_ref[owned : 2 * owned, :] = inv_b * pairs * bb_ref[...]
+    out_ref[2 * owned :, :] = jnp.broadcast_to(inv_b, (8, width))
+
+
+def split(m, rows):
+    high = m.astype(bf16)
+    low = (m - high.astype(f32)).astype(bf16)
+    pad = jnp.zeros((rows - 2 * m.shape[0], m.shape[1]), bf16)
+    return jnp.concatenate([high, low, pad], axis=0)
+
+
+def fold_kernel(width, got_ref, out_ref):
+    count, blocks, _, owned = got_ref.shape
+    rows = out_ref.shape[1]
+    extra = width // owned
+    for z in range(blocks):
+        total = got_ref[0, z, 0:rows].astype(f32)
+        for x in range(1, count):
+            total = total + got_ref[x, z, 0:rows].astype(f32)
+        out_ref[z, 0:width, :] = total[:width].astype(bf16)
+        m = total[width : width + extra] + total[width + extra : width + 2 * extra]
+        out_ref[z, width:rows, :] = split(m, rows - width)
+
+
+def finish_kernel(got_ref, side_ref, out_ref):
+    count, rows, owned = got_ref.shape
+    width = side_ref.shape[1]
+    extra = width // owned
+    total = got_ref[0].astype(f32)
+    for z in range(1, count):
+        total = total + got_ref[z].astype(f32)
+    m = total[width : width + extra] + total[width + extra : width + 2 * extra]
+    second_b = jnp.concatenate([m[i : i + 1] for i in range(extra)], axis=1)
+    w_b = total[:width].T
+    inv_b = side_ref[2 * owned : 2 * owned + 1, :]
+    result = side_ref[0:owned, :] + inv_b * w_b - side_ref[owned : 2 * owned, :] * second_b
+    n_feat, sub, _ = out_ref.shape
+    n_x = n_feat // count
+    for x in range(n_x):
+        for z in range(count):
+            first = (x * count + z) * sub
+            out_ref[z * n_x + x] = result[first : first + sub]
 
 
 def call(kernel, name, flops, shapes, *operands):
     size = lambda v: v.size * v.dtype.itemsize
-    moved = sum(size(v) for v in operands) + sum(size(v) for v in shapes)
+    outs = jax.tree.leaves(shapes)
+    moved = sum(size(v) for v in operands) + sum(size(v) for v in outs)
     return pl.pallas_call(
         kernel,
         out_shape=shapes,
         in_specs=[pl.BlockSpec(memory_space=pltpu.VMEM)] * len(operands),
-        out_specs=[pl.BlockSpec(memory_space=pltpu.VMEM)] * len(shapes),
-        compiler_params=pltpu.CompilerParams(vmem_limit_bytes=32 * 2**20),
+        out_specs=jax.tree.map(lambda _: pl.BlockSpec(memory_space=pltpu.VMEM), shapes),
+        compiler_params=pltpu.CompilerParams(vmem_limit_bytes=16 * 2**20),
         cost_estimate=pl.CostEstimate(flops=flops, bytes_accessed=moved, transcendentals=0),
         name=name,
     )(*operands)
@@ -162,25 +212,23 @@
     def swap(v):
         return lax.ppermute(v, "c", [(0, 1), (1, 0)])
 
+    with jax.named_scope("rows"):
+        rows = collect(jnp.stack([z_a, z_b]), "zh")
+
     with jax.named_scope("columns"):
         cut = jnp.stack([v.T.reshape(n_dp, sub, local_rows) for v in (z_b, h_a, h_b)], axis=1)
         cut = lax.all_to_all(cut, DP, 0, 0, tiled=True)
-    with jax.named_scope("rows"):
-        rows = collect(jnp.stack([z_a, z_b]), "zh")
-    cut, rows = together((cut, rows))
-    with jax.named_scope("columns"):
+        cut, rows = together((cut, rows))
         cut = cut.reshape(n_y, n_zh, n_c, 3, sub, local_rows)
         cut = jnp.where(core == 0, cut, jnp.flip(cut, 2))
         cut = cut.transpose(3, 4, 2, 0, 1, 5).reshape(3, sub, pairs)
-
+        cut = collect(cut, "zl").transpose(1, 0, 2, 3).reshape(3, n_zl * sub, pairs)
+        cols_b = gather(cut[:1], "x")
     with jax.named_scope("rows"):
         rows = collect(rows, "y")
+    rows, cut, cols_b = together((rows, cut, cols_b))
     with jax.named_scope("columns"):
-        cut = collect(cut, "zl")
-        cols_b = gather(cut[:, 0], "x").reshape(owned, pairs)
-    rows, cols_b, cut = together((rows, cols_b, cut))
-    with jax.named_scope("columns"):
-        cols_h = collect(cut[:, 1:], "x").reshape(2 * owned, pairs)
+        cols_h = collect(cut[1:], "x")
     with jax.named_scope("rows"):
         own = rows.reshape(n_y * n_zh, 2, local_rows, width)
         other = swap(own)
@@ -198,8 +246,8 @@
         )
 
     with jax.named_scope("grad_rows"):
-        grads = gather(grad, "zh")
-    grads, cols_h = together((grads, cols_h))
+        grads = collect(grad, "zh")
+    own, _ = together((own, grads))
 
     with jax.named_scope("grad_rows"):
         grads = gather(grads, "y")
@@ -209,22 +257,21 @@
             (shape((2 * owned, 2 * width), f32), shape((2 * owned, 2 * width), bf16), shape((8, width), f32)),
             cols_h, own, other, stats_a,
         )
-        halves = lambda v: v.reshape(n_x * n_zl, 2, sub, 2 * width)
+        halves = lambda v: v.reshape(n_x, 2, n_zl * sub, 2 * width)
         prod, centered = halves(prod), halves(centered)
         p_aa = prod[:, 0, :, :width].reshape(owned, width)
         p_bb = prod[:, 1, :, width:].reshape(owned, width)
         p_ab = centered[:, 0, :, width:].reshape(owned, width)
         p_ba = centered[:, 1, :, :width].reshape(owned, width)
-        p_ab_all = collect(p_ab, "zl")
-    grads, p_ab_all, p_ba = together((grads, p_ab_all, p_ba))
+        p_ab = collect(p_ab, "zl")
+    grads, p_ab, p_ba = together((grads, p_ab, p_ba))
+    with jax.named_scope("products"):
+        p_ab = collect(p_ab, "x")
 
     with jax.named_scope("grad_rows"):
         grads = gather(grads, "c")
         grads = grads.reshape(n_c, n_y, n_zh, n_x, n_zl, sub, width)
         grads = grads.transpose(3, 4, 1, 2, 0, 5, 6).reshape(n_x, n_zl, width, width)
-    with jax.named_scope("products"):
-        p_ab_all = collect(p_ab_all, "x")
-
     with jax.named_scope("moments"):
         g = grads.astype(f32)
         four = lambda d: lax.broadcasted_iota(jnp.int32, g.shape, d)
@@ -247,25 +294,24 @@
             pad = jnp.zeros((*lead, 16 - extra.shape[-2], owned), bf16)
             return jnp.concatenate([w, extra, pad], axis=-2)
 
-        def parted(total):
-            n_extra = width // owned
-            m = total[..., width : width + n_extra, :] + total[..., width + n_extra : width + 2 * n_extra, :]
-            return total[..., :width, :], m.reshape(*m.shape[:-2], width)
-
         got = lax.all_to_all(with_moments(w_b, part_b), "x", 0, 0, tiled=True)
-        w, m = parted(jnp.sum(got.astype(f32), 0))
-        got = lax.all_to_all(with_moments(w.astype(bf16), m), "zl", 0, 0, tiled=True)
-        w_b, second_b = parted(jnp.sum(got.astype(f32), 0))
+        rows_out = got.shape[2]
+        got = call(
+            lambda *refs: fold_kernel(width, *refs), "fold", 0,
+            shape((n_zl, rows_out, owned), bf16), got,
+        )
+        got = lax.all_to_all(got, "zl", 0, 0, tiled=True)
 
     with jax.named_scope("weight_a"):
-        w_a = dot(p_ab_all, grads, ((0, 1, 3), (0, 1, 2)))
+        side = call(
+            lambda *refs: weight_a_kernel(pairs, *refs), "weight_a", 2 * owned * n_feat * width * width,
+            shape((2 * owned + 8, width), f32),
+            p_ab, grads, p_aa, p_bb, stats_a, inverse_b, second_a[None],
+        )
 
     with jax.named_scope("finish"):
-        inv_a, inv_b = stats_a[8], inverse_b[0]
-        result = inv_a * (w_a - pairs * p_aa * second_a)
-        result = result + inv_b * (w_b.T - pairs * p_bb * second_b)
-        result = result.reshape(n_x, n_zl, sub, width).transpose(1, 0, 2, 3)
-        return result.reshape(n_feat, 1, sub, width)
+        result = call(finish_kernel, "finish", 0, shape((n_feat, sub, width), f32), got, side)
+        return result[:, None]
 
 
 def solution(mesh):

time: 230 us -> 223 us (0.970)
  blocking collectives: 115 us -> 109 us
  other arithmetic: 7.13 us -> 4.8 us
  local copies, waits for them, and re-layouts: 13.7 us -> 16 us
    all_to_all x3 -> x2, blocking collectives: 50.7 us -> 23.2 us  [gather(): return lax.all_to_all(copies, axis, 0, 0, tiled=True)]
    all_gather x3 -> x4, blocking collectives: 64.3 us -> 85.8 us  [collect(): return lax.all_gather(block, axis, axis=0, tiled=False)]
    all_gather x3, waiting for transfers between devices: 12.2 us -> 19.3 us  [collect(): return lax.all_gather(block, axis, axis=0, tiled=False)]
    all_to_all x1, waiting for transfers between devices: 6.36 us -> 0.01 us  [body(): got = lax.all_to_all(got, 'zl', 0, 0, tiled=True)]
    unnamed x14 -> x17, local copies, waits for them, and re-layouts: 7.73 us -> 11 us
    pallas_call x2 -> x5, Pallas kernels: 4.66 us -> 6.67 us  [call(): pl.pallas_call(kernel, out_shape=shapes, in_specs=[pl.BlockSpec(memory_sp...]
  transfers between devices with their start and end apart: 8 -> 8, of which waited for: 6 -> 5; matrix products, arithmetic and copies ran while one was open for 2% -> 2% of each run, Pallas kernels for 2% -> 3%
where the time goes in v3:
time: 223 us; the launch traced here: 222 us
  blocking collectives  109 us (49%)
  waiting for transfers between devices  38.4 us (17%)
  starting transfers between devices  33.2 us (15%)
  local copies, waits for them, and re-layouts  16 us (7%)
  between operations  13.3 us (6%)
  Pallas kernels  6.67 us (3%)
  other arithmetic  4.8 us (2%)
    all_gather x4, blocking collectives, collect(): return lax.all_gather(block, axis, axis=0, tiled=False)  85.8 us
    all_to_all x2, blocking collectives, gather(): return lax.all_to_all(copies, axis, 0, 0, tiled=True)  23.2 us
    all_to_all x1, starting transfers between devices, body(): cut = lax.all_to_all(cut, DP, 0, 0, tiled=True)  19.4 us
    all_gather x3, waiting for transfers between devices, collect(): return lax.all_gather(block, axis, axis=0, tiled=False)  19.3 us
    all_to_all x1, waiting for transfers between devices, body(): got = lax.all_to_all(with_moments(w_b, part_b), 'x', 0, 0, tiled=True)  14.5 us
    unnamed x17, local copies, waits for them, and re-layouts  11 us
    pallas_call x5, Pallas kernels, call(): pl.pallas_call(kernel, out_shape=shapes, in_specs=[pl.BlockSpec(memory_sp...  6.67 us
  transfers between devices with their start and end apart: 8, of which 5 were waited for; matrix products, arithmetic and copies ran while one was open for 2% of the time, Pallas kernels for 3%

profile of v3, /device:TPU:1, one launch (start us, length us, event | category | flops | bytes accessed | tf_op | source)
XLA Modules:
  0.0 222.2 jit_solution(2784536653258483435)
XLA Ops:
  6.5 0.9 copy.48
  7.5 1.0 copy.49
  8.4 1.0 copy.50
  9.4 0.7 copy.51
  10.2 19.4 %all-to-all-start = ((bf16[32,3,8,128]{3,2,1,0:T(8,128)(2,1)}), bf16[32,3,8,128]{3,2,1,0:T(8,128)(2,1)S(1)}, u32[]{:S(2)}, u32[]{:S(2)}) async-start(bf16[32,3,8,128]{3,2,1,0:T(8,128)(2,1)} %copy.51), calls=%async_computation | async-start | bytes 393216 | tf_op jit(solution)/shard_map/columns/all_to_all | solution.py:220
  29.5 0.0 all-gather.9.cloned.1.call-start
  29.6 0.9 pad_maximum_fusion.1
  30.5 34.6 %all-gather = bf16[8,128,256]{2,1,0:T(8,128)(2,1)} all-gather(bf16[2,128,256]{2,1,0:T(8,128)(2,1)S(1)} %pad_maximum_fusion.1), channel_id=2, replica_groups=mesh['y'=4,'zh'=4,'c'=2,'zl'=4,'x'=4] {'zh'}, dimensions={0}, use_global_device_ids=true | all-gather | bytes 655360 | tf_op jit(solution)/shard_map/rows/all_gather | solution.py:35
  65.1 0.0 all-gather.11.cloned.1.call-start
  65.2 15.5 %all_gather.40 = bf16[4,3,8,4096]{3,2,1,0:T(8,128)(2,1)S(1)} all-gather(bf16[1,3,8,4096]{3,2,1,0:T(8,128)(2,1)S(1)} %bitcast.68), channel_id=1, replica_groups=mesh['y'=4,'zh'=4,'c'=2,'zl'=4,'x'=4] {'zl'}, dimensions={0}, use_global_device_ids=true | all-gather | bytes 983040 | tf_op jit(solution)/shard_map/columns/all_gather | solution.py:35
  80.7 0.1 copy.64
  80.8 0.1 broadcast_in_dim.32
  80.9 14.6 %all_to_all.30.cols_ref = bf16[4,1,32,4096]{3,2,1,0:T(8,128)(2,1)S(1)} all-to-all(bf16[4,1,32,4096]{3,2,1,0:T(8,128)(2,1)S(1)} %broadcast_in_dim.32), channel_id=1, replica_groups=mesh['y'=4,'zh'=4,'c'=2,'zl'=4,'x'=4] {'x'}, dimensions={0} | all-to-all | bytes 2097152 | tf_op jit(solution)/shard_map/columns/all_to_all | solution.py:21
  95.5 5.0 %all-gather.9.cloned.1.call-done = bf16[16,2,128,256]{3,2,1,0:T(8,128)(2,1)} async-done(((bf16[4,2,128,256]{3,2,1,0:T(8,128)(2,1)}), bf16[16,2,128,256]{3,2,1,0:T(8,128)(2,1)}) %all-gather.9.cloned.1.call-update) | async-done | bytes 2097168 | tf_op jit(solution)/shard_map/rows/all_gather | solution.py:35
  100.5 0.8 slice.20
  101.4 2.6 %collective-permute-start = (bf16[16,2,128,256]{3,2,1,0:T(8,128)(2,1)}, bf16[16,2,128,256]{3,2,1,0:T(8,128)(2,1)S(1)}, u32[]{:S(2)}, u32[]{:S(2)}) collective-permute-start(bf16[16,2,128,256]{3,2,1,0:T(8,128)(2,1)} %all-gather.9.cloned.1.call-done), channel_id=1, source_target_pairs={{0,16},{16,0},{1,17},{17,1},{2,18},{18,2},{3,19},{19,3},{4,20},{20... | collective-permute-start | bytes 6291464 | tf_op jit(solution)/shard_map/rows/ppermute | solution.py:213
  104.0 3.9 %collective-permute-done.other_ref = bf16[16,2,128,256]{3,2,1,0:T(8,128)(2,1)S(1)} collective-permute-done((bf16[16,2,128,256]{3,2,1,0:T(8,128)(2,1)}, bf16[16,2,128,256]{3,2,1,0:T(8,128)(2,1)S(1)}, u32[]{:S(2)}, u32[]{:S(2)}) %collective-permute-start) | collective-permute-done | bytes 2097184 | tf_op jit(solution)/shard_map/rows/ppermute | solution.py:213
  107.9 1.6 copy-done
  109.5 1.8 grad_block.1
  111.4 1.3 copy-done.2
  112.7 22.7 %all-gather.2 = bf16[512,256]{1,0:T(8,128)(2,1)S(1)} all-gather(bf16[128,256]{1,0:T(8,128)(2,1)S(1)} %get-tuple-element.23), channel_id=4, replica_groups=mesh['y'=4,'zh'=4,'c'=2,'zl'=4,'x'=4] {'zh'}, dimensions={0}, use_global_device_ids=true | all-gather | bytes 327680 | tf_op jit(solution)/shard_map/grad_rows/all_gather | solution.py:35
  135.4 1.1 broadcast_in_dim.33
  136.5 3.5 %all-to-all-start.2 = ((bf16[4,4,128,256]{3,2,1,0:T(8,128)(2,1)}), bf16[4,4,128,256]{3,2,1,0:T(8,128)(2,1)S(1)}, u32[]{:S(2)}, u32[]{:S(2)}) async-start(bf16[4,4,128,256]{3,2,1,0:T(8,128)(2,1)} %broadcast_in_dim.33), calls=%async_computation.2 | async-start | bytes 2097152 | tf_op jit(solution)/shard_map/grad_rows/all_to_all | solution.py:21
  140.0 0.1 pad.3.clone
  140.1 1.1 all-gather.11.cloned.1.call-done
  141.2 1.6 copy-done.3
  142.8 1.6 copy-done.4
  144.4 2.7 %products.1 = (f32[256,512]{1,0:T(8,128)S(1)}, bf16[256,512]{1,0:T(8,128)(2,1)S(1)}, f32[8,256]{1,0:T(8,128)S(1)}) custom-call(bf16[4,2,32,4096]{3,2,1,0:T(8,128)(2,1)S(1)} %bitcast.53, bf16[16,2,128,256]{3,2,1,0:T(8,128)(2,1)S(1)} %copy-done.1, bf16[16,2,128,256]{3,2,1,0:T(8,128)(2,1)S(1)} %copy-done.3, f32[16,256]{1,0:T(8,128)S(1)} %get-tuple-element.26.stats_ref.refs_4_), custom_call_target="tpu_custom_call" | custom-call | flops 1073741824 | bytes 7102464 | tf_op jit(solution)/shard_map/products/products/pallas_call | solution.py:187
  147.2 0.8 copy-done.6
  148.0 13.1 %all_gather.45 = bf16[4,128,256]{2,1,0:T(8,128)(2,1)} all-gather(bf16[1,128,256]{2,1,0:T(8,128)(2,1)S(1)} %bitcast.70), channel_id=1, replica_groups=mesh['y'=4,'zh'=4,'c'=2,'zl'=4,'x'=4] {'zl'}, dimensions={0}, use_global_device_ids=true | all-gather | bytes 327680 | tf_op jit(solution)/shard_map/products/all_gather | solution.py:35
  161.0 0.2 broadcast_in_dim.34
  161.3 8.6 %all_to_all.31 = bf16[2,4,4,128,256]{4,3,2,1,0:T(8,128)(2,1)S(1)} all-to-all(bf16[2,4,4,128,256]{4,3,2,1,0:T(8,128)(2,1)S(1)} %broadcast_in_dim.34), channel_id=1, replica_groups=mesh['y'=4,'zh'=4,'c'=2,'zl'=4,'x'=4] {'c'}, dimensions={0} | all-to-all | bytes 4194304 | tf_op jit(solution)/shard_map/grad_rows/all_to_all | solution.py:21
  169.9 0.3 copy.54
  170.2 2.5 %fusion.4 = (f32[256]{0:T(256)S(1)}, f32[4,4,4,4,2,8]{5,1,0,3,2,4:T(4,128)S(1)}) fusion(bf16[4,4,4,4,2,8,256]{6,5,1,0,3,2,4:T(8,128)(2,1)S(1)} %bitcast.61, s32[4,4,2,8]{3,1,0,2:T(4,128)S(1)} %multiply_add_fusion, s32[]{:T(128)S(6)} %add.99, s32[4]{0:T(128)S(1)} %iota_multiply_fusion), kind=kLoop, calls=%fused_computation.10 | loop fusion | flops 13627136 | bytes 2115604 | tf_op jit(solution)/shard_map/moments/reduce_sum | solution.py:280
  172.6 0.2 copy.55
  172.8 0.4 reduce_sum.21
  173.2 0.7 convolution_convert_fusion
  173.9 1.3 maximum_maximum_fusion
  175.3 4.2 %all-to-all-start.4 = ((bf16[4,4,272,128]{3,2,1,0:T(8,128)(2,1)}), bf16[4,4,272,128]{3,2,1,0:T(8,128)(2,1)S(1)}, u32[]{:S(2)}, u32[]{:S(2)}) async-start(bf16[4,4,272,128]{3,2,1,0:T(8,128)(2,1)} %maximum_maximum_fusion), calls=%async_computation.4 | async-start | bytes 2228224 | tf_op jit(solution)/shard_map/weight_b/all_to_all | solution.py:297
  179.5 0.7 all-gather.13.cloned.1.call-update
  180.2 14.5 %all-to-all-done.4.refs_0_ = bf16[4,4,272,128]{3,2,1,0:T(8,128)(2,1)S(1)} async-done(((bf16[4,4,272,128]{3,2,1,0:T(8,128)(2,1)}), bf16[4,4,272,128]{3,2,1,0:T(8,128)(2,1)S(1)}, u32[]{:S(2)}, u32[]{:S(2)}) %all-to-all-start.4) | async-done | bytes 1114144 | tf_op jit(solution)/shard_map/weight_b/all_to_all | solution.py:297
  194.7 0.9 fold.1
  195.6 3.4 %all-to-all-start.5 = ((bf16[4,272,128]{2,1,0:T(8,128)(2,1)}), bf16[4,272,128]{2,1,0:T(8,128)(2,1)S(1)}, u32[]{:S(2)}, u32[]{:S(2)}) async-start(bf16[4,272,128]{2,1,0:T(8,128)(2,1)} %fold.1), calls=%async_computation.5 | async-start | bytes 557056 | tf_op jit(solution)/shard_map/weight_b/all_to_all | solution.py:303
  199.0 1.0 fusion.22
  200.0 13.2 %all-gather.13.cloned.1.call-done = bf16[16,128,256]{2,1,0:T(8,128)(2,1)} async-done(((bf16[4,128,256]{2,1,0:T(8,128)(2,1)}), bf16[16,128,256]{2,1,0:T(8,128)(2,1)}) %all-gather.13.cloned.1.call-update) | async-done | bytes 1048592 | tf_op jit(solution)/shard_map/products/all_gather | solution.py:35
  213.2 1.2 copy-done.5
  214.4 0.5 weight_a.1.side_ref
  214.9 0.8 finish.1
  (24 shorter events, 0.2 us)
Async XLA Ops:
  10.2 54.9 %all-to-all-start = ((bf16[32,3,8,128]{3,2,1,0:T(8,128)(2,1)}), bf16[32,3,8,128]{3,2,1,0:T(8,128)(2,1)S(1)}, u32[]{:S(2)}, u32[]{:S(2)}) async-start(bf16[32,3,8,128]{3,2,1,0:T(8,128)(2,1)} %copy.51), calls=%async_computation | async-start | bytes 393216 | tf_op jit(solution)/shard_map/columns/all_to_all | solution.py:220
  29.5 71.0 %all-gather.9.cloned.1.call-start = ((), (), s32[]{:S(2)}) async-start(), calls=%async_computation.6 | async-start | bytes 2621440 | tf_op jit(solution)/shard_map/rows/all_gather | solution.py:35
  65.1 76.1 %all-gather.11.cloned.1.call-start = ((), (), s32[]{:S(2)}) async-start(), calls=%async_computation.7 | async-start | bytes 2621440 | tf_op jit(solution)/shard_map/columns/all_gather | solution.py:35
  101.4 6.6 %collective-permute-start = (bf16[16,2,128,256]{3,2,1,0:T(8,128)(2,1)}, bf16[16,2,128,256]{3,2,1,0:T(8,128)(2,1)S(1)}, u32[]{:S(2)}, u32[]{:S(2)}) collective-permute-start(bf16[16,2,128,256]{3,2,1,0:T(8,128)(2,1)} %all-gather.9.cloned.1.call-done), channel_id=1, source_target_pairs={{0,16},{16,0},{1,17},{17,1},{2,18},{18,2},{3,19},{19,3},{4,20},{20... | collective-permute-start | bytes 6291464 | tf_op jit(solution)/shard_map/rows/ppermute | solution.py:213
  107.9 1.6 copy-start
  111.3 1.3 copy-start.2
  112.7 28.5 %copy-start.1 = (bf16[16,2,128,256]{3,2,1,0:T(8,128)(2,1)S(1)}, bf16[16,2,128,256]{3,2,1,0:T(8,128)(2,1)}, u32[]{:S(2)}) copy-start(bf16[16,2,128,256]{3,2,1,0:T(8,128)(2,1)} %all-gather.9.cloned.1.call-done) | copy-start | bytes 6291460
  136.5 24.5 %all-to-all-start.2 = ((bf16[4,4,128,256]{3,2,1,0:T(8,128)(2,1)}), bf16[4,4,128,256]{3,2,1,0:T(8,128)(2,1)S(1)}, u32[]{:S(2)}, u32[]{:S(2)}) async-start(bf16[4,4,128,256]{3,2,1,0:T(8,128)(2,1)} %broadcast_in_dim.33), calls=%async_computation.2 | async-start | bytes 2097152 | tf_op jit(solution)/shard_map/grad_rows/all_to_all | solution.py:21
  141.2 1.6 copy-start.3
  142.8 1.6 copy-start.4
  147.1 0.8 copy-start.6
  175.3 19.4 %all-to-all-start.4 = ((bf16[4,4,272,128]{3,2,1,0:T(8,128)(2,1)}), bf16[4,4,272,128]{3,2,1,0:T(8,128)(2,1)S(1)}, u32[]{:S(2)}, u32[]{:S(2)}) async-start(bf16[4,4,272,128]{3,2,1,0:T(8,128)(2,1)} %maximum_maximum_fusion), calls=%async_computation.4 | async-start | bytes 2228224 | tf_op jit(solution)/shard_map/weight_b/all_to_all | solution.py:297
  179.5 33.7 %all-gather.13.cloned.1.call-start = ((), (), s32[]{:S(2)}) async-start(), calls=%async_computation.8 | async-start | bytes 1310720 | tf_op jit(solution)/shard_map/products/all_gather | solution.py:35
  195.6 19.4 %all-to-all-start.5 = ((bf16[4,272,128]{2,1,0:T(8,128)(2,1)}), bf16[4,272,128]{2,1,0:T(8,128)(2,1)S(1)}, u32[]{:S(2)}, u32[]{:S(2)}) async-start(bf16[4,272,128]{2,1,0:T(8,128)(2,1)} %fold.1), calls=%async_computation.5 | async-start | bytes 557056 | tf_op jit(solution)/shard_map/weight_b/all_to_all | solution.py:303
  213.2 1.2 copy-start.5
Sparse Core Ops, SparseCore 0:
  65.2 35.2 all-gather.8
  102.6 38.5 all-gather.10
  182.4 30.7 all-gather.12

commit v4 on v3

--- a/solution.py
+++ b/solution.py
@@ -83,6 +83,17 @@
 
 def matmul(left, right):
     return jnp.dot(left, right, preferred_element_type=f32)
+
+
+def open_kernel(z_a, z_b, h_a, h_b, rows_ref, cut_ref, held_a, held_b, sems):
+    targets = (rows_ref.at[0], rows_ref.at[1], held_a, held_b)
+    copies = [pltpu.make_async_copy(v, to, sems.at[i]) for i, (v, to) in enumerate(zip((z_a, z_b, h_a, h_b), targets))]
+    for copy in copies:
+        copy.start()
+    copies[0].wait()
+    for i, ref in enumerate((rows_ref.at[1], held_a, held_b)):
+        copies[i + 1].wait()
+        cut_ref[i] = ref[...].astype(f32).T.astype(bf16)
 
 
 def grad_kernel(own_ref, other_ref, cols_ref, target_ref, grad_ref, stats_ref):
@@ -147,6 +158,33 @@
     return jnp.concatenate([high, low, pad], axis=0)
 
 
+def weight_b_kernel(pairs, block_ref, grads_ref, ba_ref, out_ref, second_ref):
+    n_x, n_zl, width, _ = grads_ref.shape
+    owned = ba_ref.shape[0]
+    square = lambda axis: lax.broadcasted_iota(jnp.int32, (width, width), axis)
+    on = square(0) == square(1)
+    lane = lax.broadcasted_iota(jnp.int32, (width, owned), 1)
+    second = jnp.zeros((8, width), f32)
+    sums = jnp.zeros((width, owned), f32)
+    for x in range(n_x):
+        for z in range(n_zl):
+            g = grads_ref[x, z]
+            part = lax.dot_general(g, ba_ref[...], (((1,), (1,)), ((), ())), preferred_element_type=f32)
+            out_ref[x, z, 0:width, :] = part.astype(bf16)
+            g = g.astype(f32)
+            diagonal = on & (block_ref[0] == x * n_zl + z)
+            w = g * jnp.where(diagonal, 1.0 + 0.5 * g, g * (0.5 / off_weight)) / pairs
+            second = second + fold(w)
+            sums = sums + jnp.where(lane == x * n_zl + z, jnp.sum(w, 1, keepdims=True), 0.0)
+    second_ref[...] = jnp.sum(second, 0, keepdims=True)
+    sums = sums.T
+    for x in range(n_x):
+        for z in range(n_zl):
+            row = sums[x * n_zl + z : x * n_zl + z + 1]
+            row = jnp.concatenate([row[:, i : i + owned] for i in range(0, width, owned)], axis=0)
+            out_ref[x, z, width:, :] = split(row, out_ref.shape[2] - width)
+
+
 def fold_kernel(width, got_ref, out_ref):
     count, blocks, _, owned = got_ref.shape
     rows = out_ref.shape[1]
@@ -180,16 +218,20 @@
             out_ref[z * n_x + x] = result[first : first + sub]
 
 
-def call(kernel, name, flops, shapes, *operands):
+def call(kernel, name, flops, shapes, *operands, scalars=0, hbm=False, scratch=(), grant=16):
     size = lambda v: v.size * v.dtype.itemsize
     outs = jax.tree.leaves(shapes)
     moved = sum(size(v) for v in operands) + sum(size(v) for v in outs)
     return pl.pallas_call(
         kernel,
         out_shape=shapes,
-        in_specs=[pl.BlockSpec(memory_space=pltpu.VMEM)] * len(operands),
+        scratch_shapes=list(scratch),
+        in_specs=[
+            pl.BlockSpec(memory_space=pltpu.SMEM if i < scalars else pl.ANY if hbm else pltpu.VMEM)
+            for i in range(len(operands))
+        ],
         out_specs=jax.tree.map(lambda _: pl.BlockSpec(memory_space=pltpu.VMEM), shapes),
-        compiler_params=pltpu.CompilerParams(vmem_limit_bytes=16 * 2**20),
+        compiler_params=pltpu.CompilerParams(vmem_limit_bytes=grant * 2**20),
         cost_estimate=pl.CostEstimate(flops=flops, bytes_accessed=moved, transcendentals=0),
         name=name,
     )(*operands)
@@ -213,10 +255,17 @@
         return lax.ppermute(v, "c", [(0, 1), (1, 0)])
 
     with jax.named_scope("rows"):
-        rows = collect(jnp.stack([z_a, z_b]), "zh")
+        held = pltpu.VMEM((local_rows, width), bf16)
+        rows, cut = call(
+            open_kernel, "open", 0,
+            (shape((2, local_rows, width), bf16), shape((3, width, local_rows), bf16)),
+            z_a, z_b, h_a, h_b, hbm=True, grant=56,
+            scratch=(held, held, pltpu.SemaphoreType.DMA((4,))),
+        )
+        rows = collect(rows, "zh")
 
     with jax.named_scope("columns"):
-        cut = jnp.stack([v.T.reshape(n_dp, sub, local_rows) for v in (z_b, h_a, h_b)], axis=1)
+        cut = cut.reshape(3, n_dp, sub, local_rows).transpose(1, 0, 2, 3)
         cut = lax.all_to_all(cut, DP, 0, 0, tiled=True)
         cut, rows = together((cut, rows))
         cut = cut.reshape(n_y, n_zh, n_c, 3, sub, local_rows)
@@ -272,29 +321,14 @@
         grads = gather(grads, "c")
         grads = grads.reshape(n_c, n_y, n_zh, n_x, n_zl, sub, width)
         grads = grads.transpose(3, 4, 1, 2, 0, 5, 6).reshape(n_x, n_zl, width, width)
-    with jax.named_scope("moments"):
-        g = grads.astype(f32)
-        four = lambda d: lax.broadcasted_iota(jnp.int32, g.shape, d)
-        on = (four(1) * n_x + four(0) == f_index) & (four(2) == four(3))
-        weighed = g * jnp.where(on, 1.0 + 0.5 * g, g * (0.5 / off_weight)) / pairs
-        second_a = jnp.sum(weighed, (0, 1, 2))
-        part_b = jnp.sum(weighed, 3)
-
     with jax.named_scope("weight_b"):
-        flat = grads.reshape(n_feat * width, width)
-        w_b = dot(flat, p_ba, ((1,), (1,))).astype(bf16).reshape(n_x, n_zl, width, owned)
-
-        def with_moments(w, m):
-            high = m.astype(bf16)
-            low = (m - high.astype(f32)).astype(bf16)
-            lead = m.shape[:-1]
-            extra = jnp.concatenate(
-                [high.reshape(*lead, -1, owned), low.reshape(*lead, -1, owned)], axis=-2
-            )
-            pad = jnp.zeros((*lead, 16 - extra.shape[-2], owned), bf16)
-            return jnp.concatenate([w, extra, pad], axis=-2)
-
-        got = lax.all_to_all(with_moments(w_b, part_b), "x", 0, 0, tiled=True)
+        block = (lax.axis_index("x") * n_zl + lax.axis_index("zl")).astype(jnp.int32)[None]
+        got, second_a = call(
+            lambda *refs: weight_b_kernel(pairs, *refs), "weight_b", 2 * owned * n_feat * width * width,
+            (shape((n_x, n_zl, width + 16, owned), bf16), shape((1, width), f32)),
+            block, grads, p_ba, scalars=1,
+        )
+        got = lax.all_to_all(got, "x", 0, 0, tiled=True)
         rows_out = got.shape[2]
         got = call(
             lambda *refs: fold_kernel(width, *refs), "fold", 0,
@@ -306,7 +340,7 @@
         side = call(
             lambda *refs: weight_a_kernel(pairs, *refs), "weight_a", 2 * owned * n_feat * width * width,
             shape((2 * owned + 8, width), f32),
-            p_ab, grads, p_aa, p_bb, stats_a, inverse_b, second_a[None],
+            p_ab, grads, p_aa, p_bb, stats_a, inverse_b, second_a,
         )
 
     with jax.named_scope("finish"):

time: 223 us -> 219 us (0.982)
  other arithmetic: 4.8 us -> 0.07 us
  blocking collectives: 109 us -> 105 us
  waiting for transfers between devices: 38.4 us -> 41.9 us
  Pallas kernels: 6.67 us -> 10 us
    all_gather x3, waiting for transfers between devices: 19.3 us -> 22.8 us  [collect(): return lax.all_gather(block, axis, axis=0, tiled=False)]
    pallas_call x5 -> x7, Pallas kernels: 6.67 us -> 10 us  [call(): pl.pallas_call(kernel, out_shape=shapes, scratch_shapes=list(scratch), in...]
    all_gather x4, blocking collectives: 85.8 us -> 83 us  [collect(): return lax.all_gather(block, axis, axis=0, tiled=False)]
    reduce_sum x1 -> x0, other arithmetic: 2.46 us -> none  [body(): second_a = jnp.sum(weighed, (0, 1, 2))]
    unnamed x17 -> x16, local copies, waits for them, and re-layouts: 11 us -> 9.17 us
  transfers between devices with their start and end apart: 8 -> 8, of which waited for: 5 -> 5; matrix products, arithmetic and copies ran while one was open for 2% -> 1% of each run, Pallas kernels for 3% -> 3%
where the time goes in v4:
time: 219 us; the launch traced here: 218 us
  blocking collectives  105 us (48%)
  waiting for transfers between devices  41.9 us (19%)
  starting transfers between devices  33.4 us (15%)
  local copies, waits for them, and re-layouts  14.4 us (7%)
  between operations  13.3 us (6%)
  Pallas kernels  10 us (5%)
    all_gather x4, blocking collectives, collect(): return lax.all_gather(block, axis, axis=0, tiled=False)  83 us
    all_gather x3, waiting for transfers between devices, collect(): return lax.all_gather(block, axis, axis=0, tiled=False)  22.8 us
    all_to_all x2, blocking collectives, gather(): return lax.all_to_all(copies, axis, 0, 0, tiled=True)  22.1 us
    all_to_all x1, starting transfers between devices, body(): cut = lax.all_to_all(cut, DP, 0, 0, tiled=True)  19.4 us
    all_to_all x1, waiting for transfers between devices, body(): got = lax.all_to_all(got, 'x', 0, 0, tiled=True)  14.5 us
    pallas_call x7, Pallas kernels, call(): pl.pallas_call(kernel, out_shape=shapes, scratch_shapes=list(scratch), in...  10 us
    unnamed x16, local copies, waits for them, and re-layouts  9.17 us
  transfers between devices with their start and end apart: 8, of which 5 were waited for; matrix products, arithmetic and copies ran while one was open for 1% of the time, Pallas kernels for 3%

profile of v4, /device:TPU:1, one launch (start us, length us, event | category | flops | bytes accessed | tf_op | source)
XLA Modules:
  0.0 218.3 jit_solution(16658262424535303311)
XLA Ops:
  6.5 1.9 open.1
  8.4 1.6 copy_bitcast_fusion.2
  10.1 19.4 %all-to-all-start = ((bf16[32,3,8,128]{3,2,1,0:T(8,128)(2,1)}), bf16[32,3,8,128]{3,2,1,0:T(8,128)(2,1)S(1)}, u32[]{:S(2)}, u32[]{:S(2)}) async-start(bf16[32,3,8,128]{3,2,1,0:T(8,128)(2,1)} %copy_bitcast_fusion.2), calls=%async_computation | async-start | bytes 393216 | tf_op jit(solution)/shard_map/columns/all_to_all | solution.py:269
  29.5 0.0 all-gather.9.cloned.1.call-start
  29.5 34.1 %all-gather = bf16[8,128,256]{2,1,0:T(8,128)(2,1)} all-gather(bf16[2,128,256]{2,1,0:T(8,128)(2,1)} %get-tuple-element.24), channel_id=2, replica_groups=mesh['y'=4,'zh'=4,'c'=2,'zl'=4,'x'=4] {'zh'}, dimensions={0}, use_global_device_ids=true | all-gather | bytes 655360 | tf_op jit(solution)/shard_map/rows/all_gather | solution.py:35
  63.6 0.0 all-to-all-done
  63.6 0.0 all-gather.9.cloned.1.call-update
  63.6 0.0 all-gather.11.cloned.1.call-start
  63.8 14.1 %all_gather.40 = bf16[4,3,8,4096]{3,2,1,0:T(8,128)(2,1)S(1)} all-gather(bf16[1,3,8,4096]{3,2,1,0:T(8,128)(2,1)S(1)} %bitcast.58), channel_id=1, replica_groups=mesh['y'=4,'zh'=4,'c'=2,'zl'=4,'x'=4] {'zl'}, dimensions={0}, use_global_device_ids=true | all-gather | bytes 983040 | tf_op jit(solution)/shard_map/columns/all_gather | solution.py:35
  77.9 0.1 copy.50
  77.9 0.1 broadcast_in_dim.30
  78.0 13.6 %all_to_all.30.cols_ref = bf16[4,1,32,4096]{3,2,1,0:T(8,128)(2,1)S(1)} all-to-all(bf16[4,1,32,4096]{3,2,1,0:T(8,128)(2,1)S(1)} %broadcast_in_dim.30), channel_id=1, replica_groups=mesh['y'=4,'zh'=4,'c'=2,'zl'=4,'x'=4] {'x'}, dimensions={0} | all-to-all | bytes 2097152 | tf_op jit(solution)/shard_map/columns/all_to_all | solution.py:21
  91.6 7.5 %all-gather.9.cloned.1.call-done = bf16[16,2,128,256]{3,2,1,0:T(8,128)(2,1)} async-done(((bf16[4,2,128,256]{3,2,1,0:T(8,128)(2,1)}), bf16[16,2,128,256]{3,2,1,0:T(8,128)(2,1)}) %all-gather.9.cloned.1.call-update) | async-done | bytes 2097168 | tf_op jit(solution)/shard_map/rows/all_gather | solution.py:35
  99.2 0.8 slice.20
  100.0 0.0 all-gather.11.cloned.1.call-update
  100.0 2.6 %collective-permute-start = (bf16[16,2,128,256]{3,2,1,0:T(8,128)(2,1)}, bf16[16,2,128,256]{3,2,1,0:T(8,128)(2,1)S(1)}, u32[]{:S(2)}, u32[]{:S(2)}) collective-permute-start(bf16[16,2,128,256]{3,2,1,0:T(8,128)(2,1)} %all-gather.9.cloned.1.call-done), channel_id=1, source_target_pairs={{0,16},{16,0},{1,17},{17,1},{2,18},{18,2},{3,19},{19,3},{4,20},{20... | collective-permute-start | bytes 6291464 | tf_op jit(solution)/shard_map/rows/ppermute | solution.py:255
  102.7 3.9 %collective-permute-done.other_ref = bf16[16,2,128,256]{3,2,1,0:T(8,128)(2,1)S(1)} collective-permute-done((bf16[16,2,128,256]{3,2,1,0:T(8,128)(2,1)}, bf16[16,2,128,256]{3,2,1,0:T(8,128)(2,1)S(1)}, u32[]{:S(2)}, u32[]{:S(2)}) %collective-permute-start) | collective-permute-done | bytes 2097184 | tf_op jit(solution)/shard_map/rows/ppermute | solution.py:255
  106.6 1.6 copy-done
  108.2 1.8 grad_block.1
  110.0 0.0 copy-start.2
  110.0 1.4 copy-done.2
  111.4 21.7 %all-gather.2 = bf16[512,256]{1,0:T(8,128)(2,1)S(1)} all-gather(bf16[128,256]{1,0:T(8,128)(2,1)S(1)} %get-tuple-element.29), channel_id=4, replica_groups=mesh['y'=4,'zh'=4,'c'=2,'zl'=4,'x'=4] {'zh'}, dimensions={0}, use_global_device_ids=true | all-gather | bytes 327680 | tf_op jit(solution)/shard_map/grad_rows/all_gather | solution.py:35
  133.1 1.1 broadcast_in_dim.31
  134.2 3.5 %all-to-all-start.2 = ((bf16[4,4,128,256]{3,2,1,0:T(8,128)(2,1)}), bf16[4,4,128,256]{3,2,1,0:T(8,128)(2,1)S(1)}, u32[]{:S(2)}, u32[]{:S(2)}) async-start(bf16[4,4,128,256]{3,2,1,0:T(8,128)(2,1)} %broadcast_in_dim.31), calls=%async_computation.2 | async-start | bytes 2097152 | tf_op jit(solution)/shard_map/grad_rows/all_to_all | solution.py:21
  137.7 2.1 all-gather.11.cloned.1.call-done
  139.9 0.0 copy-done.1
  139.9 1.6 copy-done.3
  141.5 1.6 copy-done.4
  143.1 2.7 %products.1 = (f32[256,512]{1,0:T(8,128)S(1)}, bf16[256,512]{1,0:T(8,128)(2,1)S(1)}, f32[8,256]{1,0:T(8,128)S(1)}) custom-call(bf16[4,2,32,4096]{3,2,1,0:T(8,128)(2,1)S(1)} %bitcast.45, bf16[16,2,128,256]{3,2,1,0:T(8,128)(2,1)S(1)} %copy-done.1, bf16[16,2,128,256]{3,2,1,0:T(8,128)(2,1)S(1)} %copy-done.3, f32[16,256]{1,0:T(8,128)S(1)} %get-tuple-element.32.stats_ref.refs_4_), custom_call_target="tpu_custom_call" | custom-call | flops 1073741824 | bytes 7102464 | tf_op jit(solution)/shard_map/products/products/pallas_call | solution.py:225
  145.8 0.8 copy-done.7
  146.6 13.1 %all_gather.45 = bf16[4,128,256]{2,1,0:T(8,128)(2,1)} all-gather(bf16[1,128,256]{2,1,0:T(8,128)(2,1)S(1)} %bitcast.59), channel_id=1, replica_groups=mesh['y'=4,'zh'=4,'c'=2,'zl'=4,'x'=4] {'zl'}, dimensions={0}, use_global_device_ids=true | all-gather | bytes 327680 | tf_op jit(solution)/shard_map/products/all_gather | solution.py:35
  159.7 0.0 all-to-all-done.2
  159.7 0.2 broadcast_in_dim.32
  159.9 8.5 %all_to_all.31 = bf16[2,4,4,128,256]{4,3,2,1,0:T(8,128)(2,1)S(1)} all-to-all(bf16[2,4,4,128,256]{4,3,2,1,0:T(8,128)(2,1)S(1)} %broadcast_in_dim.32), channel_id=1, replica_groups=mesh['y'=4,'zh'=4,'c'=2,'zl'=4,'x'=4] {'c'}, dimensions={0} | all-to-all | bytes 4194304 | tf_op jit(solution)/shard_map/grad_rows/all_to_all | solution.py:21
  168.5 0.3 copy.40
  168.7 1.5 weight_b.1
  170.2 1.0 copy-done.5
  171.2 4.4 %all-to-all-start.4 = ((bf16[4,4,272,128]{3,2,1,0:T(8,128)(2,1)}), bf16[4,4,272,128]{3,2,1,0:T(8,128)(2,1)S(1)}, u32[]{:S(2)}, u32[]{:S(2)}) async-start(bf16[4,4,272,128]{3,2,1,0:T(8,128)(2,1)} %copy-done.5), calls=%async_computation.4 | async-start | bytes 2228224 | tf_op jit(solution)/shard_map/weight_b/all_to_all | solution.py:331
  175.6 0.7 all-gather.13.cloned.1.call-update
  176.3 14.5 %all-to-all-done.4.refs_0_ = bf16[4,4,272,128]{3,2,1,0:T(8,128)(2,1)S(1)} async-done(((bf16[4,4,272,128]{3,2,1,0:T(8,128)(2,1)}), bf16[4,4,272,128]{3,2,1,0:T(8,128)(2,1)S(1)}, u32[]{:S(2)}, u32[]{:S(2)}) %all-to-all-start.4) | async-done | bytes 1114144 | tf_op jit(solution)/shard_map/weight_b/all_to_all | solution.py:331
  190.8 0.9 fold.1
  191.7 3.4 %all-to-all-start.5 = ((bf16[4,272,128]{2,1,0:T(8,128)(2,1)}), bf16[4,272,128]{2,1,0:T(8,128)(2,1)S(1)}, u32[]{:S(2)}, u32[]{:S(2)}) async-start(bf16[4,272,128]{2,1,0:T(8,128)(2,1)} %fold.1), calls=%async_computation.5 | async-start | bytes 557056 | tf_op jit(solution)/shard_map/weight_b/all_to_all | solution.py:337
  195.1 1.0 fusion.16
  196.1 13.1 %all-gather.13.cloned.1.call-done = bf16[16,128,256]{2,1,0:T(8,128)(2,1)} async-done(((bf16[4,128,256]{2,1,0:T(8,128)(2,1)}), bf16[16,128,256]{2,1,0:T(8,128)(2,1)}) %all-gather.13.cloned.1.call-update) | async-done | bytes 1048592 | tf_op jit(solution)/shard_map/products/all_gather | solution.py:35
  209.2 1.2 copy-done.6
  210.5 0.5 weight_a.1.side_ref
  210.9 0.0 all-to-all-done.5.got_ref
  211.0 0.8 finish.1
  (13 shorter events, 0.2 us)
Async XLA Ops:
  10.1 53.5 %all-to-all-start = ((bf16[32,3,8,128]{3,2,1,0:T(8,128)(2,1)}), bf16[32,3,8,128]{3,2,1,0:T(8,128)(2,1)S(1)}, u32[]{:S(2)}, u32[]{:S(2)}) async-start(bf16[32,3,8,128]{3,2,1,0:T(8,128)(2,1)} %copy_bitcast_fusion.2), calls=%async_computation | async-start | bytes 393216 | tf_op jit(solution)/shard_map/columns/all_to_all | solution.py:269
  29.5 69.7 %all-gather.9.cloned.1.call-start = ((), (), s32[]{:S(2)}) async-start(), calls=%async_computation.6 | async-start | bytes 2621440 | tf_op jit(solution)/shard_map/rows/all_gather | solution.py:35
  63.6 76.2 %all-gather.11.cloned.1.call-start = ((), (), s32[]{:S(2)}) async-start(), calls=%async_computation.7 | async-start | bytes 2621440 | tf_op jit(solution)/shard_map/columns/all_gather | solution.py:35
  100.0 6.6 %collective-permute-start = (bf16[16,2,128,256]{3,2,1,0:T(8,128)(2,1)}, bf16[16,2,128,256]{3,2,1,0:T(8,128)(2,1)S(1)}, u32[]{:S(2)}, u32[]{:S(2)}) collective-permute-start(bf16[16,2,128,256]{3,2,1,0:T(8,128)(2,1)} %all-gather.9.cloned.1.call-done), channel_id=1, source_target_pairs={{0,16},{16,0},{1,17},{17,1},{2,18},{18,2},{3,19},{19,3},{4,20},{20... | collective-permute-start | bytes 6291464 | tf_op jit(solution)/shard_map/rows/ppermute | solution.py:255
  106.6 1.6 copy-start
  110.0 1.4 copy-start.2
  111.4 28.5 %copy-start.1 = (bf16[16,2,128,256]{3,2,1,0:T(8,128)(2,1)S(1)}, bf16[16,2,128,256]{3,2,1,0:T(8,128)(2,1)}, u32[]{:S(2)}) copy-start(bf16[16,2,128,256]{3,2,1,0:T(8,128)(2,1)} %all-gather.9.cloned.1.call-done) | copy-start | bytes 6291460
  134.2 25.5 %all-to-all-start.2 = ((bf16[4,4,128,256]{3,2,1,0:T(8,128)(2,1)}), bf16[4,4,128,256]{3,2,1,0:T(8,128)(2,1)S(1)}, u32[]{:S(2)}, u32[]{:S(2)}) async-start(bf16[4,4,128,256]{3,2,1,0:T(8,128)(2,1)} %broadcast_in_dim.31), calls=%async_computation.2 | async-start | bytes 2097152 | tf_op jit(solution)/shard_map/grad_rows/all_to_all | solution.py:21
  139.9 1.6 copy-start.3
  141.5 1.6 copy-start.4
  145.8 0.8 copy-start.7
  170.2 1.0 copy-start.5
  171.2 19.6 %all-to-all-start.4 = ((bf16[4,4,272,128]{3,2,1,0:T(8,128)(2,1)}), bf16[4,4,272,128]{3,2,1,0:T(8,128)(2,1)S(1)}, u32[]{:S(2)}, u32[]{:S(2)}) async-start(bf16[4,4,272,128]{3,2,1,0:T(8,128)(2,1)} %copy-done.5), calls=%async_computation.4 | async-start | bytes 2228224 | tf_op jit(solution)/shard_map/weight_b/all_to_all | solution.py:331
  175.6 33.6 %all-gather.13.cloned.1.call-start = ((), (), s32[]{:S(2)}) async-start(), calls=%async_computation.8 | async-start | bytes 1310720 | tf_op jit(solution)/shard_map/products/all_gather | solution.py:35
  191.7 19.3 %all-to-all-start.5 = ((bf16[4,272,128]{2,1,0:T(8,128)(2,1)}), bf16[4,272,128]{2,1,0:T(8,128)(2,1)S(1)}, u32[]{:S(2)}, u32[]{:S(2)}) async-start(bf16[4,272,128]{2,1,0:T(8,128)(2,1)} %fold.1), calls=%async_computation.5 | async-start | bytes 557056 | tf_op jit(solution)/shard_map/weight_b/all_to_all | solution.py:337
  209.2 1.2 copy-start.6
Sparse Core Ops, SparseCore 0:
  63.8 35.3 all-gather.8
  101.3 38.5 all-gather.10
  178.5 30.6 all-gather.12

commit v5 on v4

--- a/solution.py
+++ b/solution.py
@@ -114,10 +114,11 @@
     grad_ref[...] = jnp.where(diagonal, -2.0 * (1.0 - corr), 2.0 * off_weight * corr).astype(bf16)
 
 
-def product_kernel(cols_ref, own_ref, other_ref, stats_ref, prod_ref, centered_ref, inverse_ref):
+def product_kernel(cols_ref, own_ref, other_ref, stats_ref, aa_ref, bb_ref, ab_ref, ba_ref, inverse_ref):
     pairs = cols_ref.shape[3]
     halves = (own_ref, other_ref)
-    owned, width = prod_ref.shape[0], prod_ref.shape[1] // 2
+    count, part = cols_ref.shape[0], cols_ref.shape[2]
+    owned, width = 2 * aa_ref.shape[0], aa_ref.shape[1]
     mean_a, inverse_a = stats_ref[0:1, :], stats_ref[8:9, :]
     mean_b, inverse_b = column_stats(halves, 1, pairs)
     inverse_ref[...] = jnp.broadcast_to(inverse_b, (8, width))
@@ -132,11 +133,15 @@
         sum_a, sum_b = sum_a + fold(a.astype(f32)), sum_b + fold(b.astype(f32))
         sum_h = sum_h + lanes(h.astype(f32))
     sum_h = jnp.sum(sum_h, 1, keepdims=True)
-    for side, prod, sums in ((0, prod_a, sum_a), (1, prod_b, sum_b)):
-        cols = pl.ds(side * width, width)
-        sums = jnp.sum(sums, 0, keepdims=True) / pairs
-        prod_ref[:, cols] = prod
-        centered_ref[:, cols] = (prod - sum_h * sums).astype(bf16)
+    for side, prod, sums, plain_ref, centered_ref in (
+        (0, prod_a, sum_a, aa_ref, ba_ref),
+        (1, prod_b, sum_b, bb_ref, ab_ref),
+    ):
+        centered = prod - sum_h * (jnp.sum(sums, 0, keepdims=True) / pairs)
+        for x in range(count):
+            block = lambda v, view: v[(2 * x + view) * part : (2 * x + view + 1) * part]
+            plain_ref[x * part : (x + 1) * part, :] = block(prod, side)
+            centered_ref[x * part : (x + 1) * part, :] = block(centered, 1 - side).astype(bf16)
 
 
 def weight_a_kernel(pairs, blocks_ref, grads_ref, aa_ref, bb_ref, stats_ref, inverse_ref, second_ref, out_ref):
@@ -301,17 +306,11 @@
     with jax.named_scope("grad_rows"):
         grads = gather(grads, "y")
     with jax.named_scope("products"):
-        prod, centered, inverse_b = call(
+        p_aa, p_bb, p_ab, p_ba, inverse_b = call(
             product_kernel, "products", 8 * pairs * owned * width,
-            (shape((2 * owned, 2 * width), f32), shape((2 * owned, 2 * width), bf16), shape((8, width), f32)),
+            (shape((owned, width), f32),) * 2 + (shape((owned, width), bf16),) * 2 + (shape((8, width), f32),),
             cols_h, own, other, stats_a,
         )
-        halves = lambda v: v.reshape(n_x, 2, n_zl * sub, 2 * width)
-        prod, centered = halves(prod), halves(centered)
-        p_aa = prod[:, 0, :, :width].reshape(owned, width)
-        p_bb = prod[:, 1, :, width:].reshape(owned, width)
-        p_ab = centered[:, 0, :, width:].reshape(owned, width)
-        p_ba = centered[:, 1, :, :width].reshape(owned, width)
         p_ab = collect(p_ab, "zl")
     grads, p_ab, p_ba = together((grads, p_ab, p_ba))
     with jax.named_scope("products"):

time: 219 us -> 218 us (level)
    unnamed x16 -> x14, local copies, waits for them, and re-layouts: 9.17 us -> 8.35 us
where the time goes in v5:
time: 218 us; the launch traced here: 217 us
  blocking collectives  105 us (48%)
  waiting for transfers between devices  43 us (20%)
  starting transfers between devices  33.5 us (15%)
  between operations  13.3 us (6%)
  local copies, waits for them, and re-layouts  12.6 us (6%)
  Pallas kernels  9.84 us (5%)
    all_gather x4, blocking collectives, collect(): return lax.all_gather(block, axis, axis=0, tiled=False)  83 us
    all_gather x3, waiting for transfers between devices, collect(): return lax.all_gather(block, axis, axis=0, tiled=False)  23.8 us
    all_to_all x2, blocking collectives, gather(): return lax.all_to_all(copies, axis, 0, 0, tiled=True)  22 us
    all_to_all x1, starting transfers between devices, body(): cut = lax.all_to_all(cut, DP, 0, 0, tiled=True)  19.4 us
    all_to_all x1, waiting for transfers between devices, body(): got = lax.all_to_all(got, 'x', 0, 0, tiled=True)  14.5 us
    pallas_call x7, Pallas kernels, call(): pl.pallas_call(kernel, out_shape=shapes, scratch_shapes=list(scratch), in...  9.84 us
    unnamed x14, local copies, waits for them, and re-layouts  8.35 us
    all_to_all x1, starting transfers between devices, body(): got = lax.all_to_all(got, 'x', 0, 0, tiled=True)  4.45 us
  transfers between devices with their start and end apart: 8, of which 5 were waited for; matrix products, arithmetic and copies ran while one was open for 1% of the time, Pallas kernels for 3%

profile of v5, /device:TPU:1, one launch (start us, length us, event | category | flops | bytes accessed | tf_op | source)
XLA Modules:
  0.0 217.3 jit_solution(8994765693068744575)
XLA Ops:
  6.5 1.9 open.1
  8.4 1.7 copy_bitcast_fusion.2
  10.1 19.4 %all-to-all-start = ((bf16[32,3,8,128]{3,2,1,0:T(8,128)(2,1)}), bf16[32,3,8,128]{3,2,1,0:T(8,128)(2,1)S(1)}, u32[]{:S(2)}, u32[]{:S(2)}) async-start(bf16[32,3,8,128]{3,2,1,0:T(8,128)(2,1)} %copy_bitcast_fusion.2), calls=%async_computation | async-start | bytes 393216 | tf_op jit(solution)/shard_map/columns/all_to_all | solution.py:274
  29.5 0.0 all-gather.10.cloned.1.call-start
  29.5 34.1 %all-gather = bf16[8,128,256]{2,1,0:T(8,128)(2,1)} all-gather(bf16[2,128,256]{2,1,0:T(8,128)(2,1)} %get-tuple-element.26), channel_id=2, replica_groups=mesh['y'=4,'zh'=4,'c'=2,'zl'=4,'x'=4] {'zh'}, dimensions={0}, use_global_device_ids=true | all-gather | bytes 655360 | tf_op jit(solution)/shard_map/rows/all_gather | solution.py:35
  63.6 0.0 all-to-all-done
  63.6 0.0 all-gather.10.cloned.1.call-update
  63.7 0.0 all-gather.12.cloned.1.call-start
  63.8 14.1 %all_gather.43 = bf16[4,3,8,4096]{3,2,1,0:T(8,128)(2,1)S(1)} all-gather(bf16[1,3,8,4096]{3,2,1,0:T(8,128)(2,1)S(1)} %bitcast.43), channel_id=1, replica_groups=mesh['y'=4,'zh'=4,'c'=2,'zl'=4,'x'=4] {'zl'}, dimensions={0}, use_global_device_ids=true | all-gather | bytes 983040 | tf_op jit(solution)/shard_map/columns/all_gather | solution.py:35
  77.9 0.1 copy.29
  78.0 0.1 broadcast_in_dim.30
  78.1 13.6 %all_to_all.30.cols_ref = bf16[4,1,32,4096]{3,2,1,0:T(8,128)(2,1)S(1)} all-to-all(bf16[4,1,32,4096]{3,2,1,0:T(8,128)(2,1)S(1)} %broadcast_in_dim.30), channel_id=1, replica_groups=mesh['y'=4,'zh'=4,'c'=2,'zl'=4,'x'=4] {'x'}, dimensions={0} | all-to-all | bytes 2097152 | tf_op jit(solution)/shard_map/columns/all_to_all | solution.py:21
  91.7 7.5 %all-gather.10.cloned.1.call-done = bf16[16,2,128,256]{3,2,1,0:T(8,128)(2,1)} async-done(((bf16[4,2,128,256]{3,2,1,0:T(8,128)(2,1)}), bf16[16,2,128,256]{3,2,1,0:T(8,128)(2,1)}) %all-gather.10.cloned.1.call-update) | async-done | bytes 2097168 | tf_op jit(solution)/shard_map/rows/all_gather | solution.py:35
  99.2 0.9 slice.8
  100.1 0.0 all-gather.12.cloned.1.call-update
  100.1 2.6 %collective-permute-start = (bf16[16,2,128,256]{3,2,1,0:T(8,128)(2,1)}, bf16[16,2,128,256]{3,2,1,0:T(8,128)(2,1)S(1)}, u32[]{:S(2)}, u32[]{:S(2)}) collective-permute-start(bf16[16,2,128,256]{3,2,1,0:T(8,128)(2,1)} %all-gather.10.cloned.1.call-done), channel_id=1, source_target_pairs={{0,16},{16,0},{1,17},{17,1},{2,18},{18,2},{3,19},{19,3},{4,20},{20... | collective-permute-start | bytes 6291464 | tf_op jit(solution)/shard_map/rows/ppermute | solution.py:260
  102.7 3.9 %collective-permute-done.other_ref = bf16[16,2,128,256]{3,2,1,0:T(8,128)(2,1)S(1)} collective-permute-done((bf16[16,2,128,256]{3,2,1,0:T(8,128)(2,1)}, bf16[16,2,128,256]{3,2,1,0:T(8,128)(2,1)S(1)}, u32[]{:S(2)}, u32[]{:S(2)}) %collective-permute-start) | collective-permute-done | bytes 2097184 | tf_op jit(solution)/shard_map/rows/ppermute | solution.py:260
  106.7 1.6 copy-done
  108.2 1.8 grad_block.1
  110.1 0.0 copy-start.2
  110.1 1.3 copy-done.2
  111.4 21.7 %all-gather.2 = bf16[512,256]{1,0:T(8,128)(2,1)S(1)} all-gather(bf16[128,256]{1,0:T(8,128)(2,1)S(1)} %get-tuple-element.31), channel_id=4, replica_groups=mesh['y'=4,'zh'=4,'c'=2,'zl'=4,'x'=4] {'zh'}, dimensions={0}, use_global_device_ids=true | all-gather | bytes 327680 | tf_op jit(solution)/shard_map/grad_rows/all_gather | solution.py:35
  133.2 1.1 broadcast_in_dim.31
  134.2 3.5 %all-to-all-start.2 = ((bf16[4,4,128,256]{3,2,1,0:T(8,128)(2,1)}), bf16[4,4,128,256]{3,2,1,0:T(8,128)(2,1)S(1)}, u32[]{:S(2)}, u32[]{:S(2)}) async-start(bf16[4,4,128,256]{3,2,1,0:T(8,128)(2,1)} %broadcast_in_dim.31), calls=%async_computation.2 | async-start | bytes 2097152 | tf_op jit(solution)/shard_map/grad_rows/all_to_all | solution.py:21
  137.8 2.1 all-gather.12.cloned.1.call-done
  139.9 0.0 copy-done.1
  139.9 1.6 copy-done.3
  141.5 1.6 copy-done.4
  143.1 2.6 %products.1 = (f32[128,256]{1,0:T(8,128)S(1)}, f32[128,256]{1,0:T(8,128)S(1)}, bf16[128,256]{1,0:T(8,128)(2,1)S(1)}, bf16[128,256]{1,0:T(8,128)(2,1)S(1)}, f32[8,256]{1,0:T(8,128)S(1)}) custom-call(bf16[4,2,32,4096]{3,2,1,0:T(8,128)(2,1)S(1)} %bitcast.34, bf16[16,2,128,256]{3,2,1,0:T(8,128)(2,1)S(1)} %copy-done.1, bf16[16,2,128,256]{3,2,1,0:T(8,128)(2,1)S(1)} %copy-done.3, ...), custom_call_target="tpu_custom_call" | custom-call | flops 1073741824 | bytes 6709248 | tf_op jit(solution)/shard_map/products/products/pallas_call | solution.py:230
  145.7 13.1 %all-gather.4 = bf16[512,256]{1,0:T(8,128)(2,1)} all-gather(bf16[128,256]{1,0:T(8,128)(2,1)S(1)} %get-tuple-element.35), channel_id=6, replica_groups=mesh['y'=4,'zh'=4,'c'=2,'zl'=4,'x'=4] {'zl'}, dimensions={0}, use_global_device_ids=true | all-gather | bytes 327680 | tf_op jit(solution)/shard_map/products/all_gather | solution.py:35
  158.8 0.0 all-to-all-done.2
  158.8 0.2 broadcast_in_dim.32
  159.0 8.4 %all_to_all.31 = bf16[2,4,4,128,256]{4,3,2,1,0:T(8,128)(2,1)S(1)} all-to-all(bf16[2,4,4,128,256]{4,3,2,1,0:T(8,128)(2,1)S(1)} %broadcast_in_dim.32), channel_id=1, replica_groups=mesh['y'=4,'zh'=4,'c'=2,'zl'=4,'x'=4] {'c'}, dimensions={0} | all-to-all | bytes 4194304 | tf_op jit(solution)/shard_map/grad_rows/all_to_all | solution.py:21
  167.5 0.3 copy.24
  167.7 1.4 weight_b.1
  169.2 0.0 copy-start.5
  169.2 1.0 copy-done.5
  170.2 4.5 %all-to-all-start.4 = ((bf16[4,4,272,128]{3,2,1,0:T(8,128)(2,1)}), bf16[4,4,272,128]{3,2,1,0:T(8,128)(2,1)S(1)}, u32[]{:S(2)}, u32[]{:S(2)}) async-start(bf16[4,4,272,128]{3,2,1,0:T(8,128)(2,1)} %copy-done.5), calls=%async_computation.4 | async-start | bytes 2228224 | tf_op jit(solution)/shard_map/weight_b/all_to_all | solution.py:330
  174.6 0.0 all-gather.14.cloned.1.call-start
  174.6 0.7 all-gather.14.cloned.1.call-update
  175.4 14.5 %all-to-all-done.4.refs_0_ = bf16[4,4,272,128]{3,2,1,0:T(8,128)(2,1)S(1)} async-done(((bf16[4,4,272,128]{3,2,1,0:T(8,128)(2,1)}), bf16[4,4,272,128]{3,2,1,0:T(8,128)(2,1)S(1)}, u32[]{:S(2)}, u32[]{:S(2)}) %all-to-all-start.4) | async-done | bytes 1114144 | tf_op jit(solution)/shard_map/weight_b/all_to_all | solution.py:330
  189.9 0.9 fold.1
  190.7 3.4 %all-to-all-start.5 = ((bf16[4,272,128]{2,1,0:T(8,128)(2,1)}), bf16[4,272,128]{2,1,0:T(8,128)(2,1)S(1)}, u32[]{:S(2)}, u32[]{:S(2)}) async-start(bf16[4,272,128]{2,1,0:T(8,128)(2,1)} %fold.1), calls=%async_computation.5 | async-start | bytes 557056 | tf_op jit(solution)/shard_map/weight_b/all_to_all | solution.py:336
  194.2 14.1 %all-gather.14.cloned.1.call-done = bf16[16,128,256]{2,1,0:T(8,128)(2,1)} async-done(((bf16[4,128,256]{2,1,0:T(8,128)(2,1)}), bf16[16,128,256]{2,1,0:T(8,128)(2,1)}) %all-gather.14.cloned.1.call-update) | async-done | bytes 1048592 | tf_op jit(solution)/shard_map/products/all_gather | solution.py:35
  208.3 1.2 copy-done.6
  209.5 0.4 weight_a.1.side_ref
  209.9 0.0 all-to-all-done.5.got_ref
  210.0 0.8 finish.1
  (9 shorter events, 0.1 us)
Async XLA Ops:
  10.1 53.5 %all-to-all-start = ((bf16[32,3,8,128]{3,2,1,0:T(8,128)(2,1)}), bf16[32,3,8,128]{3,2,1,0:T(8,128)(2,1)S(1)}, u32[]{:S(2)}, u32[]{:S(2)}) async-start(bf16[32,3,8,128]{3,2,1,0:T(8,128)(2,1)} %copy_bitcast_fusion.2), calls=%async_computation | async-start | bytes 393216 | tf_op jit(solution)/shard_map/columns/all_to_all | solution.py:274
  29.5 69.7 %all-gather.10.cloned.1.call-start = ((), (), s32[]{:S(2)}) async-start(), calls=%async_computation.6 | async-start | bytes 2621440 | tf_op jit(solution)/shard_map/rows/all_gather | solution.py:35
  63.7 76.2 %all-gather.12.cloned.1.call-start = ((), (), s32[]{:S(2)}) async-start(), calls=%async_computation.7 | async-start | bytes 2621440 | tf_op jit(solution)/shard_map/columns/all_gather | solution.py:35
  100.1 6.6 %collective-permute-start = (bf16[16,2,128,256]{3,2,1,0:T(8,128)(2,1)}, bf16[16,2,128,256]{3,2,1,0:T(8,128)(2,1)S(1)}, u32[]{:S(2)}, u32[]{:S(2)}) collective-permute-start(bf16[16,2,128,256]{3,2,1,0:T(8,128)(2,1)} %all-gather.10.cloned.1.call-done), channel_id=1, source_target_pairs={{0,16},{16,0},{1,17},{17,1},{2,18},{18,2},{3,19},{19,3},{4,20},{20... | collective-permute-start | bytes 6291464 | tf_op jit(solution)/shard_map/rows/ppermute | solution.py:260
  106.6 1.6 copy-start
  110.1 1.4 copy-start.2
  111.4 28.5 %copy-start.1 = (bf16[16,2,128,256]{3,2,1,0:T(8,128)(2,1)S(1)}, bf16[16,2,128,256]{3,2,1,0:T(8,128)(2,1)}, u32[]{:S(2)}) copy-start(bf16[16,2,128,256]{3,2,1,0:T(8,128)(2,1)} %all-gather.10.cloned.1.call-done) | copy-start | bytes 6291460
  134.2 24.6 %all-to-all-start.2 = ((bf16[4,4,128,256]{3,2,1,0:T(8,128)(2,1)}), bf16[4,4,128,256]{3,2,1,0:T(8,128)(2,1)S(1)}, u32[]{:S(2)}, u32[]{:S(2)}) async-start(bf16[4,4,128,256]{3,2,1,0:T(8,128)(2,1)} %broadcast_in_dim.31), calls=%async_computation.2 | async-start | bytes 2097152 | tf_op jit(solution)/shard_map/grad_rows/all_to_all | solution.py:21
  139.9 1.6 copy-start.3
  141.5 1.6 copy-start.4
  169.2 1.0 copy-start.5
  170.2 19.7 %all-to-all-start.4 = ((bf16[4,4,272,128]{3,2,1,0:T(8,128)(2,1)}), bf16[4,4,272,128]{3,2,1,0:T(8,128)(2,1)S(1)}, u32[]{:S(2)}, u32[]{:S(2)}) async-start(bf16[4,4,272,128]{3,2,1,0:T(8,128)(2,1)} %copy-done.5), calls=%async_computation.4 | async-start | bytes 2228224 | tf_op jit(solution)/shard_map/weight_b/all_to_all | solution.py:330
  174.6 33.6 %all-gather.14.cloned.1.call-start = ((), (), s32[]{:S(2)}) async-start(), calls=%async_computation.8 | async-start | bytes 1310720 | tf_op jit(solution)/shard_map/products/all_gather | solution.py:35
  190.7 19.2 %all-to-all-start.5 = ((bf16[4,272,128]{2,1,0:T(8,128)(2,1)}), bf16[4,272,128]{2,1,0:T(8,128)(2,1)S(1)}, u32[]{:S(2)}, u32[]{:S(2)}) async-start(bf16[4,272,128]{2,1,0:T(8,128)(2,1)} %fold.1), calls=%async_computation.5 | async-start | bytes 557056 | tf_op jit(solution)/shard_map/weight_b/all_to_all | solution.py:336
  208.3 1.2 copy-start.6
Sparse Core Ops, SparseCore 0:
  63.8 35.3 all-gather.9
  101.3 38.5 all-gather.11
  177.6 30.6 all-gather.13

commit v6 on v5

--- a/solution.py
+++ b/solution.py
@@ -114,11 +114,11 @@
     grad_ref[...] = jnp.where(diagonal, -2.0 * (1.0 - corr), 2.0 * off_weight * corr).astype(bf16)
 
 
-def product_kernel(cols_ref, own_ref, other_ref, stats_ref, aa_ref, bb_ref, ab_ref, ba_ref, inverse_ref):
+def product_kernel(cols_ref, own_ref, other_ref, stats_ref, plain_ref, ab_ref, ba_ref, inverse_ref):
     pairs = cols_ref.shape[3]
     halves = (own_ref, other_ref)
     count, part = cols_ref.shape[0], cols_ref.shape[2]
-    owned, width = 2 * aa_ref.shape[0], aa_ref.shape[1]
+    owned, width = 2 * ab_ref.shape[0], ab_ref.shape[1]
     mean_a, inverse_a = stats_ref[0:1, :], stats_ref[8:9, :]
     mean_b, inverse_b = column_stats(halves, 1, pairs)
     inverse_ref[...] = jnp.broadcast_to(inverse_b, (8, width))
@@ -133,26 +133,28 @@
         sum_a, sum_b = sum_a + fold(a.astype(f32)), sum_b + fold(b.astype(f32))
         sum_h = sum_h + lanes(h.astype(f32))
     sum_h = jnp.sum(sum_h, 1, keepdims=True)
-    for side, prod, sums, plain_ref, centered_ref in (
-        (0, prod_a, sum_a, aa_ref, ba_ref),
-        (1, prod_b, sum_b, bb_ref, ab_ref),
+    for side, prod, sums, centered_ref in (
+        (0, prod_a, sum_a, ba_ref),
+        (1, prod_b, sum_b, ab_ref),
     ):
         centered = prod - sum_h * (jnp.sum(sums, 0, keepdims=True) / pairs)
         for x in range(count):
             block = lambda v, view: v[(2 * x + view) * part : (2 * x + view + 1) * part]
-            plain_ref[x * part : (x + 1) * part, :] = block(prod, side)
+            plain_ref[side, x * part : (x + 1) * part, :] = block(prod, side)
             centered_ref[x * part : (x + 1) * part, :] = block(centered, 1 - side).astype(bf16)
 
 
-def weight_a_kernel(pairs, blocks_ref, grads_ref, aa_ref, bb_ref, stats_ref, inverse_ref, second_ref, out_ref):
-    owned, width = aa_ref.shape
+def weight_a_kernel(pairs, x_ref, *refs):
+    blocks, (grads_ref, plain_ref, stats_ref, inverse_ref, second_ref, out_ref) = refs[:-6], refs[-6:]
+    _, owned, width = plain_ref.shape
     total = jnp.zeros((owned, width), f32)
-    for x in range(blocks_ref.shape[0]):
-        for zl in range(blocks_ref.shape[1]):
-            total = total + matmul(blocks_ref[x, zl], grads_ref[x, zl])
+    for r, block in enumerate(blocks):
+        x = lax.rem(x_ref[0] - r + len(blocks), len(blocks))
+        for zl in range(block.shape[0]):
+            total = total + matmul(block[zl], grads_ref[x, zl])
     inv_b = inverse_ref[0:1, :]
-    out_ref[0:owned, :] = stats_ref[8:9, :] * (total - pairs * aa_ref[...] * second_ref[...])
-    out_ref[owned : 2 * owned, :] = inv_b * pairs * bb_ref[...]
+    out_ref[0:owned, :] = stats_ref[8:9, :] * (total - pairs * plain_ref[0] * second_ref[...])
+    out_ref[owned : 2 * owned, :] = inv_b * pairs * plain_ref[1]
     out_ref[2 * owned :, :] = jnp.broadcast_to(inv_b, (8, width))
 
 
@@ -255,6 +257,7 @@
     together = lax.optimization_barrier
 
     core = lax.axis_index("c")
+    x_index = lax.axis_index("x").astype(jnp.int32)[None]
 
     def swap(v):
         return lax.ppermute(v, "c", [(0, 1), (1, 0)])
@@ -306,16 +309,12 @@
     with jax.named_scope("grad_rows"):
         grads = gather(grads, "y")
     with jax.named_scope("products"):
-        p_aa, p_bb, p_ab, p_ba, inverse_b = call(
+        plain, p_ab, p_ba, inverse_b = call(
             product_kernel, "products", 8 * pairs * owned * width,
-            (shape((owned, width), f32),) * 2 + (shape((owned, width), bf16),) * 2 + (shape((8, width), f32),),
+            (shape((2, owned, width), f32),) + (shape((owned, width), bf16),) * 2 + (shape((8, width), f32),),
             cols_h, own, other, stats_a,
         )
-        p_ab = collect(p_ab, "zl")
     grads, p_ab, p_ba = together((grads, p_ab, p_ba))
-    with jax.named_scope("products"):
-        p_ab = collect(p_ab, "x")
-
     with jax.named_scope("grad_rows"):
         grads = gather(grads, "c")
         grads = grads.reshape(n_c, n_y, n_zh, n_x, n_zl, sub, width)
@@ -327,19 +326,24 @@
             (shape((n_x, n_zl, width + 16, owned), bf16), shape((1, width), f32)),
             block, grads, p_ba, scalars=1,
         )
+        got, p_ab = together((got, p_ab))
         got = lax.all_to_all(got, "x", 0, 0, tiled=True)
+        p_ab = collect(p_ab, "zl")
+        got, p_ab = together((got, p_ab))
         rows_out = got.shape[2]
         got = call(
             lambda *refs: fold_kernel(width, *refs), "fold", 0,
             shape((n_zl, rows_out, owned), bf16), got,
         )
         got = lax.all_to_all(got, "zl", 0, 0, tiled=True)
+        turn = lambda r: [(i, (i + r) % n_x) for i in range(n_x)]
+        p_ab = [p_ab] + [lax.ppermute(p_ab, "x", turn(r)) for r in range(1, n_x)]
 
     with jax.named_scope("weight_a"):
         side = call(
             lambda *refs: weight_a_kernel(pairs, *refs), "weight_a", 2 * owned * n_feat * width * width,
             shape((2 * owned + 8, width), f32),
-            p_ab, grads, p_aa, p_bb, stats_a, inverse_b, second_a,
+            x_index, *p_ab, grads, plain, stats_a, inverse_b, second_a, scalars=1,
         )
 
     with jax.named_scope("finish"):

time: 218 us -> 217 us (level)
  waiting for transfers between devices: 43 us -> 26.7 us
  starting transfers between devices: 33.5 us -> 42.8 us
  local copies, waits for them, and re-layouts: 12.6 us -> 15 us
    all_gather x3 -> x2, waiting for transfers between devices: 23.8 us -> 9.65 us  [collect(): return lax.all_gather(block, axis, axis=0, tiled=False)]
    all_to_all x1, waiting for transfers between devices: 14.5 us -> 2.14 us  [body(): got = lax.all_to_all(got, 'x', 0, 0, tiled=True)]
    ppermute x0 -> x3, waiting for transfers between devices: none -> 8.83 us  [body(): p_ab = [p_ab] + [lax.ppermute(p_ab, 'x', turn(r)) for r in range(1, n_x)]]
    ppermute x0 -> x3, starting transfers between devices: none -> 8.4 us  [body(): p_ab = [p_ab] + [lax.ppermute(p_ab, 'x', turn(r)) for r in range(1, n_x)]]
    unnamed x14 -> x24, local copies, waits for them, and re-layouts: 8.35 us -> 10.7 us
  transfers between devices with their start and end apart: 8 -> 10, of which waited for: 5 -> 8; matrix products, arithmetic and copies ran while one was open for 1% -> 1% of each run, Pallas kernels for 3% -> 2%
where the time goes in v6:
time: 217 us; the launch traced here: 215 us
  blocking collectives  107 us (49%)
  starting transfers between devices  42.8 us (20%)
  waiting for transfers between devices  26.7 us (12%)
  local copies, waits for them, and re-layouts  15 us (7%)
  between operations  13.6 us (6%)
  Pallas kernels  9.84 us (5%)
    all_gather x4, blocking collectives, collect(): return lax.all_gather(block, axis, axis=0, tiled=False)  83 us
    all_to_all x2, blocking collectives, gather(): return lax.all_to_all(copies, axis, 0, 0, tiled=True)  23.9 us
    all_to_all x1, starting transfers between devices, body(): cut = lax.all_to_all(cut, DP, 0, 0, tiled=True)  19.4 us
    unnamed x24, local copies, waits for them, and re-layouts  10.7 us
    pallas_call x7, Pallas kernels, call(): pl.pallas_call(kernel, out_shape=shapes, scratch_shapes=list(scratch), in...  9.84 us
    all_gather x2, waiting for transfers between devices, collect(): return lax.all_gather(block, axis, axis=0, tiled=False)  9.65 us
    ppermute x3, waiting for transfers between devices, body(): p_ab = [p_ab] + [lax.ppermute(p_ab, 'x', turn(r)) for r in range(1, n_x)]  8.83 us
    ppermute x3, starting transfers between devices, body(): p_ab = [p_ab] + [lax.ppermute(p_ab, 'x', turn(r)) for r in range(1, n_x)]  8.4 us
  transfers between devices with their start and end apart: 10, of which 8 were waited for; matrix products, arithmetic and copies ran while one was open for 1% of the time, Pallas kernels for 2%

profile of v6, /device:TPU:1, one launch (start us, length us, event | category | flops | bytes accessed | tf_op | source)
XLA Modules:
  0.0 214.9 jit_solution(1322724877052056635)
XLA Ops:
  6.5 1.9 open.1
  8.4 1.6 copy_bitcast_fusion.2
  10.1 19.4 %all-to-all-start = ((bf16[32,3,8,128]{3,2,1,0:T(8,128)(2,1)}), bf16[32,3,8,128]{3,2,1,0:T(8,128)(2,1)S(1)}, u32[]{:S(2)}, u32[]{:S(2)}) async-start(bf16[32,3,8,128]{3,2,1,0:T(8,128)(2,1)} %copy_bitcast_fusion.2), calls=%async_computation | async-start | bytes 393216 | tf_op jit(solution)/shard_map/columns/all_to_all | solution.py:277
  29.5 0.0 all-gather.8.cloned.1.call-start
  29.5 34.1 %all-gather = bf16[8,128,256]{2,1,0:T(8,128)(2,1)} all-gather(bf16[2,128,256]{2,1,0:T(8,128)(2,1)} %get-tuple-element.29), channel_id=2, replica_groups=mesh['y'=4,'zh'=4,'c'=2,'zl'=4,'x'=4] {'zh'}, dimensions={0}, use_global_device_ids=true | all-gather | bytes 655360 | tf_op jit(solution)/shard_map/rows/all_gather | solution.py:35
  63.6 0.0 all-gather.10.cloned.1.call-start
  63.8 14.1 %all_gather.37 = bf16[4,3,8,4096]{3,2,1,0:T(8,128)(2,1)S(1)} all-gather(bf16[1,3,8,4096]{3,2,1,0:T(8,128)(2,1)S(1)} %bitcast.45), channel_id=1, replica_groups=mesh['y'=4,'zh'=4,'c'=2,'zl'=4,'x'=4] {'zl'}, dimensions={0}, use_global_device_ids=true | all-gather | bytes 983040 | tf_op jit(solution)/shard_map/columns/all_gather | solution.py:35
  77.9 0.1 copy.29
  77.9 0.1 broadcast_in_dim.33
  78.0 13.6 %all_to_all.30.cols_ref = bf16[4,1,32,4096]{3,2,1,0:T(8,128)(2,1)S(1)} all-to-all(bf16[4,1,32,4096]{3,2,1,0:T(8,128)(2,1)S(1)} %broadcast_in_dim.33), channel_id=1, replica_groups=mesh['y'=4,'zh'=4,'c'=2,'zl'=4,'x'=4] {'x'}, dimensions={0} | all-to-all | bytes 2097152 | tf_op jit(solution)/shard_map/columns/all_to_all | solution.py:21
  91.7 7.5 %all-gather.8.cloned.1.call-done = bf16[16,2,128,256]{3,2,1,0:T(8,128)(2,1)} async-done(((bf16[4,2,128,256]{3,2,1,0:T(8,128)(2,1)}), bf16[16,2,128,256]{3,2,1,0:T(8,128)(2,1)}) %all-gather.8.cloned.1.call-update) | async-done | bytes 2097168 | tf_op jit(solution)/shard_map/rows/all_gather | solution.py:35
  99.2 0.9 slice.8
  100.1 2.6 %collective-permute-start = (bf16[16,2,128,256]{3,2,1,0:T(8,128)(2,1)}, bf16[16,2,128,256]{3,2,1,0:T(8,128)(2,1)S(1)}, u32[]{:S(2)}, u32[]{:S(2)}) collective-permute-start(bf16[16,2,128,256]{3,2,1,0:T(8,128)(2,1)} %all-gather.8.cloned.1.call-done), channel_id=1, source_target_pairs={{0,16},{16,0},{1,17},{17,1},{2,18},{18,2},{3,19},{19,3},{4,20},{20... | collective-permute-start | bytes 6291464 | tf_op jit(solution)/shard_map/rows/ppermute | solution.py:263
  102.7 3.9 %collective-permute-done.other_ref = bf16[16,2,128,256]{3,2,1,0:T(8,128)(2,1)S(1)} collective-permute-done((bf16[16,2,128,256]{3,2,1,0:T(8,128)(2,1)}, bf16[16,2,128,256]{3,2,1,0:T(8,128)(2,1)S(1)}, u32[]{:S(2)}, u32[]{:S(2)}) %collective-permute-start) | collective-permute-done | bytes 2097184 | tf_op jit(solution)/shard_map/rows/ppermute | solution.py:263
  106.6 1.6 copy-done
  108.2 1.8 grad_block.1
  110.1 1.4 copy-done.2
  111.4 21.7 %all-gather.2 = bf16[512,256]{1,0:T(8,128)(2,1)S(1)} all-gather(bf16[128,256]{1,0:T(8,128)(2,1)S(1)} %get-tuple-element.34), channel_id=4, replica_groups=mesh['y'=4,'zh'=4,'c'=2,'zl'=4,'x'=4] {'zh'}, dimensions={0}, use_global_device_ids=true | all-gather | bytes 327680 | tf_op jit(solution)/shard_map/grad_rows/all_gather | solution.py:35
  133.2 1.1 broadcast_in_dim.34
  134.2 3.5 %all-to-all-start.2 = ((bf16[4,4,128,256]{3,2,1,0:T(8,128)(2,1)}), bf16[4,4,128,256]{3,2,1,0:T(8,128)(2,1)S(1)}, u32[]{:S(2)}, u32[]{:S(2)}) async-start(bf16[4,4,128,256]{3,2,1,0:T(8,128)(2,1)} %broadcast_in_dim.34), calls=%async_computation.2 | async-start | bytes 2097152 | tf_op jit(solution)/shard_map/grad_rows/all_to_all | solution.py:21
  137.8 2.1 all-gather.10.cloned.1.call-done
  139.9 1.6 copy-done.3
  141.5 1.6 copy-done.4
  143.1 2.6 %products.1 = (f32[2,128,256]{2,1,0:T(8,128)S(1)}, bf16[128,256]{1,0:T(8,128)(2,1)S(1)}, bf16[128,256]{1,0:T(8,128)(2,1)S(1)}, f32[8,256]{1,0:T(8,128)S(1)}) custom-call(bf16[4,2,32,4096]{3,2,1,0:T(8,128)(2,1)S(1)} %bitcast.34, bf16[16,2,128,256]{3,2,1,0:T(8,128)(2,1)S(1)} %copy-done.1, bf16[16,2,128,256]{3,2,1,0:T(8,128)(2,1)S(1)} %copy-done.3, ...), custom_call_target="tpu_custom_call" | custom-call | flops 1073741824 | bytes 6709248 | tf_op jit(solution)/shard_map/products/products/pallas_call | solution.py:232
  145.7 0.7 copy-done.6
  146.4 2.1 all-to-all-done.2
  148.5 0.2 broadcast_in_dim.35
  148.8 10.3 %all_to_all.31 = bf16[2,4,4,128,256]{4,3,2,1,0:T(8,128)(2,1)S(1)} all-to-all(bf16[2,4,4,128,256]{4,3,2,1,0:T(8,128)(2,1)S(1)} %broadcast_in_dim.35), channel_id=1, replica_groups=mesh['y'=4,'zh'=4,'c'=2,'zl'=4,'x'=4] {'c'}, dimensions={0} | all-to-all | bytes 4194304 | tf_op jit(solution)/shard_map/grad_rows/all_to_all | solution.py:21
  159.1 0.3 copy.24
  159.3 1.4 weight_b.1
  160.8 1.0 copy-done.5
  161.7 0.6 copy-done.10
  162.3 4.0 %all-to-all-start.4 = ((bf16[4,4,272,128]{3,2,1,0:T(8,128)(2,1)}), bf16[4,4,272,128]{3,2,1,0:T(8,128)(2,1)S(1)}, u32[]{:S(2)}, u32[]{:S(2)}) async-start(bf16[4,4,272,128]{3,2,1,0:T(8,128)(2,1)} %copy-done.5), calls=%async_computation.4 | async-start | bytes 2228224 | tf_op jit(solution)/shard_map/weight_b/all_to_all | solution.py:330
  166.3 13.1 %all-gather.4 = bf16[512,256]{1,0:T(8,128)(2,1)S(1)} all-gather(bf16[128,256]{1,0:T(8,128)(2,1)S(1)} %get-tuple-element.45), channel_id=6, replica_groups=mesh['y'=4,'zh'=4,'c'=2,'zl'=4,'x'=4] {'zl'}, dimensions={0}, use_global_device_ids=true | all-gather | bytes 327680 | tf_op jit(solution)/shard_map/weight_b/all_gather | solution.py:35
  179.4 2.1 all-to-all-done.4.refs_0_
  181.5 0.9 fold.1
  182.4 4.9 %all-to-all-start.5 = ((bf16[4,272,128]{2,1,0:T(8,128)(2,1)}), bf16[4,272,128]{2,1,0:T(8,128)(2,1)S(1)}, u32[]{:S(2)}, u32[]{:S(2)}) async-start(bf16[4,272,128]{2,1,0:T(8,128)(2,1)} %fold.1), calls=%async_computation.5 | async-start | bytes 557056 | tf_op jit(solution)/shard_map/weight_b/all_to_all | solution.py:338
  187.2 2.2 %collective-permute-start.1 = (bf16[4,128,256]{2,1,0:T(8,128)(2,1)S(1)}, bf16[4,128,256]{2,1,0:T(8,128)(2,1)S(1)}, u32[]{:S(2)}, u32[]{:S(2)}) collective-permute-start(bf16[4,128,256]{2,1,0:T(8,128)(2,1)S(1)} %bitcast.35), channel_id=1, source_target_pairs={{0,1},{1,2},{2,3},{3,0},{4,5},{5,6},{6,7},{7,4},{8,9},{9,10},{10,1... | collective-permute-start | bytes 786440 | tf_op jit(solution)/shard_map/weight_b/ppermute | solution.py:340
  189.4 3.7 %collective-permute-start.2 = (bf16[4,128,256]{2,1,0:T(8,128)(2,1)S(1)}, bf16[4,128,256]{2,1,0:T(8,128)(2,1)S(1)}, u32[]{:S(2)}, u32[]{:S(2)}) collective-permute-start(bf16[4,128,256]{2,1,0:T(8,128)(2,1)S(1)} %bitcast.36), channel_id=1, source_target_pairs={{0,2},{1,3},{2,0},{3,1},{4,6},{5,7},{6,4},{7,5},{8,10},{9,11},{10,... | collective-permute-start | bytes 786440 | tf_op jit(solution)/shard_map/weight_b/ppermute | solution.py:340
  193.1 2.5 %collective-permute-start.3 = (bf16[4,128,256]{2,1,0:T(8,128)(2,1)S(1)}, bf16[4,128,256]{2,1,0:T(8,128)(2,1)S(1)}, u32[]{:S(2)}, u32[]{:S(2)}) collective-permute-start(bf16[4,128,256]{2,1,0:T(8,128)(2,1)S(1)} %bitcast.37), channel_id=1, source_target_pairs={{0,3},{1,0},{2,1},{3,2},{4,7},{5,4},{6,5},{7,6},{8,11},{9,8},{10,9... | collective-permute-start | bytes 786440 | tf_op jit(solution)/shard_map/weight_b/ppermute | solution.py:340
  195.6 1.4 collective-permute-done.1.refs_2_
  197.1 4.1 %collective-permute-done.2.refs_3_ = bf16[4,128,256]{2,1,0:T(8,128)(2,1)S(1)} collective-permute-done((bf16[4,128,256]{2,1,0:T(8,128)(2,1)S(1)}, bf16[4,128,256]{2,1,0:T(8,128)(2,1)S(1)}, u32[]{:S(2)}, u32[]{:S(2)}) %collective-permute-start.2) | collective-permute-done | bytes 262176 | tf_op jit(solution)/shard_map/weight_b/ppermute | solution.py:340
  201.1 3.3 %collective-permute-done.3.refs_4_ = bf16[4,128,256]{2,1,0:T(8,128)(2,1)S(1)} collective-permute-done((bf16[4,128,256]{2,1,0:T(8,128)(2,1)S(1)}, bf16[4,128,256]{2,1,0:T(8,128)(2,1)S(1)}, u32[]{:S(2)}, u32[]{:S(2)}) %collective-permute-start.3) | collective-permute-done | bytes 262176 | tf_op jit(solution)/shard_map/weight_b/ppermute | solution.py:340
  204.5 0.9 copy-done.7
  205.4 0.7 copy-done.9
  206.1 0.7 copy-done.11
  206.8 0.4 weight_a.1.side_ref
  207.3 0.8 finish.1
  (22 shorter events, 0.2 us)
Async XLA Ops:
  10.1 53.5 %all-to-all-start = ((bf16[32,3,8,128]{3,2,1,0:T(8,128)(2,1)}), bf16[32,3,8,128]{3,2,1,0:T(8,128)(2,1)S(1)}, u32[]{:S(2)}, u32[]{:S(2)}) async-start(bf16[32,3,8,128]{3,2,1,0:T(8,128)(2,1)} %copy_bitcast_fusion.2), calls=%async_computation | async-start | bytes 393216 | tf_op jit(solution)/shard_map/columns/all_to_all | solution.py:277
  29.5 69.7 %all-gather.8.cloned.1.call-start = ((), (), s32[]{:S(2)}) async-start(), calls=%async_computation.6 | async-start | bytes 2621440 | tf_op jit(solution)/shard_map/rows/all_gather | solution.py:35
  63.6 76.2 %all-gather.10.cloned.1.call-start = ((), (), s32[]{:S(2)}) async-start(), calls=%async_computation.7 | async-start | bytes 2621440 | tf_op jit(solution)/shard_map/columns/all_gather | solution.py:35
  100.1 6.6 %collective-permute-start = (bf16[16,2,128,256]{3,2,1,0:T(8,128)(2,1)}, bf16[16,2,128,256]{3,2,1,0:T(8,128)(2,1)S(1)}, u32[]{:S(2)}, u32[]{:S(2)}) collective-permute-start(bf16[16,2,128,256]{3,2,1,0:T(8,128)(2,1)} %all-gather.8.cloned.1.call-done), channel_id=1, source_target_pairs={{0,16},{16,0},{1,17},{17,1},{2,18},{18,2},{3,19},{19,3},{4,20},{20... | collective-permute-start | bytes 6291464 | tf_op jit(solution)/shard_map/rows/ppermute | solution.py:263
  106.6 1.6 copy-start
  110.1 1.4 copy-start.2
  111.4 28.4 %copy-start.1 = (bf16[16,2,128,256]{3,2,1,0:T(8,128)(2,1)S(1)}, bf16[16,2,128,256]{3,2,1,0:T(8,128)(2,1)}, u32[]{:S(2)}) copy-start(bf16[16,2,128,256]{3,2,1,0:T(8,128)(2,1)} %all-gather.8.cloned.1.call-done) | copy-start | bytes 6291460
  134.2 14.3 %all-to-all-start.2 = ((bf16[4,4,128,256]{3,2,1,0:T(8,128)(2,1)}), bf16[4,4,128,256]{3,2,1,0:T(8,128)(2,1)S(1)}, u32[]{:S(2)}, u32[]{:S(2)}) async-start(bf16[4,4,128,256]{3,2,1,0:T(8,128)(2,1)} %broadcast_in_dim.34), calls=%async_computation.2 | async-start | bytes 2097152 | tf_op jit(solution)/shard_map/grad_rows/all_to_all | solution.py:21
  139.9 1.6 copy-start.3
  141.5 1.6 copy-start.4
  145.7 0.7 copy-start.6
  146.4 12.6 %copy-start.8 = (f32[8,256]{1,0:T(8,128)}, f32[8,256]{1,0:T(8,128)S(1)}, u32[]{:S(2)}) copy-start(f32[8,256]{1,0:T(8,128)S(1)} %get-tuple-element.49.refs_8_) | copy-start | bytes 24580
  160.7 1.0 copy-start.5
  161.7 0.6 copy-start.10
  162.3 19.2 %all-to-all-start.4 = ((bf16[4,4,272,128]{3,2,1,0:T(8,128)(2,1)}), bf16[4,4,272,128]{3,2,1,0:T(8,128)(2,1)S(1)}, u32[]{:S(2)}, u32[]{:S(2)}) async-start(bf16[4,4,272,128]{3,2,1,0:T(8,128)(2,1)} %copy-done.5), calls=%async_computation.4 | async-start | bytes 2228224 | tf_op jit(solution)/shard_map/weight_b/all_to_all | solution.py:330
  182.4 24.9 %all-to-all-start.5 = ((bf16[4,272,128]{2,1,0:T(8,128)(2,1)}), bf16[4,272,128]{2,1,0:T(8,128)(2,1)S(1)}, u32[]{:S(2)}, u32[]{:S(2)}) async-start(bf16[4,272,128]{2,1,0:T(8,128)(2,1)} %fold.1), calls=%async_computation.5 | async-start | bytes 557056 | tf_op jit(solution)/shard_map/weight_b/all_to_all | solution.py:338
  187.2 9.9 %collective-permute-start.1 = (bf16[4,128,256]{2,1,0:T(8,128)(2,1)S(1)}, bf16[4,128,256]{2,1,0:T(8,128)(2,1)S(1)}, u32[]{:S(2)}, u32[]{:S(2)}) collective-permute-start(bf16[4,128,256]{2,1,0:T(8,128)(2,1)S(1)} %bitcast.35), channel_id=1, source_target_pairs={{0,1},{1,2},{2,3},{3,0},{4,5},{5,6},{6,7},{7,4},{8,9},{9,10},{10,1... | collective-permute-start | bytes 786440 | tf_op jit(solution)/shard_map/weight_b/ppermute | solution.py:340
  189.4 11.7 %collective-permute-start.2 = (bf16[4,128,256]{2,1,0:T(8,128)(2,1)S(1)}, bf16[4,128,256]{2,1,0:T(8,128)(2,1)S(1)}, u32[]{:S(2)}, u32[]{:S(2)}) collective-permute-start(bf16[4,128,256]{2,1,0:T(8,128)(2,1)S(1)} %bitcast.36), channel_id=1, source_target_pairs={{0,2},{1,3},{2,0},{3,1},{4,6},{5,7},{6,4},{7,5},{8,10},{9,11},{10,... | collective-permute-start | bytes 786440 | tf_op jit(solution)/shard_map/weight_b/ppermute | solution.py:340
  193.1 11.4 %collective-permute-start.3 = (bf16[4,128,256]{2,1,0:T(8,128)(2,1)S(1)}, bf16[4,128,256]{2,1,0:T(8,128)(2,1)S(1)}, u32[]{:S(2)}, u32[]{:S(2)}) collective-permute-start(bf16[4,128,256]{2,1,0:T(8,128)(2,1)S(1)} %bitcast.37), channel_id=1, source_target_pairs={{0,3},{1,0},{2,1},{3,2},{4,7},{5,4},{6,5},{7,6},{8,11},{9,8},{10,9... | collective-permute-start | bytes 786440 | tf_op jit(solution)/shard_map/weight_b/ppermute | solution.py:340
  204.5 0.9 copy-start.7
  205.4 0.7 copy-start.9
  206.1 0.7 copy-start.11
Sparse Core Ops, SparseCore 0:
  63.8 35.3 all-gather.7
  101.3 38.5 all-gather.9

commit v7 on v6

--- a/solution.py
+++ b/solution.py
@@ -121,7 +121,8 @@
     owned, width = 2 * ab_ref.shape[0], ab_ref.shape[1]
     mean_a, inverse_a = stats_ref[0:1, :], stats_ref[8:9, :]
     mean_b, inverse_b = column_stats(halves, 1, pairs)
-    inverse_ref[...] = jnp.broadcast_to(inverse_b, (8, width))
+    inverse_ref[0:8, :] = jnp.broadcast_to(inverse_a, (8, width))
+    inverse_ref[8:16, :] = jnp.broadcast_to(inverse_b, (8, width))
     prod_a = prod_b = jnp.zeros((owned, width), f32)
     sum_a = sum_b = jnp.zeros((8, width), f32)
     sum_h = jnp.zeros((owned, 128), f32)
@@ -145,15 +146,15 @@
 
 
 def weight_a_kernel(pairs, x_ref, *refs):
-    blocks, (grads_ref, plain_ref, stats_ref, inverse_ref, second_ref, out_ref) = refs[:-6], refs[-6:]
+    blocks, (grads_ref, plain_ref, inverse_ref, second_ref, out_ref) = refs[:-5], refs[-5:]
     _, owned, width = plain_ref.shape
     total = jnp.zeros((owned, width), f32)
     for r, block in enumerate(blocks):
         x = lax.rem(x_ref[0] - r + len(blocks), len(blocks))
         for zl in range(block.shape[0]):
             total = total + matmul(block[zl], grads_ref[x, zl])
-    inv_b = inverse_ref[0:1, :]
-    out_ref[0:owned, :] = stats_ref[8:9, :] * (total - pairs * plain_ref[0] * second_ref[...])
+    inv_b = inverse_ref[8:9, :]
+    out_ref[0:owned, :] = inverse_ref[0:1, :] * (total - pairs * plain_ref[0] * second_ref[...])
     out_ref[owned : 2 * owned, :] = inv_b * pairs * plain_ref[1]
     out_ref[2 * owned :, :] = jnp.broadcast_to(inv_b, (8, width))
 
@@ -309,9 +310,9 @@
     with jax.named_scope("grad_rows"):
         grads = gather(grads, "y")
     with jax.named_scope("products"):
-        plain, p_ab, p_ba, inverse_b = call(
+        plain, p_ab, p_ba, inverse = call(
             product_kernel, "products", 8 * pairs * owned * width,
-            (shape((2, owned, width), f32),) + (shape((owned, width), bf16),) * 2 + (shape((8, width), f32),),
+            (shape((2, owned, width), f32),) + (shape((owned, width), bf16),) * 2 + (shape((16, width), f32),),
             cols_h, own, other, stats_a,
         )
     grads, p_ab, p_ba = together((grads, p_ab, p_ba))
@@ -343,7 +344,7 @@
         side = call(
             lambda *refs: weight_a_kernel(pairs, *refs), "weight_a", 2 * owned * n_feat * width * width,
             shape((2 * owned + 8, width), f32),
-            x_index, *p_ab, grads, plain, stats_a, inverse_b, second_a, scalars=1,
+            x_index, *p_ab, grads, plain, inverse, second_a, scalars=1,
         )
 
     with jax.named_scope("finish"):

time: 217 us -> 218 us (level)
    unnamed x24 -> x20, local copies, waits for them, and re-layouts: 10.7 us -> 10 us
where the time goes in v7:
time: 218 us; the launch traced here: 216 us
  blocking collectives  107 us (49%)
  starting transfers between devices  43.5 us (20%)
  waiting for transfers between devices  26.8 us (12%)
  local copies, waits for them, and re-layouts  15.7 us (7%)
  between operations  13.6 us (6%)
  Pallas kernels  9.84 us (5%)
    all_gather x4, blocking collectives, collect(): return lax.all_gather(block, axis, axis=0, tiled=False)  83 us
    all_to_all x2, blocking collectives, gather(): return lax.all_to_all(copies, axis, 0, 0, tiled=True)  23.9 us
    all_to_all x1, starting transfers between devices, body(): cut = lax.all_to_all(cut, DP, 0, 0, tiled=True)  19.4 us
    unnamed x20, local copies, waits for them, and re-layouts  10 us
    pallas_call x7, Pallas kernels, call(): pl.pallas_call(kernel, out_shape=shapes, scratch_shapes=list(scratch), in...  9.84 us
    ppermute x3, waiting for transfers between devices, body(): p_ab = [p_ab] + [lax.ppermute(p_ab, 'x', turn(r)) for r in range(1, n_x)]  8.83 us
    all_gather x2, waiting for transfers between devices, collect(): return lax.all_gather(block, axis, axis=0, tiled=False)  8.75 us
    ppermute x3, starting transfers between devices, body(): p_ab = [p_ab] + [lax.ppermute(p_ab, 'x', turn(r)) for r in range(1, n_x)]  8.4 us
  transfers between devices with their start and end apart: 10, of which 8 were waited for; matrix products, arithmetic and copies ran while one was open for 1% of the time, Pallas kernels for 2%

profile of v7, /device:TPU:1, one launch (start us, length us, event | category | flops | bytes accessed | tf_op | source)
XLA Modules:
  0.0 216.4 jit_solution(10293988487551627287)
XLA Ops:
  6.5 1.9 open.1
  8.4 1.6 copy_bitcast_fusion.2
  10.1 19.4 %all-to-all-start = ((bf16[32,3,8,128]{3,2,1,0:T(8,128)(2,1)}), bf16[32,3,8,128]{3,2,1,0:T(8,128)(2,1)S(1)}, u32[]{:S(2)}, u32[]{:S(2)}) async-start(bf16[32,3,8,128]{3,2,1,0:T(8,128)(2,1)} %copy_bitcast_fusion.2), calls=%async_computation | async-start | bytes 393216 | tf_op jit(solution)/shard_map/columns/all_to_all | solution.py:278
  29.5 0.0 all-gather.8.cloned.1.call-start
  29.5 34.1 %all-gather = bf16[8,128,256]{2,1,0:T(8,128)(2,1)} all-gather(bf16[2,128,256]{2,1,0:T(8,128)(2,1)} %get-tuple-element.29), channel_id=2, replica_groups=mesh['y'=4,'zh'=4,'c'=2,'zl'=4,'x'=4] {'zh'}, dimensions={0}, use_global_device_ids=true | all-gather | bytes 655360 | tf_op jit(solution)/shard_map/rows/all_gather | solution.py:35
  63.6 0.0 all-gather.8.cloned.1.call-update
  63.6 0.0 all-gather.10.cloned.1.call-start
  63.8 14.1 %all_gather.37 = bf16[4,3,8,4096]{3,2,1,0:T(8,128)(2,1)S(1)} all-gather(bf16[1,3,8,4096]{3,2,1,0:T(8,128)(2,1)S(1)} %bitcast.45), channel_id=1, replica_groups=mesh['y'=4,'zh'=4,'c'=2,'zl'=4,'x'=4] {'zl'}, dimensions={0}, use_global_device_ids=true | all-gather | bytes 983040 | tf_op jit(solution)/shard_map/columns/all_gather | solution.py:35
  77.9 0.1 copy.29
  77.9 0.1 broadcast_in_dim.33
  78.0 13.6 %all_to_all.30.cols_ref = bf16[4,1,32,4096]{3,2,1,0:T(8,128)(2,1)S(1)} all-to-all(bf16[4,1,32,4096]{3,2,1,0:T(8,128)(2,1)S(1)} %broadcast_in_dim.33), channel_id=1, replica_groups=mesh['y'=4,'zh'=4,'c'=2,'zl'=4,'x'=4] {'x'}, dimensions={0} | all-to-all | bytes 2097152 | tf_op jit(solution)/shard_map/columns/all_to_all | solution.py:21
  91.6 7.5 %all-gather.8.cloned.1.call-done = bf16[16,2,128,256]{3,2,1,0:T(8,128)(2,1)} async-done(((bf16[4,2,128,256]{3,2,1,0:T(8,128)(2,1)}), bf16[16,2,128,256]{3,2,1,0:T(8,128)(2,1)}) %all-gather.8.cloned.1.call-update) | async-done | bytes 2097168 | tf_op jit(solution)/shard_map/rows/all_gather | solution.py:35
  99.2 0.9 slice.8
  100.1 2.6 %collective-permute-start = (bf16[16,2,128,256]{3,2,1,0:T(8,128)(2,1)}, bf16[16,2,128,256]{3,2,1,0:T(8,128)(2,1)S(1)}, u32[]{:S(2)}, u32[]{:S(2)}) collective-permute-start(bf16[16,2,128,256]{3,2,1,0:T(8,128)(2,1)} %all-gather.8.cloned.1.call-done), channel_id=1, source_target_pairs={{0,16},{16,0},{1,17},{17,1},{2,18},{18,2},{3,19},{19,3},{4,20},{20... | collective-permute-start | bytes 6291464 | tf_op jit(solution)/shard_map/rows/ppermute | solution.py:264
  102.8 3.9 %collective-permute-done.other_ref = bf16[16,2,128,256]{3,2,1,0:T(8,128)(2,1)S(1)} collective-permute-done((bf16[16,2,128,256]{3,2,1,0:T(8,128)(2,1)}, bf16[16,2,128,256]{3,2,1,0:T(8,128)(2,1)S(1)}, u32[]{:S(2)}, u32[]{:S(2)}) %collective-permute-start) | collective-permute-done | bytes 2097184 | tf_op jit(solution)/shard_map/rows/ppermute | solution.py:264
  106.7 1.6 copy-done
  108.3 1.8 grad_block.1
  110.1 1.4 copy-done.2
  111.5 21.7 %all-gather.2 = bf16[512,256]{1,0:T(8,128)(2,1)S(1)} all-gather(bf16[128,256]{1,0:T(8,128)(2,1)S(1)} %get-tuple-element.34), channel_id=4, replica_groups=mesh['y'=4,'zh'=4,'c'=2,'zl'=4,'x'=4] {'zh'}, dimensions={0}, use_global_device_ids=true | all-gather | bytes 327680 | tf_op jit(solution)/shard_map/grad_rows/all_gather | solution.py:35
  133.2 1.2 broadcast_in_dim.34
  134.4 4.3 %all-to-all-start.2 = ((bf16[4,4,128,256]{3,2,1,0:T(8,128)(2,1)}), bf16[4,4,128,256]{3,2,1,0:T(8,128)(2,1)}, u32[]{:S(2)}, u32[]{:S(2)}) async-start(bf16[4,4,128,256]{3,2,1,0:T(8,128)(2,1)} %broadcast_in_dim.34), calls=%async_computation.2 | async-start | bytes 2097152 | tf_op jit(solution)/shard_map/grad_rows/all_to_all | solution.py:21
  138.7 1.2 all-gather.10.cloned.1.call-done
  139.9 1.6 copy-done.3
  141.5 1.6 copy-done.4
  143.1 2.6 %products.1 = (f32[2,128,256]{2,1,0:T(8,128)S(1)}, bf16[128,256]{1,0:T(8,128)(2,1)S(1)}, bf16[128,256]{1,0:T(8,128)(2,1)S(1)}, f32[16,256]{1,0:T(8,128)S(1)}) custom-call(bf16[4,2,32,4096]{3,2,1,0:T(8,128)(2,1)S(1)} %bitcast.34, bf16[16,2,128,256]{3,2,1,0:T(8,128)(2,1)S(1)} %copy-done.1, bf16[16,2,128,256]{3,2,1,0:T(8,128)(2,1)S(1)} %copy-done.3, ...), custom_call_target="tpu_custom_call" | custom-call | flops 1073741824 | bytes 6717440 | tf_op jit(solution)/shard_map/products/products/pallas_call | solution.py:233
  145.7 0.7 copy-done.6
  146.4 3.1 %all-to-all-done.2 = bf16[4,4,128,256]{3,2,1,0:T(8,128)(2,1)} async-done(((bf16[4,4,128,256]{3,2,1,0:T(8,128)(2,1)}), bf16[4,4,128,256]{3,2,1,0:T(8,128)(2,1)}, u32[]{:S(2)}, u32[]{:S(2)}) %all-to-all-start.2) | async-done | bytes 1048608 | tf_op jit(solution)/shard_map/grad_rows/all_to_all | solution.py:21
  149.5 1.5 broadcast_in_dim.35
  151.0 10.3 %all_to_all.31 = bf16[2,4,4,128,256]{4,3,2,1,0:T(8,128)(2,1)S(1)} all-to-all(bf16[2,4,4,128,256]{4,3,2,1,0:T(8,128)(2,1)S(1)} %broadcast_in_dim.35), channel_id=1, replica_groups=mesh['y'=4,'zh'=4,'c'=2,'zl'=4,'x'=4] {'c'}, dimensions={0} | all-to-all | bytes 4194304 | tf_op jit(solution)/shard_map/grad_rows/all_to_all | solution.py:21
  161.3 0.3 copy.24
  161.5 1.4 weight_b.1
  163.0 1.0 copy-done.5
  164.0 0.6 copy-done.8
  164.5 4.0 %all-to-all-start.4 = ((bf16[4,4,272,128]{3,2,1,0:T(8,128)(2,1)}), bf16[4,4,272,128]{3,2,1,0:T(8,128)(2,1)S(1)}, u32[]{:S(2)}, u32[]{:S(2)}) async-start(bf16[4,4,272,128]{3,2,1,0:T(8,128)(2,1)} %copy-done.5), calls=%async_computation.4 | async-start | bytes 2228224 | tf_op jit(solution)/shard_map/weight_b/all_to_all | solution.py:331
  168.5 13.1 %all-gather.4 = bf16[512,256]{1,0:T(8,128)(2,1)S(1)} all-gather(bf16[128,256]{1,0:T(8,128)(2,1)S(1)} %get-tuple-element.45), channel_id=6, replica_groups=mesh['y'=4,'zh'=4,'c'=2,'zl'=4,'x'=4] {'zl'}, dimensions={0}, use_global_device_ids=true | all-gather | bytes 327680 | tf_op jit(solution)/shard_map/weight_b/all_gather | solution.py:35
  181.6 2.1 all-to-all-done.4.refs_0_
  183.7 0.9 fold.1
  184.6 4.9 %all-to-all-start.5 = ((bf16[4,272,128]{2,1,0:T(8,128)(2,1)}), bf16[4,272,128]{2,1,0:T(8,128)(2,1)S(1)}, u32[]{:S(2)}, u32[]{:S(2)}) async-start(bf16[4,272,128]{2,1,0:T(8,128)(2,1)} %fold.1), calls=%async_computation.5 | async-start | bytes 557056 | tf_op jit(solution)/shard_map/weight_b/all_to_all | solution.py:339
  189.5 2.2 %collective-permute-start.1 = (bf16[4,128,256]{2,1,0:T(8,128)(2,1)S(1)}, bf16[4,128,256]{2,1,0:T(8,128)(2,1)S(1)}, u32[]{:S(2)}, u32[]{:S(2)}) collective-permute-start(bf16[4,128,256]{2,1,0:T(8,128)(2,1)S(1)} %bitcast.35), channel_id=1, source_target_pairs={{0,1},{1,2},{2,3},{3,0},{4,5},{5,6},{6,7},{7,4},{8,9},{9,10},{10,1... | collective-permute-start | bytes 786440 | tf_op jit(solution)/shard_map/weight_b/ppermute | solution.py:341
  191.6 3.7 %collective-permute-start.2 = (bf16[4,128,256]{2,1,0:T(8,128)(2,1)S(1)}, bf16[4,128,256]{2,1,0:T(8,128)(2,1)S(1)}, u32[]{:S(2)}, u32[]{:S(2)}) collective-permute-start(bf16[4,128,256]{2,1,0:T(8,128)(2,1)S(1)} %bitcast.36), channel_id=1, source_target_pairs={{0,2},{1,3},{2,0},{3,1},{4,6},{5,7},{6,4},{7,5},{8,10},{9,11},{10,... | collective-permute-start | bytes 786440 | tf_op jit(solution)/shard_map/weight_b/ppermute | solution.py:341
  195.3 2.5 %collective-permute-start.3 = (bf16[4,128,256]{2,1,0:T(8,128)(2,1)S(1)}, bf16[4,128,256]{2,1,0:T(8,128)(2,1)S(1)}, u32[]{:S(2)}, u32[]{:S(2)}) collective-permute-start(bf16[4,128,256]{2,1,0:T(8,128)(2,1)S(1)} %bitcast.37), channel_id=1, source_target_pairs={{0,3},{1,0},{2,1},{3,2},{4,7},{5,4},{6,5},{7,6},{8,11},{9,8},{10,9... | collective-permute-start | bytes 786440 | tf_op jit(solution)/shard_map/weight_b/ppermute | solution.py:341
  197.9 1.4 collective-permute-done.1.refs_2_
  199.3 4.0 %collective-permute-done.2.refs_3_ = bf16[4,128,256]{2,1,0:T(8,128)(2,1)S(1)} collective-permute-done((bf16[4,128,256]{2,1,0:T(8,128)(2,1)S(1)}, bf16[4,128,256]{2,1,0:T(8,128)(2,1)S(1)}, u32[]{:S(2)}, u32[]{:S(2)}) %collective-permute-start.2) | collective-permute-done | bytes 262176 | tf_op jit(solution)/shard_map/weight_b/ppermute | solution.py:341
  203.4 3.3 %collective-permute-done.3.refs_4_ = bf16[4,128,256]{2,1,0:T(8,128)(2,1)S(1)} collective-permute-done((bf16[4,128,256]{2,1,0:T(8,128)(2,1)S(1)}, bf16[4,128,256]{2,1,0:T(8,128)(2,1)S(1)}, u32[]{:S(2)}, u32[]{:S(2)}) %collective-permute-start.3) | collective-permute-done | bytes 262176 | tf_op jit(solution)/shard_map/weight_b/ppermute | solution.py:341
  206.7 0.9 copy-done.7
  207.7 0.7 copy-done.9
  208.3 0.5 weight_a.1.side_ref
  208.8 0.8 finish.1
  (18 shorter events, 0.2 us)
Async XLA Ops:
  10.1 53.5 %all-to-all-start = ((bf16[32,3,8,128]{3,2,1,0:T(8,128)(2,1)}), bf16[32,3,8,128]{3,2,1,0:T(8,128)(2,1)S(1)}, u32[]{:S(2)}, u32[]{:S(2)}) async-start(bf16[32,3,8,128]{3,2,1,0:T(8,128)(2,1)} %copy_bitcast_fusion.2), calls=%async_computation | async-start | bytes 393216 | tf_op jit(solution)/shard_map/columns/all_to_all | solution.py:278
  29.5 69.7 %all-gather.8.cloned.1.call-start = ((), (), s32[]{:S(2)}) async-start(), calls=%async_computation.6 | async-start | bytes 2621440 | tf_op jit(solution)/shard_map/rows/all_gather | solution.py:35
  63.6 76.2 %all-gather.10.cloned.1.call-start = ((), (), s32[]{:S(2)}) async-start(), calls=%async_computation.7 | async-start | bytes 2621440 | tf_op jit(solution)/shard_map/columns/all_gather | solution.py:35
  100.1 6.6 %collective-permute-start = (bf16[16,2,128,256]{3,2,1,0:T(8,128)(2,1)}, bf16[16,2,128,256]{3,2,1,0:T(8,128)(2,1)S(1)}, u32[]{:S(2)}, u32[]{:S(2)}) collective-permute-start(bf16[16,2,128,256]{3,2,1,0:T(8,128)(2,1)} %all-gather.8.cloned.1.call-done), channel_id=1, source_target_pairs={{0,16},{16,0},{1,17},{17,1},{2,18},{18,2},{3,19},{19,3},{4,20},{20... | collective-permute-start | bytes 6291464 | tf_op jit(solution)/shard_map/rows/ppermute | solution.py:264
  106.7 1.6 copy-start
  110.1 1.4 copy-start.2
  111.5 28.4 %copy-start.1 = (bf16[16,2,128,256]{3,2,1,0:T(8,128)(2,1)S(1)}, bf16[16,2,128,256]{3,2,1,0:T(8,128)(2,1)}, u32[]{:S(2)}) copy-start(bf16[16,2,128,256]{3,2,1,0:T(8,128)(2,1)} %all-gather.8.cloned.1.call-done) | copy-start | bytes 6291460
  134.4 15.1 %all-to-all-start.2 = ((bf16[4,4,128,256]{3,2,1,0:T(8,128)(2,1)}), bf16[4,4,128,256]{3,2,1,0:T(8,128)(2,1)}, u32[]{:S(2)}, u32[]{:S(2)}) async-start(bf16[4,4,128,256]{3,2,1,0:T(8,128)(2,1)} %broadcast_in_dim.34), calls=%async_computation.2 | async-start | bytes 2097152 | tf_op jit(solution)/shard_map/grad_rows/all_to_all | solution.py:21
  139.9 1.6 copy-start.3
  141.5 1.6 copy-start.4
  145.7 0.7 copy-start.6
  163.0 1.0 copy-start.5
  164.0 0.6 copy-start.8
  164.5 19.2 %all-to-all-start.4 = ((bf16[4,4,272,128]{3,2,1,0:T(8,128)(2,1)}), bf16[4,4,272,128]{3,2,1,0:T(8,128)(2,1)S(1)}, u32[]{:S(2)}, u32[]{:S(2)}) async-start(bf16[4,4,272,128]{3,2,1,0:T(8,128)(2,1)} %copy-done.5), calls=%async_computation.4 | async-start | bytes 2228224 | tf_op jit(solution)/shard_map/weight_b/all_to_all | solution.py:331
  184.6 24.2 %all-to-all-start.5 = ((bf16[4,272,128]{2,1,0:T(8,128)(2,1)}), bf16[4,272,128]{2,1,0:T(8,128)(2,1)S(1)}, u32[]{:S(2)}, u32[]{:S(2)}) async-start(bf16[4,272,128]{2,1,0:T(8,128)(2,1)} %fold.1), calls=%async_computation.5 | async-start | bytes 557056 | tf_op jit(solution)/shard_map/weight_b/all_to_all | solution.py:339
  189.5 9.9 %collective-permute-start.1 = (bf16[4,128,256]{2,1,0:T(8,128)(2,1)S(1)}, bf16[4,128,256]{2,1,0:T(8,128)(2,1)S(1)}, u32[]{:S(2)}, u32[]{:S(2)}) collective-permute-start(bf16[4,128,256]{2,1,0:T(8,128)(2,1)S(1)} %bitcast.35), channel_id=1, source_target_pairs={{0,1},{1,2},{2,3},{3,0},{4,5},{5,6},{6,7},{7,4},{8,9},{9,10},{10,1... | collective-permute-start | bytes 786440 | tf_op jit(solution)/shard_map/weight_b/ppermute | solution.py:341
  191.6 11.7 %collective-permute-start.2 = (bf16[4,128,256]{2,1,0:T(8,128)(2,1)S(1)}, bf16[4,128,256]{2,1,0:T(8,128)(2,1)S(1)}, u32[]{:S(2)}, u32[]{:S(2)}) collective-permute-start(bf16[4,128,256]{2,1,0:T(8,128)(2,1)S(1)} %bitcast.36), channel_id=1, source_target_pairs={{0,2},{1,3},{2,0},{3,1},{4,6},{5,7},{6,4},{7,5},{8,10},{9,11},{10,... | collective-permute-start | bytes 786440 | tf_op jit(solution)/shard_map/weight_b/ppermute | solution.py:341
  195.3 11.4 %collective-permute-start.3 = (bf16[4,128,256]{2,1,0:T(8,128)(2,1)S(1)}, bf16[4,128,256]{2,1,0:T(8,128)(2,1)S(1)}, u32[]{:S(2)}, u32[]{:S(2)}) collective-permute-start(bf16[4,128,256]{2,1,0:T(8,128)(2,1)S(1)} %bitcast.37), channel_id=1, source_target_pairs={{0,3},{1,0},{2,1},{3,2},{4,7},{5,4},{6,5},{7,6},{8,11},{9,8},{10,9... | collective-permute-start | bytes 786440 | tf_op jit(solution)/shard_map/weight_b/ppermute | solution.py:341
  206.7 0.9 copy-start.7
  207.7 0.7 copy-start.9
Sparse Core Ops, SparseCore 0:
  63.8 35.3 all-gather.7
  101.3 38.5 all-gather.9
